TPU v7x, 256 devices: a whole 4x4x8 slice. The times are simulated.
256 devices in a mesh: group: 4 (over y_lo, core), dp: 8 (over x, y_hi), mp: 8 (over z).
Axes of the slice: x: 4, y: 4 (y_hi: 2, y_lo: 2; y = y_hi * 2 + y_lo), z: 8, core: 2. Of those that a mesh axis runs over, the one named last changes fastest.
Arguments:
- latent_noise: bfloat16 [16, 256, 1280], P('dp'), may hold values from -6 to 6
- score_noise: bfloat16 [16, 256, 1280], P('dp'), may hold values from -6 to 6
- timesteps: int32 [16], P('dp'), may hold values from 20 to 979
- classes: int32 [16], P('dp'), may hold values from 0 to 999
- class_table: bfloat16 [1000, 1280], replicated, may hold values from -6 to 6
- gen_weights: bfloat16 [1280, 2, 5120], P(('group', 'dp'), None, 'mp'), may hold values from -0.15625 to 0.15625
- real_weights: bfloat16 [1280, 2, 5120], P(('group', 'dp'), None, 'mp'), may hold values from -0.15625 to 0.15625
- fake_weights: bfloat16 [1280, 2, 5120], P(('group', 'dp'), None, 'mp'), may hold values from -0.15625 to 0.15625
Outputs:
- gen_grad: float32 [1280, 2, 5120], P(('group', 'dp'), None, 'mp')
- fake_grad: float32 [1280, 2, 5120], P(('group', 'dp'), None, 'mp')
All inputs are finite; a program needn't handle non-finite values. Where the computation divides by a largest or mean magnitude, that divisor is 1e-20 or more.
Results may differ from a plain program's by a relative error of at most 0.015.
Values may be sent and summed in bfloat16 or wider, within the bound.
No kernel may reach another device: no remote copies, remote signals or barrier semaphores. Data moves between devices by JAX's collectives and lax.ppermute only.
A program may use at most 128 MiB of HBM per device.

v0:
```python
import math

import jax
import jax.numpy as jnp
from jax import lax
from jax.sharding import PartitionSpec as P

TSTEPS = 1000


GUIDANCE = 3.0
EPSILON = 1e-06
MEAN_EPS = 1e-05


def from_root(block, axis, owner):
    block = jnp.where(lax.axis_index(axis) == owner, block, jnp.zeros_like(block))
    return lax.psum(block, axis)


def normalize(stream_in, embedding):
    summed = stream_in.astype(jnp.float32) + embedding.astype(jnp.float32)[:, None, :]
    factor = lax.rsqrt(jnp.mean(summed * summed, axis=-1, keepdims=True) + EPSILON)
    return (summed * factor).astype(jnp.bfloat16).reshape(-1, summed.shape[-1])


def forward_part(normed, w_in, w_out):
    preact = jnp.dot(normed, w_in, preferred_element_type=jnp.float32)
    active = jax.nn.gelu(preact).astype(jnp.bfloat16)
    partial_sum = lax.dot_general(
        active, w_out, (((1,), (1,)), ((), ())), preferred_element_type=jnp.float32
    )
    return (preact, active, partial_sum)


def spare_part(row_count, hidden, feature_width):
    return (
        jnp.zeros((row_count, hidden), jnp.float32),
        jnp.zeros((row_count, hidden), jnp.bfloat16),
        jnp.zeros((row_count, feature_width), jnp.float32),
    )


def channel_total(partial_sum):
    return lax.psum(partial_sum.astype(jnp.bfloat16), "mp").astype(jnp.float32)


def grad_block(normed_cols, delta_cols, active, pre_delta):
    in_part = lax.dot_general(
        normed_cols, pre_delta, (((0,), (0,)), ((), ())), preferred_element_type=jnp.float32
    )
    out_part = lax.dot_general(
        delta_cols, active, (((0,), (0,)), ((), ())), preferred_element_type=jnp.float32
    )
    return jnp.stack([in_part, out_part], axis=1)


def local(
    latent_noise,
    score_noise,
    timesteps,
    classes,
    class_table,
    gen_weights,
    real_weights,
    fake_weights,
):
    group_index = lax.axis_index("group")
    n_dp = lax.axis_size("dp")
    samples, positions, feature_width = latent_noise.shape
    row_count = samples * positions
    row_piece = gen_weights.shape[0]
    hidden = gen_weights.shape[2]
    table_rows = class_table.shape[0]
    loss_scale = 1.0 / math.sqrt(samples * n_dp * positions)
    stacked = jnp.stack([gen_weights, real_weights, fake_weights, real_weights])
    outgoing = jnp.repeat(stacked, n_dp, axis=0)
    incoming = lax.all_to_all(outgoing, ("group", "dp"), split_axis=0, concat_axis=0, tiled=True)
    weights = incoming.reshape(feature_width, 2, hidden)
    w_in = weights[:, 0, :]
    w_out = weights[:, 1, :]
    onehot = (classes[:, None] == lax.iota(jnp.int32, table_rows)[None, :]).astype(jnp.bfloat16)
    embedding = jnp.dot(onehot, class_table, preferred_element_type=jnp.float32).astype(
        jnp.bfloat16
    )
    is_gen = group_index == 0
    trains = jnp.logical_or(is_gen, group_index == 2)
    normed_gen = normalize(latent_noise, embedding)
    preact_gen, active_gen, partial_gen = lax.cond(
        is_gen,
        lambda: forward_part(normed_gen, w_in, w_out),
        lambda: spare_part(row_count, hidden, feature_width),
    )
    latents_own = latent_noise.reshape(row_count, feature_width).astype(
        jnp.float32
    ) + channel_total(partial_gen)
    latents = from_root(latents_own, "group", 0)
    phase_angle = 0.5 * jnp.pi / TSTEPS * timesteps.astype(jnp.float32)
    signal_scale = jnp.cos(phase_angle)[:, None, None]
    noise_scale = jnp.sin(phase_angle)[:, None, None]
    noised = (
        signal_scale * latents.reshape(samples, positions, feature_width)
        + noise_scale * score_noise.astype(jnp.float32)
    ).astype(jnp.bfloat16)
    cond_embed = jnp.where(group_index == 1, jnp.zeros_like(embedding), embedding)
    normed_score = normalize(noised, cond_embed)
    preact_score, active_score, partial_score = lax.cond(
        is_gen,
        lambda: spare_part(row_count, hidden, feature_width),
        lambda: forward_part(normed_score, w_in, w_out),
    )
    pred_f = noised.reshape(row_count, feature_width).astype(jnp.float32) + channel_total(
        partial_score
    )
    collected = lax.all_gather(pred_f[None], "group", axis=0, tiled=True)
    uncond_f = collected[1]
    real_mix = uncond_f + GUIDANCE * (collected[3] - uncond_f)
    fake_f = collected[2]
    gap = jnp.mean(jnp.abs(latents - real_mix).reshape(samples, positions * feature_width), axis=1)
    sample_weight = 1.0 / (gap + MEAN_EPS)
    row_weight = jnp.repeat(sample_weight, positions)[:, None]
    gen_delta = ((fake_f - real_mix) * row_weight * loss_scale).astype(jnp.bfloat16)
    fake_delta = (2.0 * (pred_f - latents) * loss_scale).astype(jnp.bfloat16)
    delta = jnp.where(is_gen, gen_delta, fake_delta)
    normed = jnp.where(is_gen, normed_gen, normed_score)
    preact = jnp.where(is_gen, preact_gen, preact_score)
    active = jnp.where(is_gen, active_gen, active_score)

    def backward_prep():
        back = jnp.dot(delta, w_out, preferred_element_type=jnp.float32)
        unused, pull = jax.vjp(jax.nn.gelu, preact)
        return pull(back)[0].astype(jnp.bfloat16)

    pre_delta = lax.cond(
        trains, backward_prep, lambda: jnp.zeros((row_count, hidden), jnp.bfloat16)
    )
    gen_mask = jnp.where(is_gen, 1.0, 0.0)
    fake_mask = jnp.where(group_index == 2, 1.0, 0.0)
    block = lax.cond(
        trains,
        lambda: grad_block(normed, delta, active, pre_delta),
        lambda: jnp.zeros((row_piece * lax.axis_size(("group", "dp")), 2, hidden), jnp.float32),
    )
    summed = lax.psum_scatter(
        jnp.stack([block * gen_mask, block * fake_mask], axis=1),
        ("group", "dp"),
        scatter_dimension=0,
        tiled=True,
    )
    gen_grad = summed[:, 0]
    fake_grad = summed[:, 1]
    return (gen_grad, fake_grad)


def solution(mesh):
    return jax.shard_map(
        local,
        mesh=mesh,
        in_specs=(
            P("dp", None, None),
            P("dp", None, None),
            P("dp"),
            P("dp"),
            P(),
            P(("group", "dp"), None, "mp"),
            P(("group", "dp"), None, "mp"),
            P(("group", "dp"), None, "mp"),
        ),
        out_specs=(P(("group", "dp"), None, "mp"), P(("group", "dp"), None, "mp")),
        check_vma=False,
    )
```

profile of v0, /device:TPU:1, one launch (start us, length us, event | category | flops | bytes accessed | tf_op | source)
XLA Modules:
  0.0 801.3 jit_solution(10637176779545660946)
XLA Ops:
  7.2 1.9 pad_maximum_fusion.2
  9.2 2.0 broadcast_in_dim.8
  11.2 8.8 %all-to-all-start = ((bf16[32,40,2,640]{3,1,2,0:T(8,128)(2,1)}), bf16[32,40,2,640]{3,1,2,0:T(8,128)(2,1)}, u32[]{:S(2)}, u32[]{:S(2)}) async-start(bf16[32,40,2,640]{3,1,2,0:T(8,128)(2,1)} %bitcast.56), calls=%async_computation | async-start | bytes 6553600 | tf_op jit(solution)/shard_map/all_to_all | solution.py:78
  20.0 0.5 fusion.35
  20.5 0.8 copy-done.3
  21.3 0.4 multiply_reduce_fusion.1
  21.8 1.4 multiply_convert_fusion.2
  23.2 41.3 %all-to-all-done = bf16[32,40,2,640]{3,1,2,0:T(8,128)(2,1)} async-done(((bf16[32,40,2,640]{3,1,2,0:T(8,128)(2,1)}), bf16[32,40,2,640]{3,1,2,0:T(8,128)(2,1)}, u32[]{:S(2)}, u32[]{:S(2)}) %all-to-all-start) | async-done | bytes 3276832 | tf_op jit(solution)/shard_map/all_to_all | solution.py:78
  64.5 2.2 copy.25
  66.8 0.3 slice_bitcast_fusion
  67.1 1.2 copy-done.9
  68.3 0.5 copy-done.7
  68.7 3.2 conditional.4
  68.7 1.2 broadcast.88
  69.9 1.2 broadcast.90
  71.1 0.9 broadcast.89
  72.1 74.1 %all-reduce.4.cloned.1.call-done = bf16[512,1280]{1,0:T(8,128)(2,1)} async-done(((bf16[512,1280]{1,0:T(8,128)(2,1)}), bf16[512,1280]{1,0:T(8,128)(2,1)}) %all-reduce.4.cloned.1.call-update) | async-done | bytes 1310736 | tf_op jit(solution)/shard_map/psum | solution.py:45
  146.1 3.2 fusion.31
  149.4 0.6 copy-done.14
  150.0 73.7 %all-reduce.6.cloned.1.call-done = f32[512,1280]{1,0:T(8,128)} async-done(((f32[512,1280]{1,0:T(8,128)}), f32[512,1280]{1,0:T(8,128)}) %all-reduce.6.cloned.1.call-update) | async-done | bytes 2621456 | tf_op jit(solution)/shard_map/psum | solution.py:18
  223.7 3.0 multiply_reduce_fusion
  226.8 1.4 multiply_convert_fusion.1
  228.2 0.3 copy-done.6
  228.4 5.9 conditional.5
  228.4 3.6 fusion.15
  232.1 2.3 fusion.40
  234.5 73.6 %all-reduce.8.cloned.1.call-done = bf16[512,1280]{1,0:T(8,128)(2,1)} async-done(((bf16[512,1280]{1,0:T(8,128)(2,1)}), bf16[512,1280]{1,0:T(8,128)(2,1)}) %all-reduce.8.cloned.1.call-update) | async-done | bytes 1310736 | tf_op jit(solution)/shard_map/psum | solution.py:45
  308.0 3.0 bitcast_add_fusion
  311.2 104.7 %all-gather.3.cloned.1.call-done = f32[2048,1280]{1,0:T(8,128)} async-done(((f32[512,1280]{1,0:T(8,128)}), f32[2048,1280]{1,0:T(8,128)}) %all-gather.3.cloned.1.call-update) | async-done | bytes 10485776 | tf_op jit(solution)/shard_map/all_gather | solution.py:115
  415.9 3.9 abs_reduce_fusion
  419.8 0.1 reduce_sum.38
  419.9 0.1 broadcast_bitcast_fusion
  420.0 6.6 fusion.32
  426.6 0.2 conditional.6
  426.6 0.1 broadcast.102
  426.8 0.8 copy-done.11
  427.7 0.2 select_n.54
  427.8 0.3 copy-done.10
  428.1 1.8 conditional.7
  428.1 1.8 broadcast.108.clone
  429.9 2.7 copy-done.2
  432.6 8.5 %multiply_bitcast_fusion.1 = (f32[1280,1,2,640]{3,2,0,1:T(2,128)S(1)}, f32[1280,1,2,640]{3,2,0,1:T(2,128)}) fusion(f32[1280,2,640]{2,1,0:T(2,128)} %copy-done.2, f32[]{:T(128)S(6)} %select_n.59, f32[]{:T(128)S(6)} %select_n.60), kind=kLoop, calls=%fused_computation.35 | loop fusion | flops 3276800 | bytes 19660808 | tf_op jit(solution)/shard_map/stack | solution.py:145
  441.2 7.5 pad_maximum_fusion.1
  448.6 6.0 copy.29
  454.6 17.0 %reshape.63 = f32[1280,2560]{1,0:T(8,128)} reshape(f32[1280,2,2,640]{3,2,1,0:T(2,128)} %copy.29) | data formatting | bytes 26214400
  471.7 321.0 %reduce-scatter.4.cloned.1.call-done = f32[40,2560]{1,0:T(8,128)} async-done(((f32[1280,2560]{1,0:T(8,128)}), f32[40,2560]{1,0:T(8,128)}) %reduce-scatter.4.cloned.1.call-update) | async-done | bytes 409616
  792.7 1.3 reshape.64
  793.9 0.8 slice_bitcast_fusion.2
  (37 shorter events, 0.5 us)
Async XLA Ops:
  7.2 12.8 %copy-start = (bf16[1000,1280]{1,0:T(8,128)(2,1)S(1)}, bf16[1000,1280]{1,0:T(8,128)(2,1)}, u32[]{:S(2)}) copy-start(bf16[1000,1280]{1,0:T(8,128)(2,1)} %param.20) | copy-start | bytes 7680004
  11.2 8.9 %copy-start.13 = (s32[2]{0:T(128)S(1)}, s32[2]{0:T(128)}, u32[]{:S(2)}) copy-start(s32[2]{0:T(128)} %param.19) | copy-start | bytes 28
  11.2 53.4 %all-to-all-start = ((bf16[32,40,2,640]{3,1,2,0:T(8,128)(2,1)}), bf16[32,40,2,640]{3,1,2,0:T(8,128)(2,1)}, u32[]{:S(2)}, u32[]{:S(2)}) async-start(bf16[32,40,2,640]{3,1,2,0:T(8,128)(2,1)} %bitcast.56), calls=%async_computation | async-start | bytes 6553600 | tf_op jit(solution)/shard_map/all_to_all | solution.py:78
  19.9 126.2 %all-reduce.4.cloned.1.call-start = ((), (), s32[]{:S(2)}) async-start(), calls=%async_computation.2 | async-start | bytes 2621440 | tf_op jit(solution)/shard_map/psum | solution.py:45
  20.0 1.3 copy-start.3
  66.7 1.5 copy-start.9
  67.0 1.2 copy-start.5
  67.1 1.7 copy-start.7
  72.0 74.1 %copy-start.4 = (bf16[2,256,1280]{2,1,0:T(8,128)(2,1)S(1)}, bf16[2,256,1280]{2,1,0:T(8,128)(2,1)}, u32[]{:S(2)}) copy-start(bf16[2,256,1280]{2,1,0:T(8,128)(2,1)} %param.16) | copy-start | bytes 3932164
  72.0 151.7 %all-reduce.6.cloned.1.call-start = ((), (), s32[]{:S(2)}) async-start(), calls=%async_computation.3 | async-start | bytes 5242880 | tf_op jit(solution)/shard_map/psum | solution.py:18
  149.3 0.7 copy-start.14
  149.3 158.7 %all-reduce.8.cloned.1.call-start = ((), (), s32[]{:S(2)}) async-start(), calls=%async_computation.4 | async-start | bytes 2621440 | tf_op jit(solution)/shard_map/psum | solution.py:45
  223.7 4.5 copy-start.8
  226.7 1.7 copy-start.6
  234.4 181.5 %all-gather.3.cloned.1.call-start = ((), (), s32[]{:S(2)}) async-start(), calls=%async_computation.5 | async-start | bytes 13107200 | tf_op jit(solution)/shard_map/all_gather | solution.py:115
  311.1 481.6 %reduce-scatter.4.cloned.1.call-start = ((), (), s32[]{:S(2)}) async-start(), calls=%async_computation.6 | async-start | bytes 13516800
  426.6 1.6 copy-start.10
  426.8 0.8 copy-start.11
  429.9 2.7 copy-start.2
  471.7 323.1 %copy-start.1 = (bf16[1000,1280]{1,0:T(8,128)(2,1)S(1)}, bf16[1000,1280]{1,0:T(8,128)(2,1)}, u32[]{:S(2)}) copy-start(bf16[1000,1280]{1,0:T(8,128)(2,1)} %param.20) | copy-start | bytes 7680004
Sparse Core Ops, SparseCore 0:
  72.1 73.9 all-reduce.3
  149.4 74.2 all-reduce.5
  234.5 73.4 all-reduce.7
  311.2 104.6 all-gather.2
  471.8 320.8 reduce-scatter.3
where the time goes:
time: 803 us; the launch traced here: 801 us
  waiting for transfers between devices  688 us (86%)
  local copies, waits for them, and re-layouts  42.2 us (5%)
  other arithmetic  41.1 us (5%)
  between operations  14 us (2%)
  starting transfers between devices  8.98 us (1%)
    unnamed x6, waiting for transfers between devices  321 us
    psum x2, waiting for transfers between devices, channel_total(): return lax.psum(partial_sum.astype(jnp.bfloat16), 'mp').astype(jnp.float32)  148 us
    all_gather x1, waiting for transfers between devices, local(): collected = lax.all_gather(pred_f[None], 'group', axis=0, tiled=True)  105 us
    psum x1, waiting for transfers between devices, from_root(): return lax.psum(block, axis)  73.7 us
    all_to_all x1, waiting for transfers between devices, local(): lax.all_to_all(outgoing, ('group', 'dp'), split_axis=0, concat_axis=0, ti...  41.3 us
    unnamed x33, local copies, waits for them, and re-layouts  31.6 us
  transfers between devices with their start and end apart: 6, of which 6 were waited for; matrix products, arithmetic and copies ran while one was open for 0% of the time, Pallas kernels for 0%

commit v1 on v0

v1 whole, which is shorter than its diff:
```python
import math

import jax
import jax.numpy as jnp
from jax import lax
from jax.experimental import pallas as pl
from jax.experimental.pallas import tpu as pltpu
from jax.sharding import PartitionSpec as P

TSTEPS = 1000
GUIDANCE = 3.0
EPSILON = 1e-06
MEAN_EPS = 1e-05

PLANE = ("group", "dp")
LANES = 128
SMEM = pl.BlockSpec(memory_space=pltpu.SMEM)
VMEM = pl.BlockSpec(memory_space=pltpu.VMEM)
F32 = jnp.float32
BF16 = jnp.bfloat16


def call(body, name, inputs, scalars, outs, flops=0, scratch=()):
    moved = sum(math.prod(a.shape) * a.dtype.itemsize for a in list(inputs) + list(outs))
    return pl.pallas_call(
        body,
        name=name,
        out_shape=outs,
        in_specs=[SMEM] * len(scalars) + [VMEM] * len(inputs),
        out_specs=[VMEM] * len(outs),
        scratch_shapes=list(scratch),
        compiler_params=pltpu.CompilerParams(vmem_limit_bytes=40 * 2**20),
        cost_estimate=pl.CostEstimate(flops=flops, bytes_accessed=moved, transcendentals=0),
    )(*scalars, *inputs)


def shape(dims, dtype):
    return jax.ShapeDtypeStruct(dims, dtype)


def normalize(summed):
    factor = lax.rsqrt(jnp.mean(summed * summed, axis=-1, keepdims=True) + EPSILON)
    return (summed * factor).astype(BF16)


def dot_t(left, right):
    return lax.dot_general(left, right, (((1,), (1,)), ((), ())), preferred_element_type=F32)


def forward_part(normed, w_in, w_out):
    preact = jnp.dot(normed, w_in, preferred_element_type=F32)
    active = jax.nn.gelu(preact).astype(BF16)
    return preact, active, dot_t(active, w_out).astype(BF16)


def core_swap(block):
    return lax.ppermute(block, "group", [(0, 1), (1, 0), (2, 3), (3, 2)])


def shift(block, step):
    n_mp = lax.axis_size("mp")
    return lax.ppermute(block, "mp", [(i, (i + step) % n_mp) for i in range(n_mp)])


def spread(block):
    return [block] + [shift(block, k) for k in range(1, lax.axis_size("mp"))]


def to_owner(blocks):
    return [blocks[0]] + [shift(blocks[k], -k) for k in range(1, len(blocks))]


def on_core(place, run, mine, other):
    pl.when(place[0] == 0)(lambda: run(mine, other))
    pl.when(place[0] != 0)(lambda: run(other, mine))


def power_of(peak):
    return jnp.floor(jnp.log(jnp.maximum(peak, 1e-30)) * (1.0 / math.log(2.0))) - 13.0


def top_of(value):
    by_row = jnp.max(jnp.abs(value), axis=1, keepdims=True)
    return jnp.max(by_row, axis=0, keepdims=True)


def ring_place(place, k, piece, n_mp):
    return pl.multiple_of(lax.rem(place[2] + n_mp - k, n_mp) * piece, piece)


def prepare_kernel(place, scales, latent, noise, embed, normed, stream, scaled, *, piece, n_mp):
    base = pl.multiple_of(place[0] * (piece * n_mp), piece)
    rows = latent[place[1], pl.ds(base, piece * n_mp), :].astype(F32)
    normed[...] = normalize(rows + embed[...])
    at = pl.multiple_of(base + place[2] * piece, piece)
    stream[...] = latent[place[1], pl.ds(at, piece), :].astype(F32)
    scaled[...] = scales[1] * noise[place[1], pl.ds(at, piece), :].astype(F32)


def gen_kernel(place, normed, mine, other, *refs, piece):
    preact_ref, active_ref, parts, whole = refs[0], refs[1], refs[2:-1], refs[-1]

    def run(w_in, w_out):
        preact, active, partial = forward_part(normed[...], w_in[...], w_out[...])
        preact_ref[...] = preact
        active_ref[...] = active
        whole[...] = partial

    on_core(place, run, mine, other)
    for k, part in enumerate(parts):
        part[...] = whole[pl.ds(ring_place(place, k, piece, len(parts)), piece), :]


def score_kernel(place, *refs, piece, n_mp, hidden):
    blocks, refs = refs[:n_mp], refs[n_mp:]
    embed, score_mine, score_other, normed_ref, preact_ref, active_ref, out, both = refs
    rows = piece * n_mp
    width = embed.shape[1]
    for k, block in enumerate(blocks):
        summed = block[...].astype(F32)
        at = ring_place(place, k, piece, n_mp)
        both[pl.ds(at, piece), :] = normalize(summed + embed[...])
        both[pl.ds(pl.multiple_of(rows + at, piece), piece), :] = normalize(summed)
    normed_ref[...] = both[:rows, :]

    def run(mine, other):
        preact, active, fake = forward_part(both[:rows, :], mine[:, :hidden], other[:, :hidden])
        preact_ref[...] = preact
        active_ref[...] = active
        fake = fake.astype(F32)
        real = forward_part(both[...], mine[:, hidden:], other[:, hidden:])[2].astype(F32)
        uncond, cond = real[rows:], real[:rows]
        mix = uncond + GUIDANCE * (cond - uncond)
        fake_power, mix_power = power_of(top_of(fake)), power_of(top_of(mix))
        fake = fake * jnp.exp2(-fake_power)
        mix = mix * jnp.exp2(-mix_power)
        line = lax.broadcasted_iota(jnp.int32, (piece, LANES), 0)
        tail = jnp.where(line < 8, fake_power, mix_power)
        for j in range(n_mp):
            out[j, :, :width] = fake[j * piece : (j + 1) * piece, :]
            out[j, :, width : 2 * width] = mix[j * piece : (j + 1) * piece, :]
            out[j, :, 2 * width :] = tail

    on_core(place, run, score_mine, score_other)


def mix_kernel(blocks, latents, noised, fake_delta, gap_ref, apart, *, n_mp, loss_scale):
    base = noised[...].astype(F32)
    width = base.shape[1]
    fake = real = 0.0
    for j in range(n_mp):
        tail = blocks[j, :, 2 * width :]
        fake = fake + blocks[j, :, :width] * jnp.exp2(tail[0:1, 0:1])
        real = real + blocks[j, :, width : 2 * width] * jnp.exp2(tail[8:9, 0:1])
    fake = base + fake
    real_mix = base + real
    fake_delta[...] = (2.0 * (fake - latents[...]) * loss_scale).astype(BF16)
    apart[...] = fake - real_mix
    away = jnp.sum(jnp.abs(latents[...] - real_mix), axis=1, keepdims=True)
    gap_ref[...] = jnp.broadcast_to(jnp.sum(away, axis=0, keepdims=True), gap_ref.shape)


def pack_kernel(fake_delta, apart, gap_own, gap_other, out):
    width = apart.shape[1]
    fake = fake_delta[...].astype(F32)
    fake_power, apart_power = power_of(top_of(fake)), power_of(top_of(apart[...]))
    out[:, :width] = fake * jnp.exp2(-fake_power)
    out[:, width : 2 * width] = apart[...] * jnp.exp2(-apart_power)
    gap = gap_own[0:1, 0:1] + gap_other[0:1, 0:1]
    gap_power = power_of(gap)
    scaled = gap * jnp.exp2(-gap_power)
    high = jnp.floor(scaled * (1.0 / 16.0)) * 16.0
    line = lax.broadcasted_iota(jnp.int32, (fake.shape[0], LANES), 0)
    tail = jnp.where(line < 4, fake_power, apart_power)
    tail = jnp.where(line == 8, gap_power, tail)
    tail = jnp.where(line == 9, high, tail)
    out[:, 2 * width :] = jnp.where(line == 10, scaled - high, tail)


def back_kernel(place, blocks, *refs, n_mp, loss_scale, count, hidden):
    score_mine, score_other, gen_mine, gen_other = refs[:4]
    slopes, normed, active = refs[4:6], refs[6:8], refs[8:10]
    left, right, away = refs[10:]
    width = normed[0].shape[1]
    piece = blocks.shape[1]
    gap = 0.0
    for j in range(n_mp):
        tail = blocks[j, :, 2 * width :]
        gap = gap + (tail[9:10, 0:1] + tail[10:11, 0:1]) * jnp.exp2(tail[8:9, 0:1])
    weight = 1.0 / (gap / count + MEAN_EPS)
    for j in range(n_mp):
        tail = blocks[j, :, 2 * width :]
        fake = blocks[j, :, :width] * jnp.exp2(tail[0:1, 0:1])
        apart = blocks[j, :, width : 2 * width] * jnp.exp2(tail[4:5, 0:1])
        left[0, j * piece : (j + 1) * piece, :] = fake.astype(BF16)
        left[1, j * piece : (j + 1) * piece, :] = (apart * weight * loss_scale).astype(BF16)

    def run(score_out, gen_out):
        back = jnp.dot(left[0], score_out[:, :hidden], preferred_element_type=F32)
        right[0] = (back * slopes[0][...]).astype(BF16)
        back = jnp.dot(left[1], gen_out[...], preferred_element_type=F32)
        right[1] = (back * slopes[1][...]).astype(BF16)

    @pl.when(place[0] == 0)
    def _():
        run(score_other, gen_other)
        for m in range(2):
            away[m, :, :width] = left[m]
            away[m, :, width:] = active[m][...]
            left[m] = normed[m][...]

    @pl.when(place[0] != 0)
    def _():
        run(score_mine, gen_mine)
        for m in range(2):
            away[m, :, :width] = normed[m][...]
            away[m, :, width:] = right[m]
            right[m] = active[m][...]


def grad_kernel(left, right, came, out, both, grads, *, width, row_piece):
    rows = left.shape[1]
    size = (out.shape[1] - 16) // 2
    chunk = row_piece * 8
    powers = []
    for m in range(2):
        both[:rows, :width] = left[m]
        both[:rows, width:] = right[m]
        both[rows:, :] = came[m]
        turned = both[:, :width].T
        highest = jnp.zeros((8, LANES), F32)
        for c in range(width // chunk):
            block = jnp.dot(
                turned[c * chunk : (c + 1) * chunk, :], both[:, width:], preferred_element_type=F32
            )
            grads[c * chunk : (c + 1) * chunk, :] = block
            for t in range(block.shape[1] // LANES):
                lanes = jnp.abs(block[:, t * LANES : (t + 1) * LANES]).reshape(-1, 8, LANES)
                highest = jnp.maximum(highest, jnp.max(lanes, axis=0))
        power = power_of(top_of(highest))
        factor = jnp.exp2(-power)
        for d in range(width // row_piece):
            for t in range(grads.shape[1] // LANES):
                out[d, m * size + t * row_piece : m * size + (t + 1) * row_piece, :] = (
                    grads[d * row_piece : (d + 1) * row_piece, t * LANES : (t + 1) * LANES] * factor
                )
        powers.append(power)
    line = lax.broadcasted_iota(jnp.int32, (16, LANES), 0)
    tail = jnp.where(line < 8, powers[0], powers[1])
    for d in range(width // row_piece):
        out[d, 2 * size :, :] = tail


def local(
    latent_noise,
    score_noise,
    timesteps,
    classes,
    class_table,
    gen_weights,
    real_weights,
    fake_weights,
):
    group_index = lax.axis_index("group")
    core = group_index % 2
    y_lo = group_index // 2
    n_dp = lax.axis_size("dp")
    n_mp = lax.axis_size("mp")
    samples, positions, width = latent_noise.shape
    rows = positions // 2
    piece = rows // n_mp
    row_piece, _, hidden = gen_weights.shape
    loss_scale = 1.0 / math.sqrt(samples * n_dp * positions)
    place = jnp.stack([core, y_lo, lax.axis_index("mp")]).astype(jnp.int32)
    work = 2 * rows * width * hidden

    def outgoing(models):
        side = jnp.concatenate(models, axis=2)
        part_in = jnp.broadcast_to(side[None, :, 0], (n_dp,) + side[:, 0].shape)
        part_out = jnp.broadcast_to(side[None, :, 1], (n_dp,) + side[:, 1].shape)
        return jnp.concatenate([part_in, part_out, part_in, part_out], axis=0)

    def gather(blocks):
        return lax.all_to_all(blocks, PLANE, 0, 0, tiled=True).reshape(width, -1)

    own_class = lax.dynamic_index_in_dim(classes, y_lo, keepdims=False)
    embedding = lax.dynamic_index_in_dim(class_table, own_class, keepdims=True).astype(F32)
    own_step = lax.dynamic_index_in_dim(timesteps, y_lo, keepdims=False)
    phase_angle = 0.5 * jnp.pi / TSTEPS * own_step.astype(F32)
    signal_scale = jnp.cos(phase_angle)
    scales = jnp.stack([signal_scale, jnp.sin(phase_angle)])
    prepared = call(
        lambda *refs: prepare_kernel(*refs, piece=piece, n_mp=n_mp),
        "prepare",
        [latent_noise, score_noise, embedding],
        [place, scales],
        [shape((rows, width), BF16), shape((piece, width), F32), shape((piece, width), F32)],
    )

    gen_mine, score_blocks, prepared, embedding, signal_scale = lax.optimization_barrier(
        (
            gather(outgoing([gen_weights])),
            outgoing([fake_weights, real_weights]),
            prepared,
            embedding,
            signal_scale,
        )
    )
    normed_gen, stream, scaled_noise = prepared
    score_mine = gather(score_blocks)
    gen_other = core_swap(gen_mine)

    preact_gen, active_gen, *parts = call(
        lambda *refs: gen_kernel(*refs, piece=piece),
        "generate",
        [normed_gen, gen_mine, gen_other],
        [place],
        [shape((rows, hidden), F32), shape((rows, hidden), BF16)]
        + [shape((piece, width), BF16)] * n_mp,
        2 * work,
        [pltpu.VMEM((rows, width), BF16)],
    )
    total = sum(block.astype(F32) for block in to_owner(parts))
    latents = stream + total
    noised = (signal_scale * latents + scaled_noise).astype(BF16)

    score_mine, _ = lax.optimization_barrier((score_mine, noised))
    score_other = core_swap(score_mine)
    normed_cond, preact_fake, active_fake, score_parts = call(
        lambda *refs: score_kernel(*refs, piece=piece, n_mp=n_mp, hidden=hidden),
        "score",
        spread(noised) + [embedding, score_mine, score_other],
        [place],
        [
            shape((rows, width), BF16),
            shape((rows, hidden), F32),
            shape((rows, hidden), BF16),
            shape((n_mp, piece, 2 * width + LANES), F32),
        ],
        6 * work,
        [pltpu.VMEM((2 * rows, width), BF16)],
    )

    def exchange(blocks):
        return lax.all_to_all(blocks.astype(jnp.float16), "mp", 0, 0, tiled=True).astype(F32)

    fake_delta, gap_own, apart = call(
        lambda *refs: mix_kernel(*refs, n_mp=n_mp, loss_scale=loss_scale),
        "mix",
        [exchange(score_parts), latents, noised],
        [],
        [shape((piece, width), BF16), shape((8, LANES), F32), shape((piece, width), F32)],
    )
    (message,) = call(
        pack_kernel,
        "pack",
        [fake_delta, apart, gap_own, core_swap(gap_own)],
        [],
        [shape((piece, 2 * width + LANES), F32)],
    )

    def slope_of(preact):
        return jax.vjp(jax.nn.gelu, preact)[1](jnp.ones_like(preact))[0]

    left, right, away = call(
        lambda *refs: back_kernel(
            *refs, n_mp=n_mp, loss_scale=loss_scale, count=positions * width, hidden=hidden
        ),
        "back",
        [
            exchange(jnp.broadcast_to(message[None], (n_mp,) + message.shape)),
            score_mine,
            score_other,
            gen_mine,
            gen_other,
            slope_of(preact_fake),
            slope_of(preact_gen),
            normed_cond,
            normed_gen,
            active_fake,
            active_gen,
        ],
        [place],
        [
            shape((2, rows, width), BF16),
            shape((2, rows, hidden), BF16),
            shape((2, rows, width + hidden), BF16),
        ],
        2 * work,
    )
    size = row_piece * hidden // LANES
    (grads,) = call(
        lambda *refs: grad_kernel(*refs, width=width, row_piece=row_piece),
        "outer",
        [left, right, core_swap(away)],
        [],
        [shape((width // row_piece, 2 * size + 16, LANES), F32)],
        4 * work,
        [pltpu.VMEM((2 * rows, width + hidden), BF16), pltpu.VMEM((width, hidden), F32)],
    )
    came = lax.all_to_all(grads.astype(jnp.float16), PLANE, 0, 0, tiled=True)

    def collect(index):
        factor = jnp.exp2(came[:, 2 * size + 8 * index, 0].astype(F32))[:, None, None]
        own = came[:, index * size : (index + 1) * size].astype(F32) * factor
        summed = jnp.sum(own.reshape(2, 2, n_dp, size, LANES), axis=(0, 2))
        summed = summed.reshape(2, hidden // LANES, row_piece, LANES)
        return summed.transpose(2, 0, 1, 3).reshape(row_piece, 2, hidden)

    return (collect(1), collect(0))


def solution(mesh):
    return jax.shard_map(
        local,
        mesh=mesh,
        in_specs=(
            P("dp", None, None),
            P("dp", None, None),
            P("dp"),
            P("dp"),
            P(),
            P(("group", "dp"), None, "mp"),
            P(("group", "dp"), None, "mp"),
            P(("group", "dp"), None, "mp"),
        ),
        out_specs=(P(("group", "dp"), None, "mp"), P(("group", "dp"), None, "mp")),
        check_vma=False,
    )
```

time: 803 us -> 238 us (0.30)
  waiting for transfers between devices: 688 us -> 61.6 us
  blocking collectives: 0 us -> 71.9 us
  starting transfers between devices: 8.98 us -> 51.7 us
  other arithmetic: 41.1 us -> 15.7 us
  local copies, waits for them, and re-layouts: 42.2 us -> 22 us
  Pallas kernels: 0 us -> 10.4 us
  between operations: 14 us -> 3.71 us
    unnamed x6 -> x0, waiting for transfers between devices: 321 us -> none
    psum x3 -> x0, waiting for transfers between devices: 221 us -> none  [the longest x2 148 us: channel_total(): return lax.psum(partial_sum.astype(jnp.bfloat16), 'mp').astype(jnp.float32)]
    all_gather x1 -> x0, waiting for transfers between devices: 105 us -> none  [local(): collected = lax.all_gather(pred_f[None], 'group', axis=0, tiled=True)]
    all_to_all x0 -> x2, blocking collectives: none -> 71.9 us  [the longest x1 46.2 us: local(): came = lax.all_to_all(grads.astype(jnp.float16), PLANE, 0, 0, tiled=True)]
    ppermute x0 -> x18, starting transfers between devices: none -> 34.3 us  [the longest x14 30.4 us: shift(): lax.ppermute(block, 'mp', [(i, (i + step) % n_mp) for i in range(n_mp)])]
    another operation x3 -> x2, other arithmetic: 17.9 us -> 0.15 us  [the longest x1 0.08 us: local(): scales = jnp.stack([signal_scale, jnp.sin(phase_angle)])]
    unnamed x33 -> x57, local copies, waits for them, and re-layouts: 31.6 us -> 17.3 us
    ppermute x0 -> x18, waiting for transfers between devices: none -> 13.6 us  [the longest x14 7.06 us: shift(): lax.ppermute(block, 'mp', [(i, (i + step) % n_mp) for i in range(n_mp)])]
  transfers between devices with their start and end apart: 6 -> 21, of which waited for: 6 -> 11; matrix products, arithmetic and copies ran while one was open for 0% -> 4% of each run, Pallas kernels for 0% -> 1%
where the time goes in v1:
time: 238 us; the launch traced here: 237 us
  blocking collectives  71.9 us (30%)
  waiting for transfers between devices  61.6 us (26%)
  starting transfers between devices  51.7 us (22%)
  local copies, waits for them, and re-layouts  22 us (9%)
  other arithmetic  15.7 us (7%)
  Pallas kernels  10.4 us (4%)
  between operations  3.71 us (2%)
    all_to_all x1, blocking collectives, local(): came = lax.all_to_all(grads.astype(jnp.float16), PLANE, 0, 0, tiled=True)  46.2 us
    ppermute x14, starting transfers between devices, shift(): lax.ppermute(block, 'mp', [(i, (i + step) % n_mp) for i in range(n_mp)])  30.4 us
    all_to_all x2, waiting for transfers between devices, gather(): return lax.all_to_all(blocks, PLANE, 0, 0, tiled=True).reshape(width, -1)  30.3 us
    all_to_all x1, blocking collectives, exchange(): lax.all_to_all(blocks.astype(jnp.float16), 'mp', 0, 0, tiled=True)  25.6 us
    all_to_all x1, waiting for transfers between devices, exchange(): lax.all_to_all(blocks.astype(jnp.float16), 'mp', 0, 0, tiled=True)  17.7 us
    unnamed x57, local copies, waits for them, and re-layouts  17.3 us
    all_to_all x2, starting transfers between devices, gather(): return lax.all_to_all(blocks, PLANE, 0, 0, tiled=True).reshape(width, -1)  13.1 us
    pallas_call x7, Pallas kernels, call(): pl.pallas_call(body, name=name, out_shape=outs, in_specs=[SMEM] * len(sca...  10.4 us
  transfers between devices with their start and end apart: 21, of which 11 were waited for; matrix products, arithmetic and copies ran while one was open for 4% of the time, Pallas kernels for 1%

profile of v1, /device:TPU:1, one launch (start us, length us, event | category | flops | bytes accessed | tf_op | source)
XLA Modules:
  0.0 236.8 jit_solution(16886688845156495197)
XLA Ops:
  0.6 1.2 fusion.18
  1.9 1.4 pad_maximum_fusion.1
  3.4 8.7 %all-to-all-start = ((bf16[32,40,640]{2,1,0:T(8,128)(2,1)}), bf16[32,40,640]{2,1,0:T(8,128)(2,1)S(1)}, u32[]{:S(2)}, u32[]{:S(2)}) async-start(bf16[32,40,640]{2,1,0:T(8,128)(2,1)} %pad_maximum_fusion.1), calls=%async_computation | async-start | bytes 3276800 | tf_op jit(solution)/shard_map/all_to_all | solution.py:284
  17.0 1.3 copy-done.12
  19.1 1.0 copy_dynamic-update-slice_fusion
  20.3 2.0 pad_maximum_fusion
  22.3 13.9 %all-to-all-done = bf16[32,40,640]{2,1,0:T(8,128)(2,1)S(1)} async-done(((bf16[32,40,640]{2,1,0:T(8,128)(2,1)}), bf16[32,40,640]{2,1,0:T(8,128)(2,1)S(1)}, u32[]{:S(2)}, u32[]{:S(2)}) %all-to-all-start) | async-done | bytes 1638432 | tf_op jit(solution)/shard_map/all_to_all | solution.py:284
  36.2 1.2 copy-done
  37.3 4.4 %all-to-all-start.1 = ((bf16[32,40,1280]{2,1,0:T(8,128)(2,1)}), bf16[32,40,1280]{2,1,0:T(8,128)(2,1)S(1)}, u32[]{:S(2)}, u32[]{:S(2)}) async-start(bf16[32,40,1280]{2,1,0:T(8,128)(2,1)} %pad_maximum_fusion), calls=%async_computation.1 | async-start | bytes 6553600 | tf_op jit(solution)/shard_map/all_to_all | solution.py:284
  42.1 3.5 %collective-permute-done.refs_3_.refs_5_ = bf16[1280,640]{1,0:T(8,128)(2,1)S(1)} collective-permute-done((bf16[1280,640]{1,0:T(8,128)(2,1)}, bf16[1280,640]{1,0:T(8,128)(2,1)S(1)}, u32[]{:S(2)}, u32[]{:S(2)}) %collective-permute-start) | collective-permute-done | bytes 1638432 | tf_op jit(solution)/shard_map/ppermute | solution.py:57
  45.6 1.4 copy-done.1
  47.0 1.0 copy-done.9
  48.0 1.6 generate.1
  50.9 5.6 %collective-permute-start.1 = (bf16[16,1280]{1,0:T(8,128)(2,1)S(1)}, bf16[16,1280]{1,0:T(8,128)(2,1)S(1)}, u32[]{:S(2)}, u32[]{:S(2)}) collective-permute-start(bf16[16,1280]{1,0:T(8,128)(2,1)S(1)} %get-tuple-element.41), channel_id=1, source_target_pairs={{0,7},{1,0},{2,1},{3,2},{4,3},{5,4},{6,5},{7,6},{8,15},{9,8},{10,9... | collective-permute-start | bytes 122888 | tf_op jit(solution)/shard_map/ppermute | solution.py:62
  56.5 1.2 collective-permute-start.2
  58.1 4.5 %collective-permute-start.4 = (bf16[16,1280]{1,0:T(8,128)(2,1)S(1)}, bf16[16,1280]{1,0:T(8,128)(2,1)S(1)}, u32[]{:S(2)}, u32[]{:S(2)}) collective-permute-start(bf16[16,1280]{1,0:T(8,128)(2,1)S(1)} %get-tuple-element.44), channel_id=1, source_target_pairs={{0,4},{1,5},{2,6},{3,7},{4,0},{5,1},{6,2},{7,3},{8,12},{9,13},{10,... | collective-permute-start | bytes 122888 | tf_op jit(solution)/shard_map/ppermute | solution.py:62
  62.6 2.1 collective-permute-start.6
  64.7 1.5 collective-permute-start.7
  66.1 2.3 collective-permute-done.5
  68.5 1.3 collective-permute-done.6
  69.8 16.5 %all-to-all-done.1 = bf16[32,40,1280]{2,1,0:T(8,128)(2,1)S(1)} async-done(((bf16[32,40,1280]{2,1,0:T(8,128)(2,1)}), bf16[32,40,1280]{2,1,0:T(8,128)(2,1)S(1)}, u32[]{:S(2)}, u32[]{:S(2)}) %all-to-all-start.1) | async-done | bytes 3276832 | tf_op jit(solution)/shard_map/all_to_all | solution.py:284
  86.3 5.6 %collective-permute-start.14 = (bf16[16,1280]{1,0:T(8,128)(2,1)S(1)}, bf16[16,1280]{1,0:T(8,128)(2,1)S(1)}, u32[]{:S(2)}, u32[]{:S(2)}) collective-permute-start(bf16[16,1280]{1,0:T(8,128)(2,1)S(1)} %get-tuple-element.68.refs_1_.refs_2_), channel_id=1, source_target_pairs={{0,7},{1,0},{2,1},{3,2},{4,3},{5,4},{6,5},{7,6},{8,15},{9,8},{10,9... | collective-permute-start | bytes 122888 | tf_op jit(solution)/shard_map/ppermute | solution.py:62
  91.9 1.2 collective-permute-start.13
  93.5 4.5 %collective-permute-start.11 = (bf16[16,1280]{1,0:T(8,128)(2,1)S(1)}, bf16[16,1280]{1,0:T(8,128)(2,1)S(1)}, u32[]{:S(2)}, u32[]{:S(2)}) collective-permute-start(bf16[16,1280]{1,0:T(8,128)(2,1)S(1)} %get-tuple-element.68.refs_1_.refs_2_), channel_id=1, source_target_pairs={{0,4},{1,5},{2,6},{3,7},{4,0},{5,1},{6,2},{7,3},{8,12},{9,13},{10,... | collective-permute-start | bytes 122888 | tf_op jit(solution)/shard_map/ppermute | solution.py:62
  98.0 2.1 collective-permute-start.9
  100.0 1.5 collective-permute-start.8
  101.5 2.3 collective-permute-done.10.refs_4_
  103.8 1.0 collective-permute-done.9.refs_3_
  105.0 3.1 %score.1 = (bf16[128,1280]{1,0:T(8,128)(2,1)S(1)}, f32[128,640]{1,0:T(8,128)S(1)}, bf16[128,640]{1,0:T(8,128)(2,1)S(1)}, f32[8,16,2688]{2,1,0:T(8,128)S(1)}) custom-call(s32[3]{0:T(128)S(1)} %pad_add_fusion.refs_0_, bf16[16,1280]{1,0:T(8,128)(2,1)S(1)} %get-tuple-element.68.refs_1_.refs_2_, bf16[16,1280]{1,0:T(8,128)(2,1)S(1)} %collective-permute-done.8.refs_2_, ...), custom_call_target="tpu_custom_call" | custom-call | flops 1258291200 | bytes 9081856 | tf_op jit(solution)/shard_map/score/pallas_call | solution.py:25
  108.8 25.6 %all_to_all.25 = f16[8,16,2688]{2,1,0:T(8,128)(2,1)S(1)} all-to-all(f16[8,16,2688]{2,1,0:T(8,128)(2,1)S(1)} %convert_element_type.75), channel_id=1, replica_groups=mesh['group'=4,'dp'=8,'mp'=8] {'mp'}, dimensions={0} | all-to-all | bytes 1376256 | tf_op jit(solution)/shard_map/all_to_all | solution.py:345
  134.8 2.9 %collective-permute-start.16 = (f32[8,128]{1,0:T(8,128)S(1)}, f32[8,128]{1,0:T(8,128)S(1)}, u32[]{:S(2)}, u32[]{:S(2)}) collective-permute-start(f32[8,128]{1,0:T(8,128)S(1)} %get-tuple-element.55.gap_own), channel_id=1, source_target_pairs={{0,64},{64,0},{128,192},{192,128},{1,65},{65,1},{129,193},{193,129... | collective-permute-start | bytes 12296 | tf_op jit(solution)/shard_map/ppermute | solution.py:57
  138.6 1.0 broadcast_in_dim.44
  139.6 4.2 %all-to-all-start.3 = ((f16[8,16,2688]{2,1,0:T(8,128)(2,1)}), f16[8,16,2688]{2,1,0:T(8,128)(2,1)}, u32[]{:S(2)}, u32[]{:S(2)}) async-start(f16[8,16,2688]{2,1,0:T(8,128)(2,1)} %broadcast_in_dim.44), calls=%async_computation.3 | async-start | bytes 1376256 | tf_op jit(solution)/shard_map/all_to_all | solution.py:345
  143.8 1.9 fusion.11.refs_7_
  145.7 1.9 fusion.5.refs_6_
  147.6 17.7 %all-to-all-done.3 = f16[8,16,2688]{2,1,0:T(8,128)(2,1)} async-done(((f16[8,16,2688]{2,1,0:T(8,128)(2,1)}), f16[8,16,2688]{2,1,0:T(8,128)(2,1)}, u32[]{:S(2)}, u32[]{:S(2)}) %all-to-all-start.3) | async-done | bytes 688160 | tf_op jit(solution)/shard_map/all_to_all | solution.py:345
  165.3 1.2 convert_element_type.78.refs_1_
  166.5 1.4 copy-done.2
  167.9 1.4 copy-done.5
  169.3 1.0 copy-done.6
  170.3 1.0 copy-done.7
  174.1 2.8 %back.1 = (bf16[2,128,1280]{2,1,0:T(8,128)(2,1)S(1)}, bf16[2,128,640]{2,1,0:T(8,128)(2,1)S(1)}, bf16[2,128,1920]{2,1,0:T(8,128)(2,1)S(1)}) custom-call(s32[3]{0:T(128)S(1)} %pad_add_fusion.refs_0_, f32[8,16,2688]{2,1,0:T(8,128)S(1)} %convert_element_type.78.refs_1_, bf16[1280,1280]{1,0:T(8,128)(2,1)S(1)} %bitcast.25, bf16[1280,1280]{1,0:T(8,128)(2,1)} %copy-done.3, ...), custom_call_target="tpu_custom_call" | custom-call | flops 419430400 | bytes 14811136 | tf_op jit(solution)/shard_map/back/pallas_call | solution.py:25
  177.7 2.2 collective-permute-done.17.refs_2_
  179.9 1.8 outer.1
  182.2 46.2 %all_to_all.26 = f16[32,416,128]{2,1,0:T(8,128)(2,1)S(1)} all-to-all(f16[32,416,128]{2,1,0:T(8,128)(2,1)S(1)} %convert_element_type.79), channel_id=1, replica_groups=mesh['group'=4,'dp'=8,'mp'=8] {'group','dp'}, dimensions={0} | all-to-all | bytes 6815744 | tf_op jit(solution)/shard_map/all_to_all | solution.py:401
  228.8 2.4 %convert_multiply_fusion = (f32[32,200,128]{2,1,0:T(8,128)}, f32[32,200,128]{2,1,0:T(8,128)S(1)}) fusion(f16[32,416,128]{2,1,0:T(8,128)(2,1)S(1)} %all_to_all.26, f32[32]{0:T(128)S(1)} %get-tuple-element.66, f32[32]{0:T(128)S(1)} %get-tuple-element.67), kind=kLoop, calls=%fused_computation.1 | loop fusion | flops 3276800 | bytes 9830656 | tf_op jit(solution)/shard_map/mul | solution.py:405
  231.2 2.1 reduce_sum.19
  234.2 1.0 copy.18
  (88 shorter events, 14.9 us)
Async XLA Ops:
  1.8 10.3 %copy-start.24 = (s32[2]{0:T(128)S(1)}, s32[2]{0:T(128)}, u32[]{:S(2)}) copy-start(s32[2]{0:T(128)} %param.10) | copy-start | bytes 28
  1.8 11.7 %copy-start.25 = (s32[2]{0:T(128)S(1)}, s32[2]{0:T(128)}, u32[]{:S(2)}) copy-start(s32[2]{0:T(128)} %param.11) | copy-start | bytes 28
  1.8 15.1 %copy-start.11 = (bf16[2,256,1280]{2,1,0:T(8,128)(2,1)S(1)}, bf16[2,256,1280]{2,1,0:T(8,128)(2,1)}, u32[]{:S(2)}) copy-start(bf16[2,256,1280]{2,1,0:T(8,128)(2,1)} %refs_2_.1) | copy-start | bytes 3932164
  3.4 15.7 %copy-start.23 = (bf16[40,2,640]{2,1,0:T(2,128)(2,1)S(1)}, bf16[40,2,640]{2,1,0:T(2,128)(2,1)}, u32[]{:S(2)}) copy-start(bf16[40,2,640]{2,1,0:T(2,128)(2,1)} %param.15) | copy-start | bytes 307204
  3.4 32.8 %all-to-all-start = ((bf16[32,40,640]{2,1,0:T(8,128)(2,1)}), bf16[32,40,640]{2,1,0:T(8,128)(2,1)S(1)}, u32[]{:S(2)}, u32[]{:S(2)}) async-start(bf16[32,40,640]{2,1,0:T(8,128)(2,1)} %pad_maximum_fusion.1), calls=%async_computation | async-start | bytes 3276800 | tf_op jit(solution)/shard_map/all_to_all | solution.py:284
  17.0 1.3 copy-start.12
  19.0 1.2 copy-start.8
  19.0 1.2 copy-start.21
  36.2 1.2 copy-start
  37.3 48.9 %all-to-all-start.1 = ((bf16[32,40,1280]{2,1,0:T(8,128)(2,1)}), bf16[32,40,1280]{2,1,0:T(8,128)(2,1)S(1)}, u32[]{:S(2)}, u32[]{:S(2)}) async-start(bf16[32,40,1280]{2,1,0:T(8,128)(2,1)} %pad_maximum_fusion), calls=%async_computation.1 | async-start | bytes 6553600 | tf_op jit(solution)/shard_map/all_to_all | solution.py:284
  41.7 3.8 %collective-permute-start = (bf16[1280,640]{1,0:T(8,128)(2,1)}, bf16[1280,640]{1,0:T(8,128)(2,1)S(1)}, u32[]{:S(2)}, u32[]{:S(2)}) collective-permute-start(bf16[1280,640]{1,0:T(8,128)(2,1)} %bitcast.26), channel_id=1, source_target_pairs={{0,64},{64,0},{128,192},{192,128},{1,65},{65,1},{129,193},{193,129... | collective-permute-start | bytes 4915208 | tf_op jit(solution)/shard_map/ppermute | solution.py:57
  45.5 1.4 copy-start.1
  47.0 1.0 copy-start.9
  48.0 21.8 %copy-start.4 = (bf16[1280,640]{1,0:T(8,128)(2,1)}, bf16[1280,640]{1,0:T(8,128)(2,1)S(1)}, u32[]{:S(2)}) copy-start(bf16[1280,640]{1,0:T(8,128)(2,1)S(1)} %collective-permute-done.refs_3_.refs_5_) | copy-start | bytes 4915204
  48.0 21.8 %copy-start.22 = (f32[16,1280]{1,0:T(8,128)S(1)}, f32[16,1280]{1,0:T(8,128)}, u32[]{:S(2)}) copy-start(f32[16,1280]{1,0:T(8,128)} %copy-done.21) | copy-start | bytes 245764
  49.5 0.7 copy-start.15
  50.3 0.7 copy-start.17
  50.9 11.7 %collective-permute-start.1 = (bf16[16,1280]{1,0:T(8,128)(2,1)S(1)}, bf16[16,1280]{1,0:T(8,128)(2,1)S(1)}, u32[]{:S(2)}, u32[]{:S(2)}) collective-permute-start(bf16[16,1280]{1,0:T(8,128)(2,1)S(1)} %get-tuple-element.41), channel_id=1, source_target_pairs={{0,7},{1,0},{2,1},{3,2},{4,3},{5,4},{6,5},{7,6},{8,15},{9,8},{10,9... | collective-permute-start | bytes 122888 | tf_op jit(solution)/shard_map/ppermute | solution.py:62
  56.5 8.2 %collective-permute-start.2 = (bf16[16,1280]{1,0:T(8,128)(2,1)S(1)}, bf16[16,1280]{1,0:T(8,128)(2,1)S(1)}, u32[]{:S(2)}, u32[]{:S(2)}) collective-permute-start(bf16[16,1280]{1,0:T(8,128)(2,1)S(1)} %get-tuple-element.42), channel_id=1, source_target_pairs={{0,6},{1,7},{2,0},{3,1},{4,2},{5,3},{6,4},{7,5},{8,14},{9,15},{10,... | collective-permute-start | bytes 122888 | tf_op jit(solution)/shard_map/ppermute | solution.py:62
  57.7 8.5 %collective-permute-start.3 = (bf16[16,1280]{1,0:T(8,128)(2,1)S(1)}, bf16[16,1280]{1,0:T(8,128)(2,1)S(1)}, u32[]{:S(2)}, u32[]{:S(2)}) collective-permute-start(bf16[16,1280]{1,0:T(8,128)(2,1)S(1)} %get-tuple-element.43), channel_id=1, source_target_pairs={{0,5},{1,6},{2,7},{3,0},{4,1},{5,2},{6,3},{7,4},{8,13},{9,14},{10,... | collective-permute-start | bytes 122888 | tf_op jit(solution)/shard_map/ppermute | solution.py:62
  58.1 8.0 %collective-permute-start.4 = (bf16[16,1280]{1,0:T(8,128)(2,1)S(1)}, bf16[16,1280]{1,0:T(8,128)(2,1)S(1)}, u32[]{:S(2)}, u32[]{:S(2)}) collective-permute-start(bf16[16,1280]{1,0:T(8,128)(2,1)S(1)} %get-tuple-element.44), channel_id=1, source_target_pairs={{0,4},{1,5},{2,6},{3,7},{4,0},{5,1},{6,2},{7,3},{8,12},{9,13},{10,... | collective-permute-start | bytes 122888 | tf_op jit(solution)/shard_map/ppermute | solution.py:62
  62.6 5.9 %collective-permute-start.5 = (bf16[16,1280]{1,0:T(8,128)(2,1)S(1)}, bf16[16,1280]{1,0:T(8,128)(2,1)S(1)}, u32[]{:S(2)}, u32[]{:S(2)}) collective-permute-start(bf16[16,1280]{1,0:T(8,128)(2,1)S(1)} %get-tuple-element.45), channel_id=1, source_target_pairs={{0,3},{1,4},{2,5},{3,6},{4,7},{5,0},{6,1},{7,2},{8,11},{9,12},{10,... | collective-permute-start | bytes 122888 | tf_op jit(solution)/shard_map/ppermute | solution.py:62
  62.6 7.1 %collective-permute-start.6 = (bf16[16,1280]{1,0:T(8,128)(2,1)S(1)}, bf16[16,1280]{1,0:T(8,128)(2,1)S(1)}, u32[]{:S(2)}, u32[]{:S(2)}) collective-permute-start(bf16[16,1280]{1,0:T(8,128)(2,1)S(1)} %get-tuple-element.46), channel_id=1, source_target_pairs={{0,2},{1,3},{2,4},{3,5},{4,6},{5,7},{6,0},{7,1},{8,10},{9,11},{10,... | collective-permute-start | bytes 122888 | tf_op jit(solution)/shard_map/ppermute | solution.py:62
  64.7 5.1 %collective-permute-start.7 = (bf16[16,1280]{1,0:T(8,128)(2,1)S(1)}, bf16[16,1280]{1,0:T(8,128)(2,1)S(1)}, u32[]{:S(2)}, u32[]{:S(2)}) collective-permute-start(bf16[16,1280]{1,0:T(8,128)(2,1)S(1)} %get-tuple-element.47), channel_id=1, source_target_pairs={{0,1},{1,2},{2,3},{3,4},{4,5},{5,6},{6,7},{7,0},{8,9},{9,10},{10,1... | collective-permute-start | bytes 122888 | tf_op jit(solution)/shard_map/ppermute | solution.py:62
  86.3 18.7 %collective-permute-start.15 = (bf16[1280,1280]{1,0:T(8,128)(2,1)S(1)}, bf16[1280,1280]{1,0:T(8,128)(2,1)S(1)}, u32[]{:S(2)}, u32[]{:S(2)}) collective-permute-start(bf16[1280,1280]{1,0:T(8,128)(2,1)S(1)} %bitcast.23), channel_id=1, source_target_pairs={{0,64},{64,0},{128,192},{192,128},{1,65},{65,1},{129,193},{193,129... | collective-permute-start | bytes 9830408 | tf_op jit(solution)/shard_map/ppermute | solution.py:57
  86.3 11.7 %collective-permute-start.14 = (bf16[16,1280]{1,0:T(8,128)(2,1)S(1)}, bf16[16,1280]{1,0:T(8,128)(2,1)S(1)}, u32[]{:S(2)}, u32[]{:S(2)}) collective-permute-start(bf16[16,1280]{1,0:T(8,128)(2,1)S(1)} %get-tuple-element.68.refs_1_.refs_2_), channel_id=1, source_target_pairs={{0,7},{1,0},{2,1},{3,2},{4,3},{5,4},{6,5},{7,6},{8,15},{9,8},{10,9... | collective-permute-start | bytes 122888 | tf_op jit(solution)/shard_map/ppermute | solution.py:62
  91.9 6.1 %collective-permute-start.13 = (bf16[16,1280]{1,0:T(8,128)(2,1)S(1)}, bf16[16,1280]{1,0:T(8,128)(2,1)S(1)}, u32[]{:S(2)}, u32[]{:S(2)}) collective-permute-start(bf16[16,1280]{1,0:T(8,128)(2,1)S(1)} %get-tuple-element.68.refs_1_.refs_2_), channel_id=1, source_target_pairs={{0,6},{1,7},{2,0},{3,1},{4,2},{5,3},{6,4},{7,5},{8,14},{9,15},{10,... | collective-permute-start | bytes 122888 | tf_op jit(solution)/shard_map/ppermute | solution.py:62
  93.0 7.0 %collective-permute-start.12 = (bf16[16,1280]{1,0:T(8,128)(2,1)S(1)}, bf16[16,1280]{1,0:T(8,128)(2,1)S(1)}, u32[]{:S(2)}, u32[]{:S(2)}) collective-permute-start(bf16[16,1280]{1,0:T(8,128)(2,1)S(1)} %get-tuple-element.68.refs_1_.refs_2_), channel_id=1, source_target_pairs={{0,5},{1,6},{2,7},{3,0},{4,1},{5,2},{6,3},{7,4},{8,13},{9,14},{10,... | collective-permute-start | bytes 122888 | tf_op jit(solution)/shard_map/ppermute | solution.py:62
  93.5 8.0 %collective-permute-start.11 = (bf16[16,1280]{1,0:T(8,128)(2,1)S(1)}, bf16[16,1280]{1,0:T(8,128)(2,1)S(1)}, u32[]{:S(2)}, u32[]{:S(2)}) collective-permute-start(bf16[16,1280]{1,0:T(8,128)(2,1)S(1)} %get-tuple-element.68.refs_1_.refs_2_), channel_id=1, source_target_pairs={{0,4},{1,5},{2,6},{3,7},{4,0},{5,1},{6,2},{7,3},{8,12},{9,13},{10,... | collective-permute-start | bytes 122888 | tf_op jit(solution)/shard_map/ppermute | solution.py:62
  98.0 5.9 %collective-permute-start.10 = (bf16[16,1280]{1,0:T(8,128)(2,1)S(1)}, bf16[16,1280]{1,0:T(8,128)(2,1)S(1)}, u32[]{:S(2)}, u32[]{:S(2)}) collective-permute-start(bf16[16,1280]{1,0:T(8,128)(2,1)S(1)} %get-tuple-element.68.refs_1_.refs_2_), channel_id=1, source_target_pairs={{0,3},{1,4},{2,5},{3,6},{4,7},{5,0},{6,1},{7,2},{8,11},{9,12},{10,... | collective-permute-start | bytes 122888 | tf_op jit(solution)/shard_map/ppermute | solution.py:62
  98.0 6.9 %collective-permute-start.9 = (bf16[16,1280]{1,0:T(8,128)(2,1)S(1)}, bf16[16,1280]{1,0:T(8,128)(2,1)S(1)}, u32[]{:S(2)}, u32[]{:S(2)}) collective-permute-start(bf16[16,1280]{1,0:T(8,128)(2,1)S(1)} %get-tuple-element.68.refs_1_.refs_2_), channel_id=1, source_target_pairs={{0,2},{1,3},{2,4},{3,5},{4,6},{5,7},{6,0},{7,1},{8,10},{9,11},{10,... | collective-permute-start | bytes 122888 | tf_op jit(solution)/shard_map/ppermute | solution.py:62
  100.0 4.9 %collective-permute-start.8 = (bf16[16,1280]{1,0:T(8,128)(2,1)S(1)}, bf16[16,1280]{1,0:T(8,128)(2,1)S(1)}, u32[]{:S(2)}, u32[]{:S(2)}) collective-permute-start(bf16[16,1280]{1,0:T(8,128)(2,1)S(1)} %get-tuple-element.68.refs_1_.refs_2_), channel_id=1, source_target_pairs={{0,1},{1,2},{2,3},{3,4},{4,5},{5,6},{6,7},{7,0},{8,9},{9,10},{10,1... | collective-permute-start | bytes 122888 | tf_op jit(solution)/shard_map/ppermute | solution.py:62
  105.0 3.1 %copy-start.3 = (bf16[1280,1280]{1,0:T(8,128)(2,1)}, bf16[1280,1280]{1,0:T(8,128)(2,1)S(1)}, u32[]{:S(2)}) copy-start(bf16[1280,1280]{1,0:T(8,128)(2,1)S(1)} %collective-permute-done.15.refs_11_.refs_3_) | copy-start | bytes 9830404
  108.0 0.8 copy-start.13
  108.1 26.7 %copy-start.16 = (f32[128,640]{1,0:T(8,128)}, f32[128,640]{1,0:T(8,128)S(1)}, u32[]{:S(2)}) copy-start(f32[128,640]{1,0:T(8,128)S(1)} %get-tuple-element.56) | copy-start | bytes 983044
  108.1 26.7 %copy-start.19 = (bf16[128,640]{1,0:T(8,128)(2,1)}, bf16[128,640]{1,0:T(8,128)(2,1)S(1)}, u32[]{:S(2)}) copy-start(bf16[128,640]{1,0:T(8,128)(2,1)S(1)} %get-tuple-element.59.refs_10_) | copy-start | bytes 491524
  134.8 31.7 %copy-start.18 = (bf16[128,640]{1,0:T(8,128)(2,1)S(1)}, bf16[128,640]{1,0:T(8,128)(2,1)}, u32[]{:S(2)}) copy-start(bf16[128,640]{1,0:T(8,128)(2,1)} %copy-done.17) | copy-start | bytes 491524
  134.8 3.7 %collective-permute-start.16 = (f32[8,128]{1,0:T(8,128)S(1)}, f32[8,128]{1,0:T(8,128)S(1)}, u32[]{:S(2)}, u32[]{:S(2)}) collective-permute-start(f32[8,128]{1,0:T(8,128)S(1)} %get-tuple-element.55.gap_own), channel_id=1, source_target_pairs={{0,64},{64,0},{128,192},{192,128},{1,65},{65,1},{129,193},{193,129... | collective-permute-start | bytes 12296 | tf_op jit(solution)/shard_map/ppermute | solution.py:57
  139.6 25.7 %all-to-all-start.3 = ((f16[8,16,2688]{2,1,0:T(8,128)(2,1)}), f16[8,16,2688]{2,1,0:T(8,128)(2,1)}, u32[]{:S(2)}, u32[]{:S(2)}) async-start(f16[8,16,2688]{2,1,0:T(8,128)(2,1)} %broadcast_in_dim.44), calls=%async_computation.3 | async-start | bytes 1376256 | tf_op jit(solution)/shard_map/all_to_all | solution.py:345
  166.5 1.4 copy-start.2
  167.9 1.4 copy-start.5
  169.3 1.0 copy-start.6
  170.3 1.0 copy-start.7
  171.3 1.0 copy-start.10
  172.3 1.0 copy-start.14
  173.2 0.9 copy-start.20
  177.0 2.9 %collective-permute-start.17 = (bf16[2,128,1920]{2,1,0:T(8,128)(2,1)S(1)}, bf16[2,128,1920]{2,1,0:T(8,128)(2,1)S(1)}, u32[]{:S(2)}, u32[]{:S(2)}) collective-permute-start(bf16[2,128,1920]{2,1,0:T(8,128)(2,1)S(1)} %get-tuple-element.63), channel_id=1, source_target_pairs={{0,64},{64,0},{128,192},{192,128},{1,65},{65,1},{129,193},{193,129... | collective-permute-start | bytes 2949128 | tf_op jit(solution)/shard_map/ppermute | solution.py:57

commit v2 on v1

v2 whole, which is shorter than its diff:
```python
import math

import jax
import jax.numpy as jnp
from jax import lax
from jax.experimental import pallas as pl
from jax.experimental.pallas import tpu as pltpu
from jax.sharding import PartitionSpec as P

TSTEPS = 1000
GUIDANCE = 3.0
EPSILON = 1e-06
MEAN_EPS = 1e-05

PLANE = ("group", "dp")
LANES = 128
WALK = [(0, 0), (1, 0), (2, 0), (3, 0), (3, 1), (2, 1), (1, 1), (1, 2)]
WALK += [(2, 2), (3, 2), (3, 3), (2, 3), (1, 3), (0, 3), (0, 2), (0, 1)]
SLOTS = [
    (WALK.index((x, y_hi * 2 + y_lo)), core)
    for y_lo in range(2)
    for core in range(2)
    for x in range(4)
    for y_hi in range(2)
]
PEERS = [[((y % 2) * 2 + core) * 8 + x * 2 + y // 2 for x, y in WALK] for core in range(2)]
SMEM = pl.BlockSpec(memory_space=pltpu.SMEM)
VMEM = pl.BlockSpec(memory_space=pltpu.VMEM)
F32 = jnp.float32
BF16 = jnp.bfloat16


def call(body, name, inputs, scalars, outs, flops=0, scratch=()):
    moved = sum(math.prod(a.shape) * a.dtype.itemsize for a in list(inputs) + list(outs))
    return pl.pallas_call(
        body,
        name=name,
        out_shape=outs,
        in_specs=[SMEM] * len(scalars) + [VMEM] * len(inputs),
        out_specs=[VMEM] * len(outs),
        scratch_shapes=list(scratch),
        compiler_params=pltpu.CompilerParams(vmem_limit_bytes=40 * 2**20),
        cost_estimate=pl.CostEstimate(flops=flops, bytes_accessed=moved, transcendentals=0),
    )(*scalars, *inputs)


def shape(dims, dtype):
    return jax.ShapeDtypeStruct(dims, dtype)


def normalize(summed):
    factor = lax.rsqrt(jnp.mean(summed * summed, axis=-1, keepdims=True) + EPSILON)
    return (summed * factor).astype(BF16)


def dot_t(left, right):
    return lax.dot_general(left, right, (((1,), (1,)), ((), ())), preferred_element_type=F32)


def forward_part(normed, w_in, w_out):
    preact = jnp.dot(normed, w_in, preferred_element_type=F32)
    active = jax.nn.gelu(preact).astype(BF16)
    return preact, active, dot_t(active, w_out).astype(BF16)


def core_swap(block):
    return lax.ppermute(block, "group", [(0, 1), (1, 0), (2, 3), (3, 2)])


def shift(block, step):
    n_mp = lax.axis_size("mp")
    return lax.ppermute(block, "mp", [(i, (i + step) % n_mp) for i in range(n_mp)])


def spread(block):
    return [block] + [shift(block, k) for k in range(1, lax.axis_size("mp"))]


def to_owner(blocks):
    return [blocks[0]] + [shift(blocks[k], -k) for k in range(1, len(blocks))]


def on_core(place, run, mine, other):
    pl.when(place[0] == 0)(lambda: run(mine, other))
    pl.when(place[0] != 0)(lambda: run(other, mine))


def power_of(peak):
    return jnp.floor(jnp.log(jnp.maximum(peak, 1e-30)) * (1.0 / math.log(2.0))) - 13.0


def top_of(value):
    by_row = jnp.max(jnp.abs(value), axis=1, keepdims=True)
    return jnp.max(by_row, axis=0, keepdims=True)


def ring_place(place, k, piece, n_mp):
    return pl.multiple_of(lax.rem(place[2] + n_mp - k, n_mp) * piece, piece)


def lay_kernel(*refs):
    models, out = refs[:-1], refs[-1]
    count = out.shape[0] // 4
    if len(models) == 1:
        wholes = [models[0][:, side, :] for side in range(2)]
    else:
        wholes = [jnp.concatenate([m[:, 0, :], m[:, 1, :]], axis=1) for m in models]
    for core, whole in enumerate(wholes):
        for d in range(count):
            out[core * count + d] = whole
            out[(2 + core) * count + d] = whole


def prepare_kernel(place, scales, latent, noise, embed, normed, stream, scaled, *, piece):
    rows = latent[place[1]].astype(F32)
    normed[...] = normalize(rows + embed[...])
    at = pl.multiple_of(place[0] * (rows.shape[0] // 2) + place[2] * piece, piece)
    stream[...] = latent[place[1], pl.ds(at, piece), :].astype(F32)
    scaled[...] = scales[1] * noise[place[1], pl.ds(at, piece), :].astype(F32)


def gen_kernel(place, normed, mine, other, *refs, piece):
    preact_ref, active_ref, parts, whole = refs[0], refs[1], refs[2:-1], refs[-1]
    rows = whole.shape[0]
    own = normed[pl.ds(pl.multiple_of(place[0] * rows, rows), rows), :]

    def run(w_in, w_out):
        preact, active, partial = forward_part(own, w_in[...], w_out[...])
        preact_ref[...] = preact
        active_ref[...] = active
        whole[...] = partial

    on_core(place, run, mine, other)
    for k, part in enumerate(parts):
        part[...] = whole[pl.ds(ring_place(place, k, piece, len(parts)), piece), :]


def order_kernel(place, *refs):
    blocks, out = refs[:-1], refs[-1]
    piece = blocks[0].shape[0]
    for k, block in enumerate(blocks):
        out[pl.ds(ring_place(place, k, piece, len(blocks)), piece), :] = block[...]


def score_kernel(place, own, came, embed, weights, normed, preact_ref, active_ref, out, both):
    half, width = own.shape
    rows = 2 * half
    n_mp, piece = out.shape[0], out.shape[1] // 2
    hidden = weights.shape[1] // 2
    for source, core in ((own, place[0]), (came, 1 - place[0])):
        at = pl.multiple_of(core * half, half)
        summed = source[...].astype(F32)
        both[pl.ds(at, half), :] = normalize(summed + embed[...])
        both[pl.ds(pl.multiple_of(rows + at, half), half), :] = normalize(summed)
    normed[...] = both[:rows, :]

    def finish(value):
        power = power_of(top_of(value))
        value = value * jnp.exp2(-power)
        tail = jnp.broadcast_to(power, (2 * piece, LANES))
        for j in range(n_mp):
            for h in range(2):
                at = h * half + j * piece
                out[j, h * piece : (h + 1) * piece, :width] = value[at : at + piece, :]
            out[j, :, width:] = tail

    @pl.when(place[0] == 0)
    def _():
        preact, active, fake = forward_part(both[:rows, :], weights[:, :hidden], weights[:, hidden:])
        preact_ref[...] = preact
        active_ref[...] = active
        finish(fake.astype(F32))

    @pl.when(place[0] != 0)
    def _():
        preact, active, real = forward_part(both[...], weights[:, :hidden], weights[:, hidden:])
        preact_ref[...] = preact[:rows]
        active_ref[...] = active[:rows]
        uncond, cond = real[rows:].astype(F32), real[:rows].astype(F32)
        finish(uncond + GUIDANCE * (cond - uncond))


def total_kernel(blocks, out):
    width = out.shape[1]
    total = 0.0
    for j in range(blocks.shape[0]):
        total = total + blocks[j, :, :width] * jnp.exp2(blocks[j, 0:1, width : width + 1])
    out[...] = total


def pack_kernel(place, own, other, near, far, out, *, loss_scale):
    width = own.shape[1]
    piece = near.shape[1]
    first = place[0] == 0

    def run(fake_sum, real_sum, low, high):
        latents = jnp.concatenate([low[0], high[0]], axis=0)
        base = jnp.concatenate([low[1], high[1]], axis=0)
        fake = base + fake_sum[...]
        real_mix = base + real_sum[...]
        away = jnp.sum(jnp.abs(latents - real_mix), axis=1, keepdims=True)
        gap = jnp.sum(away, axis=0, keepdims=True)
        fake_delta = (2.0 * (fake - latents) * loss_scale).astype(BF16).astype(F32)
        value = jnp.where(first, fake_delta, fake - real_mix)
        power = power_of(top_of(value))
        out[:, :width] = value * jnp.exp2(-power)
        gap_power = power_of(gap)
        scaled = gap * jnp.exp2(-gap_power)
        coarse = jnp.floor(scaled * (1.0 / 16.0)) * 16.0
        line = lax.broadcasted_iota(jnp.int32, (2 * piece, LANES), 0)
        tail = jnp.where(line == 8, gap_power, power)
        tail = jnp.where(line == 9, coarse, tail)
        out[:, width:] = jnp.where(line == 10, scaled - coarse, tail)

    pl.when(first)(lambda: run(own, other, near, far))
    pl.when(place[0] != 0)(lambda: run(other, own, far, near))


def grad_kernel(
    place, blocks, weights, slope, normed, active, out, delta, grads, *, loss_scale, count, row_piece
):
    n_mp, piece = blocks.shape[0], blocks.shape[1] // 2
    rows, width = normed.shape
    hidden = active.shape[1]
    half = rows // 2
    gap = 0.0
    for j in range(n_mp):
        tail = blocks[j, :, width:]
        gap = gap + (tail[9:10, 0:1] + tail[10:11, 0:1]) * jnp.exp2(tail[8:9, 0:1])
    first = place[0] == 0
    weight = jnp.where(first, 1.0, 1.0 / (gap / count + MEAN_EPS))
    scale = jnp.where(first, 1.0, loss_scale)
    for j in range(n_mp):
        value = blocks[j, :, :width] * jnp.exp2(blocks[j, 0:1, width : width + 1])
        value = (value * weight * scale).astype(BF16)
        for h in range(2):
            at = h * half + j * piece
            delta[at : at + piece, :] = value[h * piece : (h + 1) * piece, :]
    size = row_piece * hidden // LANES
    chunk = row_piece * 8
    turned = delta[...].T
    powers = []

    def outer(side, turned, right):
        highest = jnp.zeros((8, LANES), F32)
        for c in range(width // chunk):
            block = jnp.dot(
                turned[c * chunk : (c + 1) * chunk, :], right, preferred_element_type=F32
            )
            grads[c * chunk : (c + 1) * chunk, :] = block
            for t in range(hidden // LANES):
                lanes = jnp.abs(block[:, t * LANES : (t + 1) * LANES]).reshape(-1, 8, LANES)
                highest = jnp.maximum(highest, jnp.max(lanes, axis=0))
        power = power_of(top_of(highest))
        factor = jnp.exp2(-power)
        for owner, (slot, part) in enumerate(SLOTS):
            for t in range(hidden // LANES):
                to = (part * 2 + side) * size + t * row_piece
                out[slot, to : to + row_piece, :] = (
                    grads[
                        owner * row_piece : (owner + 1) * row_piece,
                        t * LANES : (t + 1) * LANES,
                    ]
                    * factor
                )
        powers.append(power)

    outer(1, turned, active[...])
    back = jnp.dot(delta[...], weights[...], preferred_element_type=F32)
    outer(0, normed[...].T, (back * slope[...]).astype(BF16))
    line = lax.broadcasted_iota(jnp.int32, (16, LANES), 0)
    tail = jnp.where(line < 8, powers[1], powers[0])
    for d in range(out.shape[0]):
        out[d, 4 * size :, :] = tail


def collect_kernel(place, came, own, away):
    sources = came.shape[0]
    size = (came.shape[1] - 16) // 4
    for side in range(2):
        factors = [
            jnp.exp2(came[i, 4 * size + 8 * side : 4 * size + 8 * side + 1, 0:1])
            for i in range(sources)
        ]
        for out, core in ((own, place[0]), (away, 1 - place[0])):
            at = pl.multiple_of((core * 2 + side) * size, 8)
            total = came[0, pl.ds(at, size), :] * factors[0]
            for i in range(1, sources):
                total = total + came[i, pl.ds(at, size), :] * factors[i]
            out[side * size : (side + 1) * size, :] = total


def place_kernel(place, own, came, *outs):
    rows = outs[0].shape[0]
    tiles = outs[0].shape[2] // LANES

    def run(sources):
        for out, ref in zip(outs, sources):
            for side in range(2):
                for t in range(tiles):
                    at = (side * tiles + t) * rows
                    out[:, side, t * LANES : (t + 1) * LANES] = ref[at : at + rows, :]

    pl.when(place[0] == 0)(lambda: run((own, came)))
    pl.when(place[0] != 0)(lambda: run((came, own)))


def local(
    latent_noise,
    score_noise,
    timesteps,
    classes,
    class_table,
    gen_weights,
    real_weights,
    fake_weights,
):
    group_index = lax.axis_index("group")
    core = group_index % 2
    y_lo = group_index // 2
    n_dp = lax.axis_size("dp")
    n_mp = lax.axis_size("mp")
    samples, positions, width = latent_noise.shape
    rows = positions // 2
    piece = rows // n_mp
    row_piece, _, hidden = gen_weights.shape
    loss_scale = 1.0 / math.sqrt(samples * n_dp * positions)
    place = jnp.stack([core, y_lo, lax.axis_index("mp")]).astype(jnp.int32)
    work = 2 * rows * width * hidden

    def outgoing(models):
        lanes = hidden * len(models)
        return call(
            lay_kernel, "lay", models, [], [shape((4 * n_dp, row_piece, lanes), BF16)]
        )[0]

    def gather(blocks):
        return lax.all_to_all(blocks, PLANE, 0, 0, tiled=True).reshape(width, -1)

    own_class = lax.dynamic_index_in_dim(classes, y_lo, keepdims=False)
    embedding = lax.dynamic_index_in_dim(class_table, own_class, keepdims=True).astype(F32)
    own_step = lax.dynamic_index_in_dim(timesteps, y_lo, keepdims=False)
    phase_angle = 0.5 * jnp.pi / TSTEPS * own_step.astype(F32)
    signal_scale = jnp.cos(phase_angle)
    scales = jnp.stack([signal_scale, jnp.sin(phase_angle)])
    prepared = call(
        lambda *refs: prepare_kernel(*refs, piece=piece),
        "prepare",
        [latent_noise, score_noise, embedding],
        [place, scales],
        [
            shape((positions, width), BF16),
            shape((piece, width), F32),
            shape((piece, width), F32),
        ],
    )

    gen_mine, score_blocks, prepared, embedding, signal_scale = lax.optimization_barrier(
        (
            gather(outgoing([gen_weights])),
            outgoing([fake_weights, real_weights]),
            prepared,
            embedding,
            signal_scale,
        )
    )
    normed_gen, stream, scaled_noise = prepared
    score_weights = gather(score_blocks)
    gen_other = core_swap(gen_mine)

    preact_gen, active_gen, *parts = call(
        lambda *refs: gen_kernel(*refs, piece=piece),
        "generate",
        [normed_gen, gen_mine, gen_other],
        [place],
        [shape((rows, hidden), F32), shape((rows, hidden), BF16)]
        + [shape((piece, width), BF16)] * n_mp,
        2 * work,
        [pltpu.VMEM((rows, width), BF16)],
    )
    total = sum(block.astype(F32) for block in to_owner(parts))
    latents = stream + total
    noised = (signal_scale * latents + scaled_noise).astype(BF16)

    (noised_own,) = call(
        order_kernel, "order", spread(noised), [place], [shape((rows, width), BF16)]
    )
    score_weights, noised_own = lax.optimization_barrier((score_weights, noised_own))
    near = jnp.stack([latents, noised.astype(F32)])
    normed_cond, preact_fake, active_fake, score_parts = call(
        score_kernel,
        "score",
        [noised_own, core_swap(noised_own), embedding, score_weights],
        [place],
        [
            shape((positions, width), BF16),
            shape((positions, hidden), F32),
            shape((positions, hidden), BF16),
            shape((n_mp, 2 * piece, width + LANES), F32),
        ],
        8 * work,
        [pltpu.VMEM((2 * positions, width), BF16)],
    )

    def exchange(blocks):
        return lax.all_to_all(blocks.astype(jnp.float16), "mp", 0, 0, tiled=True).astype(F32)

    (total,) = call(
        total_kernel, "total", [exchange(score_parts)], [], [shape((2 * piece, width), F32)]
    )
    (message,) = call(
        lambda *refs: pack_kernel(*refs, loss_scale=loss_scale),
        "pack",
        [total, core_swap(total), near, core_swap(near)],
        [place],
        [shape((2 * piece, width + LANES), F32)],
    )

    first = core == 0

    def chosen(fake_value, gen_value):
        gen_all = jnp.concatenate([core_swap(gen_value), gen_value], axis=0)
        return jnp.where(first, fake_value, gen_all)

    preact = chosen(preact_fake, preact_gen)
    slope = jax.vjp(jax.nn.gelu, preact)[1](jnp.ones_like(preact))[0]
    size = row_piece * hidden // LANES
    (grads,) = call(
        lambda *refs: grad_kernel(
            *refs, loss_scale=loss_scale, count=positions * width, row_piece=row_piece
        ),
        "grads",
        [
            exchange(jnp.broadcast_to(message[None], (n_mp,) + message.shape)),
            jnp.where(first, score_weights[:, hidden:], gen_mine),
            slope,
            jnp.where(first, normed_cond, normed_gen),
            chosen(active_fake, active_gen),
        ],
        [place],
        [shape((len(WALK), 4 * size + 16, LANES), F32)],
        6 * work,
        [pltpu.VMEM((positions, width), BF16), pltpu.VMEM((width, hidden), F32)],
    )
    came = lax.all_to_all(
        grads.astype(jnp.float16), PLANE, 0, 0, axis_index_groups=PEERS, tiled=True
    )
    own, away = call(
        collect_kernel,
        "collect",
        [came.astype(F32)],
        [place],
        [shape((2 * size, LANES), F32)] * 2,
    )
    fake_grad, gen_grad = call(
        place_kernel,
        "place",
        [own, core_swap(away)],
        [place],
        [shape((row_piece, 2, hidden), F32)] * 2,
    )
    return (gen_grad, fake_grad)


def solution(mesh):
    return jax.shard_map(
        local,
        mesh=mesh,
        in_specs=(
            P("dp", None, None),
            P("dp", None, None),
            P("dp"),
            P("dp"),
            P(),
            P(("group", "dp"), None, "mp"),
            P(("group", "dp"), None, "mp"),
            P(("group", "dp"), None, "mp"),
        ),
        out_specs=(P(("group", "dp"), None, "mp"), P(("group", "dp"), None, "mp")),
        check_vma=False,
    )
```

time: 238 us -> 209 us (0.88)
  blocking collectives: 71.9 us -> 44.7 us
  local copies, waits for them, and re-layouts: 22 us -> 7.18 us
  waiting for transfers between devices: 61.6 us -> 71.1 us
  other arithmetic: 15.7 us -> 8.48 us
  Pallas kernels: 10.4 us -> 17.1 us
  starting transfers between devices: 51.7 us -> 56.4 us
    all_to_all x2 -> x1, blocking collectives: 71.9 us -> 44.7 us  [local(): lax.all_to_all(grads.astype(jnp.float16), PLANE, 0, 0, axis_index_groups=...]
    all_to_all x1 -> x2, waiting for transfers between devices: 17.7 us -> 37.8 us  [exchange(): lax.all_to_all(blocks.astype(jnp.float16), 'mp', 0, 0, tiled=True)]
    all_to_all x2, waiting for transfers between devices: 30.3 us -> 16.1 us  [gather(): return lax.all_to_all(blocks, PLANE, 0, 0, tiled=True).reshape(width, -1)]
    unnamed x57 -> x32, local copies, waits for them, and re-layouts: 17.3 us -> 5.08 us
    pallas_call x7 -> x11, Pallas kernels: 10.4 us -> 17.1 us  [call(): pl.pallas_call(body, name=name, out_shape=outs, in_specs=[SMEM] * len(sca...]
    all_to_all x1 -> x2, starting transfers between devices: 4.2 us -> 10.6 us  [exchange(): lax.all_to_all(blocks.astype(jnp.float16), 'mp', 0, 0, tiled=True)]
    ppermute x14, waiting for transfers between devices: 7.06 us -> 10.9 us  [shift(): lax.ppermute(block, 'mp', [(i, (i + step) % n_mp) for i in range(n_mp)])]
    concatenate x2 -> x0, other arithmetic: 3.43 us -> none  [outgoing(): return jnp.concatenate([part_in, part_out, part_in, part_out], axis=0)]
  transfers between devices with their start and end apart: 21 -> 25, of which waited for: 11 -> 13; matrix products, arithmetic and copies ran while one was open for 4% -> 4% of each run, Pallas kernels for 1% -> 2%
where the time goes in v2:
time: 209 us
  waiting for transfers between devices  71.1 us (34%)
  starting transfers between devices  56.4 us (27%)
  blocking collectives  44.7 us (21%)
  Pallas kernels  17.1 us (8%)
  other arithmetic  8.48 us (4%)
  local copies, waits for them, and re-layouts  7.18 us (3%)
  between operations  3.7 us (2%)
    all_to_all x1, blocking collectives, local(): lax.all_to_all(grads.astype(jnp.float16), PLANE, 0, 0, axis_index_groups=...  44.7 us
    all_to_all x2, waiting for transfers between devices, exchange(): lax.all_to_all(blocks.astype(jnp.float16), 'mp', 0, 0, tiled=True)  37.8 us
    ppermute x14, starting transfers between devices, shift(): lax.ppermute(block, 'mp', [(i, (i + step) % n_mp) for i in range(n_mp)])  28.1 us
    pallas_call x11, Pallas kernels, call(): pl.pallas_call(body, name=name, out_shape=outs, in_specs=[SMEM] * len(sca...  17.1 us
    all_to_all x2, waiting for transfers between devices, gather(): return lax.all_to_all(blocks, PLANE, 0, 0, tiled=True).reshape(width, -1)  16.1 us
    all_to_all x2, starting transfers between devices, gather(): return lax.all_to_all(blocks, PLANE, 0, 0, tiled=True).reshape(width, -1)  13.3 us
    ppermute x14, waiting for transfers between devices, shift(): lax.ppermute(block, 'mp', [(i, (i + step) % n_mp) for i in range(n_mp)])  10.9 us
    all_to_all x2, starting transfers between devices, exchange(): lax.all_to_all(blocks.astype(jnp.float16), 'mp', 0, 0, tiled=True)  10.6 us
  transfers between devices with their start and end apart: 25, of which 13 were waited for; matrix products, arithmetic and copies ran while one was open for 4% of the time, Pallas kernels for 2%

profile of v2, /device:TPU:1, one launch (start us, length us, event | category | flops | bytes accessed | tf_op | source)
XLA Modules:
  0.0 208.6 jit_solution(8954197026882031918)
XLA Ops:
  0.6 0.9 copy-done.11
  1.5 1.5 lay.2
  3.0 8.7 %all-to-all-start = ((bf16[32,40,640]{2,1,0:T(8,128)(2,1)}), bf16[32,40,640]{2,1,0:T(8,128)(2,1)S(1)}, u32[]{:S(2)}, u32[]{:S(2)}) async-start(bf16[32,40,640]{2,1,0:T(8,128)(2,1)} %lay.2), calls=%async_computation | async-start | bytes 3276800 | tf_op jit(solution)/shard_map/all_to_all | solution.py:338
  16.2 1.7 copy-done
  18.1 0.7 dynamic-slice_convert_fusion.refs_4_.embed
  18.8 0.8 prepare.1
  19.7 16.1 %all-to-all-done = bf16[32,40,640]{2,1,0:T(8,128)(2,1)S(1)} async-done(((bf16[32,40,640]{2,1,0:T(8,128)(2,1)}), bf16[32,40,640]{2,1,0:T(8,128)(2,1)S(1)}, u32[]{:S(2)}, u32[]{:S(2)}) %all-to-all-start) | async-done | bytes 1638432 | tf_op jit(solution)/shard_map/all_to_all | solution.py:338
  35.8 4.6 %all-to-all-start.1 = ((bf16[32,40,1280]{2,1,0:T(8,128)(2,1)}), bf16[32,40,1280]{2,1,0:T(8,128)(2,1)}, u32[]{:S(2)}, u32[]{:S(2)}) async-start(bf16[32,40,1280]{2,1,0:T(8,128)(2,1)} %copy-done), calls=%async_computation.1 | async-start | bytes 6553600 | tf_op jit(solution)/shard_map/all_to_all | solution.py:338
  40.7 3.4 %collective-permute-done.refs_3_ = bf16[1280,640]{1,0:T(8,128)(2,1)S(1)} collective-permute-done((bf16[1280,640]{1,0:T(8,128)(2,1)S(1)}, bf16[1280,640]{1,0:T(8,128)(2,1)S(1)}, u32[]{:S(2)}, u32[]{:S(2)}) %collective-permute-start) | collective-permute-done | bytes 1638432 | tf_op jit(solution)/shard_map/ppermute | solution.py:67
  44.0 2.3 %generate.1 = (f32[128,640]{1,0:T(8,128)}, bf16[128,640]{1,0:T(8,128)(2,1)S(1)}, bf16[16,1280]{1,0:T(8,128)(2,1)S(1)}, bf16[16,1280]{1,0:T(8,128)(2,1)S(1)}, bf1...) custom-call(s32[3]{0:T(128)S(1)} %pad_add_fusion.refs_0_.place, ...), custom_call_target="tpu_custom_call" | custom-call | flops 419430400 | bytes 4751360 | tf_op jit(solution)/shard_map/generate/pallas_call | solution.py:35
  46.3 5.6 %collective-permute-start.1 = (bf16[16,1280]{1,0:T(8,128)(2,1)S(1)}, bf16[16,1280]{1,0:T(8,128)(2,1)S(1)}, u32[]{:S(2)}, u32[]{:S(2)}) collective-permute-start(bf16[16,1280]{1,0:T(8,128)(2,1)S(1)} %get-tuple-element.41), channel_id=1, source_target_pairs={{0,7},{1,0},{2,1},{3,2},{4,3},{5,4},{6,5},{7,6},{8,15},{9,8},{10,9... | collective-permute-start | bytes 122888 | tf_op jit(solution)/shard_map/ppermute | solution.py:72
  51.9 1.2 collective-permute-start.2
  53.5 4.5 %collective-permute-start.4 = (bf16[16,1280]{1,0:T(8,128)(2,1)S(1)}, bf16[16,1280]{1,0:T(8,128)(2,1)S(1)}, u32[]{:S(2)}, u32[]{:S(2)}) collective-permute-start(bf16[16,1280]{1,0:T(8,128)(2,1)S(1)} %get-tuple-element.44), channel_id=1, source_target_pairs={{0,4},{1,5},{2,6},{3,7},{4,0},{5,1},{6,2},{7,3},{8,12},{9,13},{10,... | collective-permute-start | bytes 122888 | tf_op jit(solution)/shard_map/ppermute | solution.py:72
  58.0 2.1 collective-permute-start.6
  60.1 1.5 collective-permute-start.7
  61.6 2.7 %collective-permute-done.5 = bf16[16,1280]{1,0:T(8,128)(2,1)S(1)} collective-permute-done((bf16[16,1280]{1,0:T(8,128)(2,1)S(1)}, bf16[16,1280]{1,0:T(8,128)(2,1)S(1)}, u32[]{:S(2)}, u32[]{:S(2)}) %collective-permute-start.5) | collective-permute-done | bytes 40992 | tf_op jit(solution)/shard_map/ppermute | solution.py:72
  64.3 1.5 collective-permute-done.6
  65.8 2.3 %collective-permute-start.14 = (bf16[16,1280]{1,0:T(8,128)(2,1)S(1)}, bf16[16,1280]{1,0:T(8,128)(2,1)S(1)}, u32[]{:S(2)}, u32[]{:S(2)}) collective-permute-start(bf16[16,1280]{1,0:T(8,128)(2,1)S(1)} %get-tuple-element.63.refs_0_), channel_id=1, source_target_pairs={{0,7},{1,0},{2,1},{3,2},{4,3},{5,4},{6,5},{7,6},{8,15},{9,8},{10,9... | collective-permute-start | bytes 122888 | tf_op jit(solution)/shard_map/ppermute | solution.py:72
  68.2 1.7 collective-permute-start.13
  69.8 2.5 %collective-permute-start.12 = (bf16[16,1280]{1,0:T(8,128)(2,1)S(1)}, bf16[16,1280]{1,0:T(8,128)(2,1)S(1)}, u32[]{:S(2)}, u32[]{:S(2)}) collective-permute-start(bf16[16,1280]{1,0:T(8,128)(2,1)S(1)} %get-tuple-element.63.refs_0_), channel_id=1, source_target_pairs={{0,5},{1,6},{2,7},{3,0},{4,1},{5,2},{6,3},{7,4},{8,13},{9,14},{10,... | collective-permute-start | bytes 122888 | tf_op jit(solution)/shard_map/ppermute | solution.py:72
  72.3 1.3 collective-permute-start.11
  73.6 1.8 collective-permute-start.10
  75.4 3.0 %collective-permute-start.9 = (bf16[16,1280]{1,0:T(8,128)(2,1)S(1)}, bf16[16,1280]{1,0:T(8,128)(2,1)S(1)}, u32[]{:S(2)}, u32[]{:S(2)}) collective-permute-start(bf16[16,1280]{1,0:T(8,128)(2,1)S(1)} %get-tuple-element.63.refs_0_), channel_id=1, source_target_pairs={{0,2},{1,3},{2,4},{3,5},{4,6},{5,7},{6,0},{7,1},{8,10},{9,11},{10,... | collective-permute-start | bytes 122888 | tf_op jit(solution)/shard_map/ppermute | solution.py:72
  79.3 1.0 collective-permute-done.10.refs_3_
  80.2 3.0 %collective-permute-done.9.refs_2_ = bf16[16,1280]{1,0:T(8,128)(2,1)S(1)} collective-permute-done((bf16[16,1280]{1,0:T(8,128)(2,1)S(1)}, bf16[16,1280]{1,0:T(8,128)(2,1)S(1)}, u32[]{:S(2)}, u32[]{:S(2)}) %collective-permute-start.9) | collective-permute-done | bytes 40992 | tf_op jit(solution)/shard_map/ppermute | solution.py:72
  83.3 2.1 %collective-permute-done.8.refs_1_ = bf16[16,1280]{1,0:T(8,128)(2,1)S(1)} collective-permute-done((bf16[16,1280]{1,0:T(8,128)(2,1)S(1)}, bf16[16,1280]{1,0:T(8,128)(2,1)S(1)}, u32[]{:S(2)}, u32[]{:S(2)}) %collective-permute-start.8) | collective-permute-done | bytes 40992 | tf_op jit(solution)/shard_map/ppermute | solution.py:72
  86.0 1.2 collective-permute-start.15
  87.2 1.3 collective-permute-done.15.came
  88.5 5.0 %score.1 = (bf16[256,1280]{1,0:T(8,128)(2,1)S(1)}, f32[256,640]{1,0:T(8,128)S(1)}, bf16[256,640]{1,0:T(8,128)(2,1)S(1)}, f32[8,32,1408]{2,1,0:T(8,128)S(1)}) custom-call(s32[3]{0:T(128)S(1)} %pad_add_fusion.refs_0_.place, bf16[128,1280]{1,0:T(8,128)(2,1)S(1)} %order.1.own, bf16[128,1280]{1,0:T(8,128)(2,1)S(1)} %collective-permute-done.15.came, ...), custom_call_target="tpu_custom_call" | custom-call | flops 1677721600 | bytes 7017472 | tf_op jit(solution)/shard_map/score/pallas_call | solution.py:35
  93.4 0.9 copy-done.5
  94.3 0.8 copy-done.7
  95.9 0.9 convert_element_type.65
  96.8 6.2 %all-to-all-start.2 = ((f16[8,32,1408]{2,1,0:T(8,128)(2,1)}), f16[8,32,1408]{2,1,0:T(8,128)(2,1)S(1)}, u32[]{:S(2)}, u32[]{:S(2)}) async-start(f16[8,32,1408]{2,1,0:T(8,128)(2,1)} %convert_element_type.65), calls=%async_computation.2 | async-start | bytes 1441792 | tf_op jit(solution)/shard_map/all_to_all | solution.py:406
  103.2 22.0 %all-to-all-done.2 = f16[8,32,1408]{2,1,0:T(8,128)(2,1)S(1)} async-done(((f16[8,32,1408]{2,1,0:T(8,128)(2,1)}), f16[8,32,1408]{2,1,0:T(8,128)(2,1)S(1)}, u32[]{:S(2)}, u32[]{:S(2)}) %all-to-all-start.2) | async-done | bytes 720928 | tf_op jit(solution)/shard_map/all_to_all | solution.py:406
  127.0 0.7 pack.1
  127.8 0.9 broadcast_in_dim.2
  128.7 4.4 %all-to-all-start.3 = ((f16[8,32,1408]{2,1,0:T(8,128)(2,1)}), f16[8,32,1408]{2,1,0:T(8,128)(2,1)}, u32[]{:S(2)}, u32[]{:S(2)}) async-start(f16[8,32,1408]{2,1,0:T(8,128)(2,1)} %broadcast_in_dim.2), calls=%async_computation.3 | async-start | bytes 1441792 | tf_op jit(solution)/shard_map/all_to_all | solution.py:406
  133.2 1.7 slice_select_fusion.refs_2_
  134.9 1.1 maximum_select_fusion.1.refs_5_
  136.0 1.5 fusion.5.refs_3_
  137.6 15.8 %all-to-all-done.3 = f16[8,32,1408]{2,1,0:T(8,128)(2,1)} async-done(((f16[8,32,1408]{2,1,0:T(8,128)(2,1)}), f16[8,32,1408]{2,1,0:T(8,128)(2,1)}, u32[]{:S(2)}, u32[]{:S(2)}) %all-to-all-start.3) | async-done | bytes 720928 | tf_op jit(solution)/shard_map/all_to_all | solution.py:406
  153.4 1.2 convert_element_type.68.refs_1_
  154.6 2.9 %grads.1 = f32[16,816,128]{2,1,0:T(8,128)S(1)} custom-call(s32[3]{0:T(128)S(1)} %pad_add_fusion.refs_0_.place, f32[8,32,1408]{2,1,0:T(8,128)S(1)} %convert_element_type.68.refs_1_, bf16[1280,640]{1,0:T(8,128)(2,1)S(1)} %slice_select_fusion.refs_2_, f32[256,640]{1,0:T(8,128)S(1)} %fusion.5.refs_3_, bf16[256,1280]{1,0:T(8,128)(2,1)S(1)} %broadcast_select_fusion.refs_4_, ...), custom_call_target="tpu_custom_call" | custom-call | flops 1258291200 | bytes 11403264 | tf_op jit(solution)/shard_map/grads/pallas_call | solution.py:35
  158.0 44.7 %all_to_all.25 = f16[16,816,128]{2,1,0:T(8,128)(2,1)S(1)} all-to-all(f16[16,816,128]{2,1,0:T(8,128)(2,1)S(1)} %convert_element_type.69), channel_id=1, replica_groups={{0,16,32,48,176,160,144,24,40,56,184,168,152,136,8,128},{64,80,96,112,2..., dimensions={0} | all-to-all | bytes 6684672 | tf_op jit(solution)/shard_map/all_to_all | solution.py:445
  203.1 1.1 collect.1
  204.2 1.8 collective-permute-start.20
  206.0 1.1 collective-permute-done.20.came
  207.1 1.5 place.1
  (64 shorter events, 7.7 us)
Async XLA Ops:
  0.6 0.9 copy-start.11
  3.0 8.8 %copy-start.14 = (s32[2]{0:T(128)S(1)}, s32[2]{0:T(128)}, u32[]{:S(2)}) copy-start(s32[2]{0:T(128)} %param.10) | copy-start | bytes 28
  3.0 10.2 %copy-start.15 = (s32[2]{0:T(128)S(1)}, s32[2]{0:T(128)}, u32[]{:S(2)}) copy-start(s32[2]{0:T(128)} %param.11) | copy-start | bytes 28
  3.0 12.7 %copy-start.12 = (bf16[40,2,640]{2,1,0:T(2,128)(2,1)S(1)}, bf16[40,2,640]{2,1,0:T(2,128)(2,1)}, u32[]{:S(2)}) copy-start(bf16[40,2,640]{2,1,0:T(2,128)(2,1)} %refs_0_.3) | copy-start | bytes 307204
  3.0 12.7 %copy-start.13 = (bf16[40,2,640]{2,1,0:T(2,128)(2,1)S(1)}, bf16[40,2,640]{2,1,0:T(2,128)(2,1)}, u32[]{:S(2)}) copy-start(bf16[40,2,640]{2,1,0:T(2,128)(2,1)} %refs_1_.1) | copy-start | bytes 307204
  3.0 32.8 %all-to-all-start = ((bf16[32,40,640]{2,1,0:T(8,128)(2,1)}), bf16[32,40,640]{2,1,0:T(8,128)(2,1)S(1)}, u32[]{:S(2)}, u32[]{:S(2)}) async-start(bf16[32,40,640]{2,1,0:T(8,128)(2,1)} %lay.2), calls=%async_computation | async-start | bytes 3276800 | tf_op jit(solution)/shard_map/all_to_all | solution.py:338
  15.7 3.1 %copy-start.3 = (bf16[2,256,1280]{2,1,0:T(8,128)(2,1)S(1)}, bf16[2,256,1280]{2,1,0:T(8,128)(2,1)}, u32[]{:S(2)}) copy-start(bf16[2,256,1280]{2,1,0:T(8,128)(2,1)} %refs_2_.1) | copy-start | bytes 3932164
  15.7 3.1 %copy-start.4 = (bf16[2,256,1280]{2,1,0:T(8,128)(2,1)S(1)}, bf16[2,256,1280]{2,1,0:T(8,128)(2,1)}, u32[]{:S(2)}) copy-start(bf16[2,256,1280]{2,1,0:T(8,128)(2,1)} %refs_3_.1) | copy-start | bytes 3932164
  16.2 1.7 copy-start
  19.7 24.4 %copy-start.1 = (bf16[256,1280]{1,0:T(8,128)(2,1)}, bf16[256,1280]{1,0:T(8,128)(2,1)S(1)}, u32[]{:S(2)}) copy-start(bf16[256,1280]{1,0:T(8,128)(2,1)S(1)} %get-tuple-element.38.refs_1_) | copy-start | bytes 1966084
  35.8 50.2 %all-to-all-start.1 = ((bf16[32,40,1280]{2,1,0:T(8,128)(2,1)}), bf16[32,40,1280]{2,1,0:T(8,128)(2,1)}, u32[]{:S(2)}, u32[]{:S(2)}) async-start(bf16[32,40,1280]{2,1,0:T(8,128)(2,1)} %copy-done), calls=%async_computation.1 | async-start | bytes 6553600 | tf_op jit(solution)/shard_map/all_to_all | solution.py:338
  40.4 3.6 %collective-permute-start = (bf16[1280,640]{1,0:T(8,128)(2,1)S(1)}, bf16[1280,640]{1,0:T(8,128)(2,1)S(1)}, u32[]{:S(2)}, u32[]{:S(2)}) collective-permute-start(bf16[1280,640]{1,0:T(8,128)(2,1)S(1)} %bitcast.11), channel_id=1, source_target_pairs={{0,64},{64,0},{128,192},{192,128},{1,65},{65,1},{129,193},{193,129... | collective-permute-start | bytes 4915208 | tf_op jit(solution)/shard_map/ppermute | solution.py:67
  46.3 11.7 %collective-permute-start.1 = (bf16[16,1280]{1,0:T(8,128)(2,1)S(1)}, bf16[16,1280]{1,0:T(8,128)(2,1)S(1)}, u32[]{:S(2)}, u32[]{:S(2)}) collective-permute-start(bf16[16,1280]{1,0:T(8,128)(2,1)S(1)} %get-tuple-element.41), channel_id=1, source_target_pairs={{0,7},{1,0},{2,1},{3,2},{4,3},{5,4},{6,5},{7,6},{8,15},{9,8},{10,9... | collective-permute-start | bytes 122888 | tf_op jit(solution)/shard_map/ppermute | solution.py:72
  51.9 8.2 %collective-permute-start.2 = (bf16[16,1280]{1,0:T(8,128)(2,1)S(1)}, bf16[16,1280]{1,0:T(8,128)(2,1)S(1)}, u32[]{:S(2)}, u32[]{:S(2)}) collective-permute-start(bf16[16,1280]{1,0:T(8,128)(2,1)S(1)} %get-tuple-element.42), channel_id=1, source_target_pairs={{0,6},{1,7},{2,0},{3,1},{4,2},{5,3},{6,4},{7,5},{8,14},{9,15},{10,... | collective-permute-start | bytes 122888 | tf_op jit(solution)/shard_map/ppermute | solution.py:72
  53.1 8.5 %collective-permute-start.3 = (bf16[16,1280]{1,0:T(8,128)(2,1)S(1)}, bf16[16,1280]{1,0:T(8,128)(2,1)S(1)}, u32[]{:S(2)}, u32[]{:S(2)}) collective-permute-start(bf16[16,1280]{1,0:T(8,128)(2,1)S(1)} %get-tuple-element.43), channel_id=1, source_target_pairs={{0,5},{1,6},{2,7},{3,0},{4,1},{5,2},{6,3},{7,4},{8,13},{9,14},{10,... | collective-permute-start | bytes 122888 | tf_op jit(solution)/shard_map/ppermute | solution.py:72
  53.5 8.0 %collective-permute-start.4 = (bf16[16,1280]{1,0:T(8,128)(2,1)S(1)}, bf16[16,1280]{1,0:T(8,128)(2,1)S(1)}, u32[]{:S(2)}, u32[]{:S(2)}) collective-permute-start(bf16[16,1280]{1,0:T(8,128)(2,1)S(1)} %get-tuple-element.44), channel_id=1, source_target_pairs={{0,4},{1,5},{2,6},{3,7},{4,0},{5,1},{6,2},{7,3},{8,12},{9,13},{10,... | collective-permute-start | bytes 122888 | tf_op jit(solution)/shard_map/ppermute | solution.py:72
  58.0 6.3 %collective-permute-start.5 = (bf16[16,1280]{1,0:T(8,128)(2,1)S(1)}, bf16[16,1280]{1,0:T(8,128)(2,1)S(1)}, u32[]{:S(2)}, u32[]{:S(2)}) collective-permute-start(bf16[16,1280]{1,0:T(8,128)(2,1)S(1)} %get-tuple-element.45), channel_id=1, source_target_pairs={{0,3},{1,4},{2,5},{3,6},{4,7},{5,0},{6,1},{7,2},{8,11},{9,12},{10,... | collective-permute-start | bytes 122888 | tf_op jit(solution)/shard_map/ppermute | solution.py:72
  58.0 7.7 %collective-permute-start.6 = (bf16[16,1280]{1,0:T(8,128)(2,1)S(1)}, bf16[16,1280]{1,0:T(8,128)(2,1)S(1)}, u32[]{:S(2)}, u32[]{:S(2)}) collective-permute-start(bf16[16,1280]{1,0:T(8,128)(2,1)S(1)} %get-tuple-element.46), channel_id=1, source_target_pairs={{0,2},{1,3},{2,4},{3,5},{4,6},{5,7},{6,0},{7,1},{8,10},{9,11},{10,... | collective-permute-start | bytes 122888 | tf_op jit(solution)/shard_map/ppermute | solution.py:72
  60.1 5.7 %collective-permute-start.7 = (bf16[16,1280]{1,0:T(8,128)(2,1)S(1)}, bf16[16,1280]{1,0:T(8,128)(2,1)S(1)}, u32[]{:S(2)}, u32[]{:S(2)}) collective-permute-start(bf16[16,1280]{1,0:T(8,128)(2,1)S(1)} %get-tuple-element.47), channel_id=1, source_target_pairs={{0,1},{1,2},{2,3},{3,4},{4,5},{5,6},{6,7},{7,0},{8,9},{9,10},{10,1... | collective-permute-start | bytes 122888 | tf_op jit(solution)/shard_map/ppermute | solution.py:72
  65.8 9.6 %collective-permute-start.14 = (bf16[16,1280]{1,0:T(8,128)(2,1)S(1)}, bf16[16,1280]{1,0:T(8,128)(2,1)S(1)}, u32[]{:S(2)}, u32[]{:S(2)}) collective-permute-start(bf16[16,1280]{1,0:T(8,128)(2,1)S(1)} %get-tuple-element.63.refs_0_), channel_id=1, source_target_pairs={{0,7},{1,0},{2,1},{3,2},{4,3},{5,4},{6,5},{7,6},{8,15},{9,8},{10,9... | collective-permute-start | bytes 122888 | tf_op jit(solution)/shard_map/ppermute | solution.py:72
  68.2 10.2 %collective-permute-start.13 = (bf16[16,1280]{1,0:T(8,128)(2,1)S(1)}, bf16[16,1280]{1,0:T(8,128)(2,1)S(1)}, u32[]{:S(2)}, u32[]{:S(2)}) collective-permute-start(bf16[16,1280]{1,0:T(8,128)(2,1)S(1)} %get-tuple-element.63.refs_0_), channel_id=1, source_target_pairs={{0,6},{1,7},{2,0},{3,1},{4,2},{5,3},{6,4},{7,5},{8,14},{9,15},{10,... | collective-permute-start | bytes 122888 | tf_op jit(solution)/shard_map/ppermute | solution.py:72
  69.8 8.9 %collective-permute-start.12 = (bf16[16,1280]{1,0:T(8,128)(2,1)S(1)}, bf16[16,1280]{1,0:T(8,128)(2,1)S(1)}, u32[]{:S(2)}, u32[]{:S(2)}) collective-permute-start(bf16[16,1280]{1,0:T(8,128)(2,1)S(1)} %get-tuple-element.63.refs_0_), channel_id=1, source_target_pairs={{0,5},{1,6},{2,7},{3,0},{4,1},{5,2},{6,3},{7,4},{8,13},{9,14},{10,... | collective-permute-start | bytes 122888 | tf_op jit(solution)/shard_map/ppermute | solution.py:72
  72.3 6.9 %collective-permute-start.11 = (bf16[16,1280]{1,0:T(8,128)(2,1)S(1)}, bf16[16,1280]{1,0:T(8,128)(2,1)S(1)}, u32[]{:S(2)}, u32[]{:S(2)}) collective-permute-start(bf16[16,1280]{1,0:T(8,128)(2,1)S(1)} %get-tuple-element.63.refs_0_), channel_id=1, source_target_pairs={{0,4},{1,5},{2,6},{3,7},{4,0},{5,1},{6,2},{7,3},{8,12},{9,13},{10,... | collective-permute-start | bytes 122888 | tf_op jit(solution)/shard_map/ppermute | solution.py:72
  73.6 6.6 %collective-permute-start.10 = (bf16[16,1280]{1,0:T(8,128)(2,1)S(1)}, bf16[16,1280]{1,0:T(8,128)(2,1)S(1)}, u32[]{:S(2)}, u32[]{:S(2)}) collective-permute-start(bf16[16,1280]{1,0:T(8,128)(2,1)S(1)} %get-tuple-element.63.refs_0_), channel_id=1, source_target_pairs={{0,3},{1,4},{2,5},{3,6},{4,7},{5,0},{6,1},{7,2},{8,11},{9,12},{10,... | collective-permute-start | bytes 122888 | tf_op jit(solution)/shard_map/ppermute | solution.py:72
  75.4 7.9 %collective-permute-start.9 = (bf16[16,1280]{1,0:T(8,128)(2,1)S(1)}, bf16[16,1280]{1,0:T(8,128)(2,1)S(1)}, u32[]{:S(2)}, u32[]{:S(2)}) collective-permute-start(bf16[16,1280]{1,0:T(8,128)(2,1)S(1)} %get-tuple-element.63.refs_0_), channel_id=1, source_target_pairs={{0,2},{1,3},{2,4},{3,5},{4,6},{5,7},{6,0},{7,1},{8,10},{9,11},{10,... | collective-permute-start | bytes 122888 | tf_op jit(solution)/shard_map/ppermute | solution.py:72
  78.4 7.0 %collective-permute-start.8 = (bf16[16,1280]{1,0:T(8,128)(2,1)S(1)}, bf16[16,1280]{1,0:T(8,128)(2,1)S(1)}, u32[]{:S(2)}, u32[]{:S(2)}) collective-permute-start(bf16[16,1280]{1,0:T(8,128)(2,1)S(1)} %get-tuple-element.63.refs_0_), channel_id=1, source_target_pairs={{0,1},{1,2},{2,3},{3,4},{4,5},{5,6},{6,7},{7,0},{8,9},{9,10},{10,1... | collective-permute-start | bytes 122888 | tf_op jit(solution)/shard_map/ppermute | solution.py:72
  86.0 2.5 %collective-permute-start.15 = (bf16[128,1280]{1,0:T(8,128)(2,1)S(1)}, bf16[128,1280]{1,0:T(8,128)(2,1)S(1)}, u32[]{:S(2)}, u32[]{:S(2)}) collective-permute-start(bf16[128,1280]{1,0:T(8,128)(2,1)S(1)} %order.1.own), channel_id=1, source_target_pairs={{0,64},{64,0},{128,192},{192,128},{1,65},{65,1},{129,193},{193,129... | collective-permute-start | bytes 983048 | tf_op jit(solution)/shard_map/ppermute | solution.py:67
  93.4 0.9 copy-start.5
  94.3 0.8 copy-start.7
  95.1 0.7 copy-start.9
  96.8 28.3 %all-to-all-start.2 = ((f16[8,32,1408]{2,1,0:T(8,128)(2,1)}), f16[8,32,1408]{2,1,0:T(8,128)(2,1)S(1)}, u32[]{:S(2)}, u32[]{:S(2)}) async-start(f16[8,32,1408]{2,1,0:T(8,128)(2,1)} %convert_element_type.65), calls=%async_computation.2 | async-start | bytes 1441792 | tf_op jit(solution)/shard_map/all_to_all | solution.py:406
  103.1 23.5 %collective-permute-start.17 = (f32[2,16,1280]{2,1,0:T(8,128)S(1)}, f32[2,16,1280]{2,1,0:T(8,128)S(1)}, u32[]{:S(2)}, u32[]{:S(2)}) collective-permute-start(f32[2,16,1280]{2,1,0:T(8,128)S(1)} %pad_maximum_fusion.refs_3_), channel_id=1, source_target_pairs={{0,64},{64,0},{128,192},{192,128},{1,65},{65,1},{129,193},{193,129... | collective-permute-start | bytes 491528 | tf_op jit(solution)/shard_map/ppermute | solution.py:67
  125.5 1.6 collective-permute-start.16
  126.0 8.9 %collective-permute-start.19 = (bf16[128,640]{1,0:T(8,128)(2,1)S(1)}, bf16[128,640]{1,0:T(8,128)(2,1)}, u32[]{:S(2)}, u32[]{:S(2)}) collective-permute-start(bf16[128,640]{1,0:T(8,128)(2,1)S(1)} %get-tuple-element.57), channel_id=1, source_target_pairs={{0,64},{64,0},{128,192},{192,128},{1,65},{65,1},{129,193},{193,129... | collective-permute-start | bytes 491528 | tf_op jit(solution)/shard_map/ppermute | solution.py:67
  126.1 9.9 %collective-permute-start.18 = (f32[128,640]{1,0:T(8,128)}, f32[128,640]{1,0:T(8,128)}, u32[]{:S(2)}, u32[]{:S(2)}) collective-permute-start(f32[128,640]{1,0:T(8,128)} %get-tuple-element.54), channel_id=1, source_target_pairs={{0,64},{64,0},{128,192},{192,128},{1,65},{65,1},{129,193},{193,129... | collective-permute-start | bytes 983048 | tf_op jit(solution)/shard_map/ppermute | solution.py:67
  128.7 24.7 %all-to-all-start.3 = ((f16[8,32,1408]{2,1,0:T(8,128)(2,1)}), f16[8,32,1408]{2,1,0:T(8,128)(2,1)}, u32[]{:S(2)}, u32[]{:S(2)}) async-start(f16[8,32,1408]{2,1,0:T(8,128)(2,1)} %broadcast_in_dim.2), calls=%async_computation.3 | async-start | bytes 1441792 | tf_op jit(solution)/shard_map/all_to_all | solution.py:406
  133.2 1.7 copy-start.10
  133.2 2.9 %copy-start.8 = (f32[256,640]{1,0:T(8,128)S(1)}, f32[256,640]{1,0:T(8,128)}, u32[]{:S(2)}) copy-start(f32[256,640]{1,0:T(8,128)} %copy-done.7) | copy-start | bytes 1966084
  134.9 2.7 %copy-start.2 = (bf16[256,1280]{1,0:T(8,128)(2,1)S(1)}, bf16[256,1280]{1,0:T(8,128)(2,1)}, u32[]{:S(2)}) copy-start(bf16[256,1280]{1,0:T(8,128)(2,1)} %copy-done.1) | copy-start | bytes 1966084
  134.9 2.7 %copy-start.6 = (bf16[256,1280]{1,0:T(8,128)(2,1)S(1)}, bf16[256,1280]{1,0:T(8,128)(2,1)}, u32[]{:S(2)}) copy-start(bf16[256,1280]{1,0:T(8,128)(2,1)} %copy-done.5) | copy-start | bytes 1966084
  204.2 2.9 %collective-permute-start.20 = (f32[400,128]{1,0:T(8,128)S(1)}, f32[400,128]{1,0:T(8,128)S(1)}, u32[]{:S(2)}, u32[]{:S(2)}) collective-permute-start(f32[400,128]{1,0:T(8,128)S(1)} %get-tuple-element.59), channel_id=1, source_target_pairs={{0,64},{64,0},{128,192},{192,128},{1,65},{65,1},{129,193},{193,129... | collective-permute-start | bytes 614408 | tf_op jit(solution)/shard_map/ppermute | solution.py:67

commit v3 on v2

--- a/solution.py
+++ b/solution.py
@@ -30,7 +30,7 @@
 BF16 = jnp.bfloat16
 
 
-def call(body, name, inputs, scalars, outs, flops=0, scratch=()):
+def call(body, name, inputs, scalars, outs, flops=0, scratch=(), room=40):
     moved = sum(math.prod(a.shape) * a.dtype.itemsize for a in list(inputs) + list(outs))
     return pl.pallas_call(
         body,
@@ -39,7 +39,7 @@
         in_specs=[SMEM] * len(scalars) + [VMEM] * len(inputs),
         out_specs=[VMEM] * len(outs),
         scratch_shapes=list(scratch),
-        compiler_params=pltpu.CompilerParams(vmem_limit_bytes=40 * 2**20),
+        compiler_params=pltpu.CompilerParams(vmem_limit_bytes=room * 2**20),
         cost_estimate=pl.CostEstimate(flops=flops, bytes_accessed=moved, transcendentals=0),
     )(*scalars, *inputs)
 
@@ -67,17 +67,14 @@
     return lax.ppermute(block, "group", [(0, 1), (1, 0), (2, 3), (3, 2)])
 
 
-def shift(block, step):
+def paired(block, step):
     n_mp = lax.axis_size("mp")
-    return lax.ppermute(block, "mp", [(i, (i + step) % n_mp) for i in range(n_mp)])
-
-
-def spread(block):
-    return [block] + [shift(block, k) for k in range(1, lax.axis_size("mp"))]
-
-
-def to_owner(blocks):
-    return [blocks[0]] + [shift(blocks[k], -k) for k in range(1, len(blocks))]
+    pairs = []
+    for group in range(lax.axis_size("group")):
+        sign = 1 - 2 * (group % 2)
+        for z in range(n_mp):
+            pairs.append((group * n_mp + z, group * n_mp + (z + sign * step) % n_mp))
+    return lax.ppermute(block, ("group", "mp"), pairs)
 
 
 def on_core(place, run, mine, other):
@@ -94,8 +91,12 @@
     return jnp.max(by_row, axis=0, keepdims=True)
 
 
-def ring_place(place, k, piece, n_mp):
-    return pl.multiple_of(lax.rem(place[2] + n_mp - k, n_mp) * piece, piece)
+def above(place, core, step, n_mp):
+    return lax.rem(place[2] + n_mp + (1 - 2 * core) * step, n_mp)
+
+
+def row_at(index, size):
+    return pl.multiple_of(index * size, size)
 
 
 def lay_kernel(*refs):
@@ -114,45 +115,111 @@
 def prepare_kernel(place, scales, latent, noise, embed, normed, stream, scaled, *, piece):
     rows = latent[place[1]].astype(F32)
     normed[...] = normalize(rows + embed[...])
-    at = pl.multiple_of(place[0] * (rows.shape[0] // 2) + place[2] * piece, piece)
-    stream[...] = latent[place[1], pl.ds(at, piece), :].astype(F32)
-    scaled[...] = scales[1] * noise[place[1], pl.ds(at, piece), :].astype(F32)
-
-
-def gen_kernel(place, normed, mine, other, *refs, piece):
-    preact_ref, active_ref, parts, whole = refs[0], refs[1], refs[2:-1], refs[-1]
+    half = rows.shape[0] // 2
+    for core in range(2):
+        at = pl.multiple_of(core * half + place[2] * piece, piece)
+        to = slice(core * piece, (core + 1) * piece)
+        stream[to, :] = latent[place[1], pl.ds(at, piece), :].astype(F32)
+        scaled[to, :] = scales[1] * noise[place[1], pl.ds(at, piece), :].astype(F32)
+
+
+def gen_kernel(place, normed, mine, other, preact_ref, active_ref, kept, across, own, away, whole):
     rows = whole.shape[0]
-    own = normed[pl.ds(pl.multiple_of(place[0] * rows, rows), rows), :]
+    piece = own.shape[0]
+    n_mp = rows // piece
+    core = place[0]
+    rows_of = normed[pl.ds(row_at(core, rows), rows), :]
 
     def run(w_in, w_out):
-        preact, active, partial = forward_part(own, w_in[...], w_out[...])
+        preact, active, partial = forward_part(rows_of, w_in[...], w_out[...])
         preact_ref[...] = preact
         active_ref[...] = active
         whole[...] = partial
 
     on_core(place, run, mine, other)
-    for k, part in enumerate(parts):
-        part[...] = whole[pl.ds(ring_place(place, k, piece, len(parts)), piece), :]
-
-
-def order_kernel(place, *refs):
+    own[...] = whole[pl.ds(row_at(place[2], piece), piece), :]
+    across[...] = whole[pl.ds(row_at(above(place, core, n_mp // 2, n_mp), piece), piece), :]
+    for k in range(1, n_mp // 2):
+        to = slice((k - 1) * piece, k * piece)
+        kept[to, :] = whole[pl.ds(row_at(above(place, core, k, n_mp), piece), piece), :]
+        away[to, :] = whole[pl.ds(row_at(above(place, 1 - core, k, n_mp), piece), piece), :]
+
+
+def join_kernel(kept, came, *outs):
+    piece = outs[0].shape[0] // 2
+    for k, out in enumerate(outs):
+        out[:piece, :] = kept[k * piece : (k + 1) * piece, :]
+        out[piece:, :] = came[k * piece : (k + 1) * piece, :]
+
+
+def sums_kernel(own, across, *refs):
     blocks, out = refs[:-1], refs[-1]
-    piece = blocks[0].shape[0]
-    for k, block in enumerate(blocks):
-        out[pl.ds(ring_place(place, k, piece, len(blocks)), piece), :] = block[...]
-
-
-def score_kernel(place, own, came, embed, weights, normed, preact_ref, active_ref, out, both):
-    half, width = own.shape
+    piece = own.shape[0]
+    near = own[...].astype(F32) + across[...].astype(F32)
+    far = 0.0
+    for block in blocks:
+        near = near + block[:piece, :].astype(F32)
+        far = far + block[piece:, :].astype(F32)
+    out[:piece, :] = near
+    out[piece:, :] = far
+
+
+def latent_kernel(place, scales, sums, came, stream, scaled, latents, noised, mine):
+    piece = mine.shape[0]
+    totals = (sums[:piece, :] + came[piece:, :], came[:piece, :] + sums[piece:, :])
+
+    def run(ordered):
+        for core, total in enumerate(ordered):
+            at = slice(core * piece, (core + 1) * piece)
+            latents[at, :] = stream[at, :] + total
+            noised[at, :] = (scales[0] * latents[at, :] + scaled[at, :]).astype(BF16)
+
+    pl.when(place[0] == 0)(lambda: run(totals))
+    pl.when(place[0] != 0)(lambda: run(totals[::-1]))
+    mine[...] = noised[pl.ds(row_at(place[0], piece), piece), :]
+
+
+def order_kernel(*refs):
+    blocks, out = refs[:-1], refs[-1]
+    at = 0
+    for block in blocks:
+        out[at : at + block.shape[0], :] = block[...]
+        at += block.shape[0]
+
+
+def rows_in_order(place, own, came, pair, store):
+    piece = pair.shape[0] // 2
+    n_mp = (own.shape[0] // piece + 1) // 2 * 2
+    half = n_mp * piece
+
+    def at(core, z):
+        return pl.multiple_of(core * half + z * piece, piece)
+
+    for core in range(2):
+        store(at(core, place[2]), pair[core * piece : (core + 1) * piece, :])
+    for source, sender in ((own, place[0]), (came, 1 - place[0])):
+        for k in range(1, n_mp // 2):
+            z = above(place, sender, -k, n_mp)
+            for core in range(2):
+                to = ((k - 1) * 2 + core) * piece
+                store(at(core, z), source[to : to + piece, :])
+        to = (n_mp - 2) * piece
+        store(at(sender, above(place, sender, n_mp // 2, n_mp)), source[to : to + piece, :])
+
+
+def score_kernel(place, pair, own, came, embed, weights, out, both):
+    n_mp, piece = out.shape[0], out.shape[1] // 2
+    width = embed.shape[1]
+    half = n_mp * piece
     rows = 2 * half
-    n_mp, piece = out.shape[0], out.shape[1] // 2
     hidden = weights.shape[1] // 2
-    for source, core in ((own, place[0]), (came, 1 - place[0])):
-        at = pl.multiple_of(core * half, half)
-        summed = source[...].astype(F32)
-        both[pl.ds(at, half), :] = normalize(summed + embed[...])
-        both[pl.ds(pl.multiple_of(rows + at, half), half), :] = normalize(summed)
-    normed[...] = both[:rows, :]
+
+    def store(at, value):
+        summed = value.astype(F32)
+        both[pl.ds(at, piece), :] = normalize(summed + embed[...])
+        both[pl.ds(pl.multiple_of(rows + at, piece), piece), :] = normalize(summed)
+
+    rows_in_order(place, own, came, pair, store)
 
     def finish(value):
         power = power_of(top_of(value))
@@ -166,18 +233,25 @@
 
     @pl.when(place[0] == 0)
     def _():
-        preact, active, fake = forward_part(both[:rows, :], weights[:, :hidden], weights[:, hidden:])
-        preact_ref[...] = preact
-        active_ref[...] = active
+        fake = forward_part(both[:rows, :], weights[:, :hidden], weights[:, hidden:])[2]
         finish(fake.astype(F32))
 
     @pl.when(place[0] != 0)
     def _():
-        preact, active, real = forward_part(both[...], weights[:, :hidden], weights[:, hidden:])
-        preact_ref[...] = preact[:rows]
-        active_ref[...] = active[:rows]
+        real = forward_part(both[...], weights[:, :hidden], weights[:, hidden:])[2]
         uncond, cond = real[rows:].astype(F32), real[:rows].astype(F32)
         finish(uncond + GUIDANCE * (cond - uncond))
+
+
+def refresh_kernel(place, pair, own, came, embed, weights, normed, preact, active):
+    def store(at, value):
+        rows = value.shape[0]
+        normed[pl.ds(at, rows), :] = normalize(value.astype(F32) + embed[...])
+
+    rows_in_order(place, own, came, pair, store)
+    hidden = preact.shape[1]
+    preact[...] = jnp.dot(normed[...], weights[:, :hidden], preferred_element_type=F32)
+    active[...] = jax.nn.gelu(preact[...]).astype(BF16)
 
 
 def total_kernel(blocks, out):
@@ -188,14 +262,14 @@
     out[...] = total
 
 
-def pack_kernel(place, own, other, near, far, out, *, loss_scale):
+def pack_kernel(place, own, other, latents_ref, noised, out, *, loss_scale):
     width = own.shape[1]
-    piece = near.shape[1]
+    piece = own.shape[0] // 2
     first = place[0] == 0
 
-    def run(fake_sum, real_sum, low, high):
-        latents = jnp.concatenate([low[0], high[0]], axis=0)
-        base = jnp.concatenate([low[1], high[1]], axis=0)
+    def run(fake_sum, real_sum):
+        latents = latents_ref[...]
+        base = noised[...].astype(F32)
         fake = base + fake_sum[...]
         real_mix = base + real_sum[...]
         away = jnp.sum(jnp.abs(latents - real_mix), axis=1, keepdims=True)
@@ -212,8 +286,8 @@
         tail = jnp.where(line == 9, coarse, tail)
         out[:, width:] = jnp.where(line == 10, scaled - coarse, tail)
 
-    pl.when(first)(lambda: run(own, other, near, far))
-    pl.when(place[0] != 0)(lambda: run(other, own, far, near))
+    pl.when(first)(lambda: run(own, other))
+    pl.when(place[0] != 0)(lambda: run(other, own))
 
 
 def grad_kernel(
@@ -341,8 +415,7 @@
     embedding = lax.dynamic_index_in_dim(class_table, own_class, keepdims=True).astype(F32)
     own_step = lax.dynamic_index_in_dim(timesteps, y_lo, keepdims=False)
     phase_angle = 0.5 * jnp.pi / TSTEPS * own_step.astype(F32)
-    signal_scale = jnp.cos(phase_angle)
-    scales = jnp.stack([signal_scale, jnp.sin(phase_angle)])
+    scales = jnp.stack([jnp.cos(phase_angle), jnp.sin(phase_angle)])
     prepared = call(
         lambda *refs: prepare_kernel(*refs, piece=piece),
         "prepare",
@@ -350,72 +423,94 @@
         [place, scales],
         [
             shape((positions, width), BF16),
-            shape((piece, width), F32),
-            shape((piece, width), F32),
+            shape((2 * piece, width), F32),
+            shape((2 * piece, width), F32),
         ],
     )
 
-    gen_mine, score_blocks, prepared, embedding, signal_scale = lax.optimization_barrier(
+    gen_mine, score_blocks, prepared, embedding, scales = lax.optimization_barrier(
         (
             gather(outgoing([gen_weights])),
             outgoing([fake_weights, real_weights]),
             prepared,
             embedding,
-            signal_scale,
+            scales,
         )
     )
     normed_gen, stream, scaled_noise = prepared
     score_weights = gather(score_blocks)
     gen_other = core_swap(gen_mine)
 
-    preact_gen, active_gen, *parts = call(
-        lambda *refs: gen_kernel(*refs, piece=piece),
+    steps = n_mp // 2 - 1
+    some = shape((steps * piece, width), BF16)
+    one = shape((piece, width), BF16)
+    two = shape((2 * piece, width), BF16)
+    preact_gen, active_gen, kept, across, own, away = call(
+        gen_kernel,
         "generate",
         [normed_gen, gen_mine, gen_other],
         [place],
-        [shape((rows, hidden), F32), shape((rows, hidden), BF16)]
-        + [shape((piece, width), BF16)] * n_mp,
+        [shape((rows, hidden), F32), shape((rows, hidden), BF16), some, one, one, some],
         2 * work,
         [pltpu.VMEM((rows, width), BF16)],
-    )
-    total = sum(block.astype(F32) for block in to_owner(parts))
-    latents = stream + total
-    noised = (signal_scale * latents + scaled_noise).astype(BF16)
-
-    (noised_own,) = call(
-        order_kernel, "order", spread(noised), [place], [shape((rows, width), BF16)]
-    )
-    score_weights, noised_own = lax.optimization_barrier((score_weights, noised_own))
-    near = jnp.stack([latents, noised.astype(F32)])
-    normed_cond, preact_fake, active_fake, score_parts = call(
+        room=60,
+    )
+    joined = call(join_kernel, "join", [kept, core_swap(away)], [], [two] * steps)
+    came = [paired(block, k + 1) for k, block in enumerate(joined)]
+    across = paired(across, n_mp // 2)
+    both_f32 = shape((2 * piece, width), F32)
+    (sums,) = call(sums_kernel, "sums", [own, across] + came, [], [both_f32])
+    latents, noised, noised_mine = call(
+        latent_kernel,
+        "latent",
+        [sums, core_swap(sums), stream, scaled_noise],
+        [place, scales],
+        [both_f32, two, one],
+    )
+    blocks = [paired(noised, k + 1) for k in range(steps)]
+    blocks.append(paired(noised_mine, n_mp // 2))
+    (around,) = call(
+        order_kernel, "order", blocks, [], [shape(((2 * steps + 1) * piece, width), BF16)]
+    )
+    score_weights, around = lax.optimization_barrier((score_weights, around))
+    around_other = core_swap(around)
+    (score_parts,) = call(
         score_kernel,
         "score",
-        [noised_own, core_swap(noised_own), embedding, score_weights],
+        [noised, around, around_other, embedding, score_weights],
+        [place],
+        [shape((n_mp, 2 * piece, width + LANES), F32)],
+        8 * work,
+        [pltpu.VMEM((2 * positions, width), BF16)],
+    )
+
+    def exchange(blocks):
+        return lax.all_to_all(blocks.astype(jnp.float16), "mp", 0, 0, tiled=True).astype(F32)
+
+    (total,) = call(
+        total_kernel, "total", [exchange(score_parts)], [], [shape((2 * piece, width), F32)]
+    )
+    (message,) = call(
+        lambda *refs: pack_kernel(*refs, loss_scale=loss_scale),
+        "pack",
+        [total, core_swap(total), latents, noised],
+        [place],
+        [shape((2 * piece, width + LANES), F32)],
+    )
+
+    message, around, around_other = lax.optimization_barrier((message, around, around_other))
+    normed_cond, preact_fake, active_fake = call(
+        refresh_kernel,
+        "refresh",
+        [noised, around, around_other, embedding, score_weights],
         [place],
         [
             shape((positions, width), BF16),
             shape((positions, hidden), F32),
             shape((positions, hidden), BF16),
-            shape((n_mp, 2 * piece, width + LANES), F32),
         ],
-        8 * work,
-        [pltpu.VMEM((2 * positions, width), BF16)],
-    )
-
-    def exchange(blocks):
-        return lax.all_to_all(blocks.astype(jnp.float16), "mp", 0, 0, tiled=True).astype(F32)
-
-    (total,) = call(
-        total_kernel, "total", [exchange(score_parts)], [], [shape((2 * piece, width), F32)]
-    )
-    (message,) = call(
-        lambda *refs: pack_kernel(*refs, loss_scale=loss_scale),
-        "pack",
-        [total, core_swap(total), near, core_swap(near)],
-        [place],
-        [shape((2 * piece, width + LANES), F32)],
-    )
-
+        2 * work,
+    )
     first = core == 0
 
     def chosen(fake_value, gen_value):

time: 209 us -> 209 us (level)
  blocking collectives: 44.7 us -> 72.9 us
  waiting for transfers between devices: 71.1 us -> 49.3 us
  starting transfers between devices: 56.4 us -> 43.1 us
  local copies, waits for them, and re-layouts: 7.18 us -> 11.1 us
  Pallas kernels: 17.1 us -> 19.6 us
    all_to_all x0 -> x1, blocking collectives: none -> 27.7 us  [exchange(): lax.all_to_all(blocks.astype(jnp.float16), 'mp', 0, 0, tiled=True)]
    all_to_all x2 -> x1, waiting for transfers between devices: 37.8 us -> 15 us  [exchange(): lax.all_to_all(blocks.astype(jnp.float16), 'mp', 0, 0, tiled=True)]
    ppermute x14 -> x8, starting transfers between devices: 28.1 us -> 19.8 us  [paired(): return lax.ppermute(block, ('group', 'mp'), pairs)]
    all_to_all x2 -> x1, starting transfers between devices: 10.6 us -> 4.21 us  [exchange(): lax.all_to_all(blocks.astype(jnp.float16), 'mp', 0, 0, tiled=True)]
    unnamed x32 -> x52, local copies, waits for them, and re-layouts: 5.08 us -> 9.01 us
    ppermute x7 -> x8, waiting for transfers between devices: 6.22 us -> 9.1 us  [core_swap(): return lax.ppermute(block, 'group', [(0, 1), (1, 0), (2, 3), (3, 2)])]
    pallas_call x11 -> x15, Pallas kernels: 17.1 us -> 19.6 us  [call(): pl.pallas_call(body, name=name, out_shape=outs, in_specs=[SMEM] * len(sca...]
    ppermute x7 -> x8, starting transfers between devices: 4.36 us -> 5.85 us  [core_swap(): return lax.ppermute(block, 'group', [(0, 1), (1, 0), (2, 3), (3, 2)])]
  transfers between devices with their start and end apart: 25 -> 19, of which waited for: 13 -> 10; matrix products, arithmetic and copies ran while one was open for 4% -> 4% of each run, Pallas kernels for 2% -> 4%
where the time goes in v3:
time: 209 us; the launch traced here: 208 us
  blocking collectives  72.9 us (35%)
  waiting for transfers between devices  49.3 us (24%)
  starting transfers between devices  43.1 us (21%)
  Pallas kernels  19.6 us (9%)
  local copies, waits for them, and re-layouts  11.1 us (5%)
  other arithmetic  8.7 us (4%)
  between operations  3.74 us (2%)
    all_to_all x1, blocking collectives, local(): lax.all_to_all(grads.astype(jnp.float16), PLANE, 0, 0, axis_index_groups=...  45.1 us
    all_to_all x1, blocking collectives, exchange(): lax.all_to_all(blocks.astype(jnp.float16), 'mp', 0, 0, tiled=True)  27.7 us
    ppermute x8, starting transfers between devices, paired(): return lax.ppermute(block, ('group', 'mp'), pairs)  19.8 us
    pallas_call x15, Pallas kernels, call(): pl.pallas_call(body, name=name, out_shape=outs, in_specs=[SMEM] * len(sca...  19.6 us
    all_to_all x1, waiting for transfers between devices, exchange(): lax.all_to_all(blocks.astype(jnp.float16), 'mp', 0, 0, tiled=True)  15 us
    all_to_all x2, waiting for transfers between devices, gather(): return lax.all_to_all(blocks, PLANE, 0, 0, tiled=True).reshape(width, -1)  14.7 us
    all_to_all x2, starting transfers between devices, gather(): return lax.all_to_all(blocks, PLANE, 0, 0, tiled=True).reshape(width, -1)  13.2 us
    ppermute x8, waiting for transfers between devices, paired(): return lax.ppermute(block, ('group', 'mp'), pairs)  10.5 us
  transfers between devices with their start and end apart: 19, of which 10 were waited for; matrix products, arithmetic and copies ran while one was open for 4% of the time, Pallas kernels for 4%

profile of v3, /device:TPU:1, one launch (start us, length us, event | category | flops | bytes accessed | tf_op | source)
XLA Modules:
  0.0 208.5 jit_solution(9172149455879171450)
XLA Ops:
  0.6 0.9 copy-done.16
  1.5 1.5 lay.2
  3.0 8.8 %all-to-all-start = ((bf16[32,40,640]{2,1,0:T(8,128)(2,1)}), bf16[32,40,640]{2,1,0:T(8,128)(2,1)}, u32[]{:S(2)}, u32[]{:S(2)}) async-start(bf16[32,40,640]{2,1,0:T(8,128)(2,1)} %lay.2), calls=%async_computation | async-start | bytes 3276800 | tf_op jit(solution)/shard_map/all_to_all | solution.py:412
  16.3 1.6 copy-done
  18.1 0.7 dynamic-slice_convert_fusion.refs_4_.embed
  18.9 0.8 prepare.1
  19.7 0.8 copy-done.2
  20.6 0.7 copy-done.11
  21.2 14.7 %all-to-all-done = bf16[32,40,640]{2,1,0:T(8,128)(2,1)} async-done(((bf16[32,40,640]{2,1,0:T(8,128)(2,1)}), bf16[32,40,640]{2,1,0:T(8,128)(2,1)}, u32[]{:S(2)}, u32[]{:S(2)}) %all-to-all-start) | async-done | bytes 1638432 | tf_op jit(solution)/shard_map/all_to_all | solution.py:412
  35.9 4.4 %all-to-all-start.1 = ((bf16[32,40,1280]{2,1,0:T(8,128)(2,1)}), bf16[32,40,1280]{2,1,0:T(8,128)(2,1)S(1)}, u32[]{:S(2)}, u32[]{:S(2)}) async-start(bf16[32,40,1280]{2,1,0:T(8,128)(2,1)} %copy-done), calls=%async_computation.1 | async-start | bytes 6553600 | tf_op jit(solution)/shard_map/all_to_all | solution.py:412
  40.7 3.6 %collective-permute-done.other = bf16[1280,640]{1,0:T(8,128)(2,1)} collective-permute-done((bf16[1280,640]{1,0:T(8,128)(2,1)}, bf16[1280,640]{1,0:T(8,128)(2,1)}, u32[]{:S(2)}, u32[]{:S(2)}) %collective-permute-start) | collective-permute-done | bytes 1638432 | tf_op jit(solution)/shard_map/ppermute | solution.py:67
  44.3 4.0 %generate.1 = (f32[128,640]{1,0:T(8,128)}, bf16[128,640]{1,0:T(8,128)(2,1)}, bf16[48,1280]{1,0:T(8,128)(2,1)}, bf16[16,1280]{1,0:T(8,128)(2,1)}, bf16[16,1280]{1,0:T(8,128)(2,1)}, /*index=5*/bf16[48,1280]{1,0:T(8,128)(2,1)}) custom-call(s32[3]{0:T(128)} %copy-done.19, bf16[256,1280]{1,0:T(8,128)(2,1)} %copy-done.2, bf16[1280,640]{1,0:T(8,128)(2,1)} %bitcast.3.mine, ...), custom_call_target="tpu_custom_call" | custom-call | flops 419430400 | bytes 4751360 | tf_op jit(solution)/shard_map/generate/pallas_call | solution.py:35
  48.6 1.3 collective-permute-done.2.came
  49.9 0.9 copy-done.15
  50.8 5.6 %collective-permute-start.3 = (bf16[32,1280]{1,0:T(8,128)(2,1)S(1)}, bf16[32,1280]{1,0:T(8,128)(2,1)S(1)}, u32[]{:S(2)}, u32[]{:S(2)}) collective-permute-start(bf16[32,1280]{1,0:T(8,128)(2,1)S(1)} %get-tuple-element.46), channel_id=1, source_target_pairs={{0,1},{1,2},{2,3},{3,4},{4,5},{5,6},{6,7},{7,0},{64,71},{65,64},{6... | collective-permute-start | bytes 245768 | tf_op jit(solution)/shard_map/ppermute | solution.py:77
  56.5 1.2 collective-permute-start.4
  58.1 4.5 %collective-permute-start.1 = (bf16[16,1280]{1,0:T(8,128)(2,1)}, bf16[16,1280]{1,0:T(8,128)(2,1)S(1)}, u32[]{:S(2)}, u32[]{:S(2)}) collective-permute-start(bf16[16,1280]{1,0:T(8,128)(2,1)} %get-tuple-element.43), channel_id=1, source_target_pairs={{0,4},{1,5},{2,6},{3,7},{4,0},{5,1},{6,2},{7,3},{64,68},{65,69},{6... | collective-permute-start | bytes 122888 | tf_op jit(solution)/shard_map/ppermute | solution.py:77
  62.6 3.8 %collective-permute-done.1.across = bf16[16,1280]{1,0:T(8,128)(2,1)S(1)} collective-permute-done((bf16[16,1280]{1,0:T(8,128)(2,1)}, bf16[16,1280]{1,0:T(8,128)(2,1)S(1)}, u32[]{:S(2)}, u32[]{:S(2)}) %collective-permute-start.1) | collective-permute-done | bytes 40992 | tf_op jit(solution)/shard_map/ppermute | solution.py:77
  66.4 0.8 copy-done.21
  67.2 2.2 %collective-permute-start.6 = (f32[32,1280]{1,0:T(8,128)S(1)}, f32[32,1280]{1,0:T(8,128)S(1)}, u32[]{:S(2)}, u32[]{:S(2)}) collective-permute-start(f32[32,1280]{1,0:T(8,128)S(1)} %sums.1), channel_id=1, source_target_pairs={{0,64},{64,0},{128,192},{192,128},{1,65},{65,1},{129,193},{193,129... | collective-permute-start | bytes 491528 | tf_op jit(solution)/shard_map/ppermute | solution.py:67
  69.4 1.0 collective-permute-done.6.came
  71.1 0.7 copy-done.13
  71.7 1.9 collective-permute-start.9
  73.7 1.1 collective-permute-start.8
  74.8 2.0 collective-permute-start.7
  76.9 2.9 %collective-permute-start.10 = (bf16[16,1280]{1,0:T(8,128)(2,1)S(1)}, bf16[16,1280]{1,0:T(8,128)(2,1)S(1)}, u32[]{:S(2)}, u32[]{:S(2)}) collective-permute-start(bf16[16,1280]{1,0:T(8,128)(2,1)S(1)} %get-tuple-element.53), channel_id=1, source_target_pairs={{0,4},{1,5},{2,6},{3,7},{4,0},{5,1},{6,2},{7,3},{64,68},{65,69},{6... | collective-permute-start | bytes 122888 | tf_op jit(solution)/shard_map/ppermute | solution.py:77
  79.8 6.7 %collective-permute-done.10.refs_3_ = bf16[16,1280]{1,0:T(8,128)(2,1)S(1)} collective-permute-done((bf16[16,1280]{1,0:T(8,128)(2,1)S(1)}, bf16[16,1280]{1,0:T(8,128)(2,1)S(1)}, u32[]{:S(2)}, u32[]{:S(2)}) %collective-permute-start.10) | collective-permute-done | bytes 40992 | tf_op jit(solution)/shard_map/ppermute | solution.py:77
  86.5 0.7 copy-done.6
  87.6 1.4 collective-permute-done.11.came
  89.0 1.0 copy-done.7
  90.0 3.5 %score.1 = f32[8,32,1408]{2,1,0:T(8,128)S(1)} custom-call(s32[3]{0:T(128)S(1)} %copy-done.20, bf16[32,1280]{1,0:T(8,128)(2,1)S(1)} %get-tuple-element.51.pair.refs_4_, bf16[112,1280]{1,0:T(8,128)(2,1)S(1)} %copy-done.7, bf16[112,1280]{1,0:T(8,128)(2,1)S(1)} %collective-permute-done.11.came, f32[1,1280]{1,0:T(1,128)S(1)} %dynamic-slice_convert_fusion.refs_4_.embed, ...), custom_call_target="tpu_custom_call" | custom-call | flops 1677721600 | bytes 5379072 | tf_op jit(solution)/shard_map/score/pallas_call | solution.py:35
  93.7 27.7 %all_to_all.25 = f16[8,32,1408]{2,1,0:T(8,128)(2,1)S(1)} all-to-all(f16[8,32,1408]{2,1,0:T(8,128)(2,1)S(1)} %convert_element_type.28), channel_id=1, replica_groups=mesh['group'=4,'dp'=8,'mp'=8] {'mp'}, dimensions={0} | all-to-all | bytes 1441792 | tf_op jit(solution)/shard_map/all_to_all | solution.py:488
  123.3 0.9 copy-done.14
  124.3 1.1 pack.1
  125.4 0.9 broadcast_in_dim.2
  126.3 4.2 %all-to-all-start.3 = ((f16[8,32,1408]{2,1,0:T(8,128)(2,1)}), f16[8,32,1408]{2,1,0:T(8,128)(2,1)}, u32[]{:S(2)}, u32[]{:S(2)}) async-start(f16[8,32,1408]{2,1,0:T(8,128)(2,1)} %broadcast_in_dim.2), calls=%async_computation.3 | async-start | bytes 1441792 | tf_op jit(solution)/shard_map/all_to_all | solution.py:488
  130.6 3.0 %slice_select_fusion.refs_2_ = bf16[1280,640]{1,0:T(8,128)(2,1)} fusion(bf16[1280,640]{1,0:T(8,128)(2,1)} %bitcast.3.mine, bf16[1280,1280]{1,0:T(8,128)(2,1)S(1)} %bitcast.7, pred[]{:T(512)S(6)} %eq.5), kind=kLoop, calls=%fused_computation | loop fusion | flops 819200 | bytes 4915201 | tf_op jit(solution)/shard_map/jit(_where)/select_n | solution.py:530
  133.6 1.5 refresh.1
  135.1 1.1 maximum_select_fusion.1.refs_5_
  136.2 1.4 fusion.5.refs_3_
  137.7 15.0 %all-to-all-done.3 = f16[8,32,1408]{2,1,0:T(8,128)(2,1)} async-done(((f16[8,32,1408]{2,1,0:T(8,128)(2,1)}), f16[8,32,1408]{2,1,0:T(8,128)(2,1)}, u32[]{:S(2)}, u32[]{:S(2)}) %all-to-all-start.3) | async-done | bytes 720928 | tf_op jit(solution)/shard_map/all_to_all | solution.py:488
  152.7 1.2 convert_element_type.31.refs_1_
  154.0 3.0 %grads.1 = f32[16,816,128]{2,1,0:T(8,128)S(1)} custom-call(s32[3]{0:T(128)S(1)} %copy-done.20, f32[8,32,1408]{2,1,0:T(8,128)S(1)} %convert_element_type.31.refs_1_, bf16[1280,640]{1,0:T(8,128)(2,1)S(1)} %copy-done.1, f32[256,640]{1,0:T(8,128)S(1)} %fusion.5.refs_3_, bf16[256,1280]{1,0:T(8,128)(2,1)S(1)} %broadcast_select_fusion.refs_4_, ...), custom_call_target="tpu_custom_call" | custom-call | flops 1258291200 | bytes 11403264 | tf_op jit(solution)/shard_map/grads/pallas_call | solution.py:35
  157.4 45.1 %all_to_all.26 = f16[16,816,128]{2,1,0:T(8,128)(2,1)S(1)} all-to-all(f16[16,816,128]{2,1,0:T(8,128)(2,1)S(1)} %convert_element_type.32), channel_id=1, replica_groups={{0,16,32,48,176,160,144,24,40,56,184,168,152,136,8,128},{64,80,96,112,2..., dimensions={0} | all-to-all | bytes 6684672 | tf_op jit(solution)/shard_map/all_to_all | solution.py:540
  203.0 1.2 collect.1
  204.2 1.7 collective-permute-start.15
  205.9 1.1 collective-permute-done.15.came
  206.9 1.5 place.1
  (75 shorter events, 7.1 us)
Async XLA Ops:
  0.6 0.9 copy-start.16
  3.0 8.8 %copy-start.24 = (s32[2]{0:T(128)S(1)}, s32[2]{0:T(128)}, u32[]{:S(2)}) copy-start(s32[2]{0:T(128)} %param.10) | copy-start | bytes 28
  3.0 10.2 %copy-start.25 = (s32[2]{0:T(128)S(1)}, s32[2]{0:T(128)}, u32[]{:S(2)}) copy-start(s32[2]{0:T(128)} %param.11) | copy-start | bytes 28
  3.0 12.8 %copy-start.17 = (bf16[40,2,640]{2,1,0:T(2,128)(2,1)S(1)}, bf16[40,2,640]{2,1,0:T(2,128)(2,1)}, u32[]{:S(2)}) copy-start(bf16[40,2,640]{2,1,0:T(2,128)(2,1)} %refs_0_.3) | copy-start | bytes 307204
  3.0 12.8 %copy-start.18 = (bf16[40,2,640]{2,1,0:T(2,128)(2,1)S(1)}, bf16[40,2,640]{2,1,0:T(2,128)(2,1)}, u32[]{:S(2)}) copy-start(bf16[40,2,640]{2,1,0:T(2,128)(2,1)} %refs_1_.1) | copy-start | bytes 307204
  3.0 32.9 %all-to-all-start = ((bf16[32,40,640]{2,1,0:T(8,128)(2,1)}), bf16[32,40,640]{2,1,0:T(8,128)(2,1)}, u32[]{:S(2)}, u32[]{:S(2)}) async-start(bf16[32,40,640]{2,1,0:T(8,128)(2,1)} %lay.2), calls=%async_computation | async-start | bytes 3276800 | tf_op jit(solution)/shard_map/all_to_all | solution.py:412
  15.8 3.1 %copy-start.4 = (bf16[2,256,1280]{2,1,0:T(8,128)(2,1)S(1)}, bf16[2,256,1280]{2,1,0:T(8,128)(2,1)}, u32[]{:S(2)}) copy-start(bf16[2,256,1280]{2,1,0:T(8,128)(2,1)} %refs_2_.1) | copy-start | bytes 3932164
  15.8 3.1 %copy-start.5 = (bf16[2,256,1280]{2,1,0:T(8,128)(2,1)S(1)}, bf16[2,256,1280]{2,1,0:T(8,128)(2,1)}, u32[]{:S(2)}) copy-start(bf16[2,256,1280]{2,1,0:T(8,128)(2,1)} %refs_3_.1) | copy-start | bytes 3932164
  16.3 1.7 copy-start
  18.1 17.8 %copy-start.19 = (s32[3]{0:T(128)}, s32[3]{0:T(128)S(1)}, u32[]{:S(2)}) copy-start(s32[3]{0:T(128)S(1)} %pad_add_fusion.refs_0_.place) | copy-start | bytes 40
  19.7 0.8 copy-start.2
  20.6 0.7 copy-start.11
  35.9 51.2 %all-to-all-start.1 = ((bf16[32,40,1280]{2,1,0:T(8,128)(2,1)}), bf16[32,40,1280]{2,1,0:T(8,128)(2,1)S(1)}, u32[]{:S(2)}, u32[]{:S(2)}) async-start(bf16[32,40,1280]{2,1,0:T(8,128)(2,1)} %copy-done), calls=%async_computation.1 | async-start | bytes 6553600 | tf_op jit(solution)/shard_map/all_to_all | solution.py:412
  40.4 30.1 %copy-start.12 = (f32[32,1280]{1,0:T(8,128)S(1)}, f32[32,1280]{1,0:T(8,128)}, u32[]{:S(2)}) copy-start(f32[32,1280]{1,0:T(8,128)} %copy-done.11) | copy-start | bytes 491524
  40.4 30.1 %copy-start.20 = (s32[3]{0:T(128)S(1)}, s32[3]{0:T(128)}, u32[]{:S(2)}) copy-start(s32[3]{0:T(128)} %copy-done.19) | copy-start | bytes 40
  40.4 3.9 %collective-permute-start = (bf16[1280,640]{1,0:T(8,128)(2,1)}, bf16[1280,640]{1,0:T(8,128)(2,1)}, u32[]{:S(2)}, u32[]{:S(2)}) collective-permute-start(bf16[1280,640]{1,0:T(8,128)(2,1)} %bitcast.3.mine), channel_id=1, source_target_pairs={{0,64},{64,0},{128,192},{192,128},{1,65},{65,1},{129,193},{193,129... | collective-permute-start | bytes 4915208 | tf_op jit(solution)/shard_map/ppermute | solution.py:67
  48.4 1.5 collective-permute-start.2
  49.9 0.9 copy-start.15
  50.8 15.6 %collective-permute-start.3 = (bf16[32,1280]{1,0:T(8,128)(2,1)S(1)}, bf16[32,1280]{1,0:T(8,128)(2,1)S(1)}, u32[]{:S(2)}, u32[]{:S(2)}) collective-permute-start(bf16[32,1280]{1,0:T(8,128)(2,1)S(1)} %get-tuple-element.46), channel_id=1, source_target_pairs={{0,1},{1,2},{2,3},{3,4},{4,5},{5,6},{6,7},{7,0},{64,71},{65,64},{6... | collective-permute-start | bytes 245768 | tf_op jit(solution)/shard_map/ppermute | solution.py:77
  56.5 9.9 %collective-permute-start.4 = (bf16[32,1280]{1,0:T(8,128)(2,1)S(1)}, bf16[32,1280]{1,0:T(8,128)(2,1)S(1)}, u32[]{:S(2)}, u32[]{:S(2)}) collective-permute-start(bf16[32,1280]{1,0:T(8,128)(2,1)S(1)} %get-tuple-element.47), channel_id=1, source_target_pairs={{0,2},{1,3},{2,4},{3,5},{4,6},{5,7},{6,0},{7,1},{64,70},{65,71},{6... | collective-permute-start | bytes 245768 | tf_op jit(solution)/shard_map/ppermute | solution.py:77
  57.7 8.8 %collective-permute-start.5 = (bf16[32,1280]{1,0:T(8,128)(2,1)S(1)}, bf16[32,1280]{1,0:T(8,128)(2,1)S(1)}, u32[]{:S(2)}, u32[]{:S(2)}) collective-permute-start(bf16[32,1280]{1,0:T(8,128)(2,1)S(1)} %get-tuple-element.48), channel_id=1, source_target_pairs={{0,3},{1,4},{2,5},{3,6},{4,7},{5,0},{6,1},{7,2},{64,69},{65,70},{6... | collective-permute-start | bytes 245768 | tf_op jit(solution)/shard_map/ppermute | solution.py:77
  58.1 8.3 %collective-permute-start.1 = (bf16[16,1280]{1,0:T(8,128)(2,1)}, bf16[16,1280]{1,0:T(8,128)(2,1)S(1)}, u32[]{:S(2)}, u32[]{:S(2)}) collective-permute-start(bf16[16,1280]{1,0:T(8,128)(2,1)} %get-tuple-element.43), channel_id=1, source_target_pairs={{0,4},{1,5},{2,6},{3,7},{4,0},{5,1},{6,2},{7,3},{64,68},{65,69},{6... | collective-permute-start | bytes 122888 | tf_op jit(solution)/shard_map/ppermute | solution.py:77
  66.4 0.8 copy-start.21
  67.2 3.2 %collective-permute-start.6 = (f32[32,1280]{1,0:T(8,128)S(1)}, f32[32,1280]{1,0:T(8,128)S(1)}, u32[]{:S(2)}, u32[]{:S(2)}) collective-permute-start(f32[32,1280]{1,0:T(8,128)S(1)} %sums.1), channel_id=1, source_target_pairs={{0,64},{64,0},{128,192},{192,128},{1,65},{65,1},{129,193},{193,129... | collective-permute-start | bytes 491528 | tf_op jit(solution)/shard_map/ppermute | solution.py:67
  71.1 0.7 copy-start.13
  71.7 14.7 %collective-permute-start.9 = (bf16[32,1280]{1,0:T(8,128)(2,1)S(1)}, bf16[32,1280]{1,0:T(8,128)(2,1)S(1)}, u32[]{:S(2)}, u32[]{:S(2)}) collective-permute-start(bf16[32,1280]{1,0:T(8,128)(2,1)S(1)} %get-tuple-element.51.pair.refs_4_), channel_id=1, source_target_pairs={{0,3},{1,4},{2,5},{3,6},{4,7},{5,0},{6,1},{7,2},{64,69},{65,70},{6... | collective-permute-start | bytes 245768 | tf_op jit(solution)/shard_map/ppermute | solution.py:77
  73.7 12.8 %collective-permute-start.8 = (bf16[32,1280]{1,0:T(8,128)(2,1)S(1)}, bf16[32,1280]{1,0:T(8,128)(2,1)S(1)}, u32[]{:S(2)}, u32[]{:S(2)}) collective-permute-start(bf16[32,1280]{1,0:T(8,128)(2,1)S(1)} %get-tuple-element.51.pair.refs_4_), channel_id=1, source_target_pairs={{0,2},{1,3},{2,4},{3,5},{4,6},{5,7},{6,0},{7,1},{64,70},{65,71},{6... | collective-permute-start | bytes 245768 | tf_op jit(solution)/shard_map/ppermute | solution.py:77
  74.8 11.6 %collective-permute-start.7 = (bf16[32,1280]{1,0:T(8,128)(2,1)S(1)}, bf16[32,1280]{1,0:T(8,128)(2,1)S(1)}, u32[]{:S(2)}, u32[]{:S(2)}) collective-permute-start(bf16[32,1280]{1,0:T(8,128)(2,1)S(1)} %get-tuple-element.51.pair.refs_4_), channel_id=1, source_target_pairs={{0,1},{1,2},{2,3},{3,4},{4,5},{5,6},{6,7},{7,0},{64,71},{65,64},{6... | collective-permute-start | bytes 245768 | tf_op jit(solution)/shard_map/ppermute | solution.py:77
  76.9 9.6 %collective-permute-start.10 = (bf16[16,1280]{1,0:T(8,128)(2,1)S(1)}, bf16[16,1280]{1,0:T(8,128)(2,1)S(1)}, u32[]{:S(2)}, u32[]{:S(2)}) collective-permute-start(bf16[16,1280]{1,0:T(8,128)(2,1)S(1)} %get-tuple-element.53), channel_id=1, source_target_pairs={{0,4},{1,5},{2,6},{3,7},{4,0},{5,1},{6,2},{7,3},{64,68},{65,69},{6... | collective-permute-start | bytes 122888 | tf_op jit(solution)/shard_map/ppermute | solution.py:77
  86.5 0.7 copy-start.6
  87.2 1.9 collective-permute-start.11
  89.0 1.0 copy-start.7
  90.0 3.6 %copy-start.9 = (bf16[112,1280]{1,0:T(8,128)(2,1)}, bf16[112,1280]{1,0:T(8,128)(2,1)S(1)}, u32[]{:S(2)}) copy-start(bf16[112,1280]{1,0:T(8,128)(2,1)S(1)} %collective-permute-done.11.came) | copy-start | bytes 860164
  121.7 1.6 collective-permute-start.12
  122.2 12.9 %collective-permute-start.14 = (bf16[128,640]{1,0:T(8,128)(2,1)}, bf16[128,640]{1,0:T(8,128)(2,1)}, u32[]{:S(2)}, u32[]{:S(2)}) collective-permute-start(bf16[128,640]{1,0:T(8,128)(2,1)} %get-tuple-element.65), channel_id=1, source_target_pairs={{0,64},{64,0},{128,192},{192,128},{1,65},{65,1},{129,193},{193,129... | collective-permute-start | bytes 491528 | tf_op jit(solution)/shard_map/ppermute | solution.py:67
  122.3 13.9 %collective-permute-start.13 = (f32[128,640]{1,0:T(8,128)}, f32[128,640]{1,0:T(8,128)}, u32[]{:S(2)}, u32[]{:S(2)}) collective-permute-start(f32[128,640]{1,0:T(8,128)} %get-tuple-element.62), channel_id=1, source_target_pairs={{0,64},{64,0},{128,192},{192,128},{1,65},{65,1},{129,193},{193,129... | collective-permute-start | bytes 983048 | tf_op jit(solution)/shard_map/ppermute | solution.py:67
  123.3 0.9 copy-start.14
  126.3 26.4 %all-to-all-start.3 = ((f16[8,32,1408]{2,1,0:T(8,128)(2,1)}), f16[8,32,1408]{2,1,0:T(8,128)(2,1)}, u32[]{:S(2)}, u32[]{:S(2)}) async-start(f16[8,32,1408]{2,1,0:T(8,128)(2,1)} %broadcast_in_dim.2), calls=%async_computation.3 | async-start | bytes 1441792 | tf_op jit(solution)/shard_map/all_to_all | solution.py:488
  130.5 3.0 %copy-start.8 = (bf16[112,1280]{1,0:T(8,128)(2,1)S(1)}, bf16[112,1280]{1,0:T(8,128)(2,1)}, u32[]{:S(2)}) copy-start(bf16[112,1280]{1,0:T(8,128)(2,1)} %copy-done.6) | copy-start | bytes 860164
  130.6 3.0 %copy-start.10 = (bf16[112,1280]{1,0:T(8,128)(2,1)S(1)}, bf16[112,1280]{1,0:T(8,128)(2,1)}, u32[]{:S(2)}) copy-start(bf16[112,1280]{1,0:T(8,128)(2,1)} %copy-done.9) | copy-start | bytes 860164
  133.6 1.6 copy-start.23
  133.6 2.6 %copy-start.22 = (f32[128,640]{1,0:T(8,128)S(1)}, f32[128,640]{1,0:T(8,128)}, u32[]{:S(2)}) copy-start(f32[128,640]{1,0:T(8,128)} %get-tuple-element.62) | copy-start | bytes 983044
  135.1 2.5 %copy-start.3 = (bf16[256,1280]{1,0:T(8,128)(2,1)S(1)}, bf16[256,1280]{1,0:T(8,128)(2,1)}, u32[]{:S(2)}) copy-start(bf16[256,1280]{1,0:T(8,128)(2,1)} %copy-done.2) | copy-start | bytes 1966084
  137.6 16.3 %copy-start.1 = (bf16[1280,640]{1,0:T(8,128)(2,1)S(1)}, bf16[1280,640]{1,0:T(8,128)(2,1)}, u32[]{:S(2)}) copy-start(bf16[1280,640]{1,0:T(8,128)(2,1)} %slice_select_fusion.refs_2_) | copy-start | bytes 4915204
  204.2 2.8 %collective-permute-start.15 = (f32[400,128]{1,0:T(8,128)S(1)}, f32[400,128]{1,0:T(8,128)S(1)}, u32[]{:S(2)}, u32[]{:S(2)}) collective-permute-start(f32[400,128]{1,0:T(8,128)S(1)} %get-tuple-element.67), channel_id=1, source_target_pairs={{0,64},{64,0},{128,192},{192,128},{1,65},{65,1},{129,193},{193,129... | collective-permute-start | bytes 614408 | tf_op jit(solution)/shard_map/ppermute | solution.py:67

commit v4 on v3

--- a/solution.py
+++ b/solution.py
@@ -123,73 +123,57 @@
         scaled[to, :] = scales[1] * noise[place[1], pl.ds(at, piece), :].astype(F32)
 
 
-def gen_kernel(place, normed, mine, other, preact_ref, active_ref, kept, across, own, away, whole):
-    rows = whole.shape[0]
+def gen_rows(place, core, piece, n_mp):
+    half = n_mp * piece
+    for k in range(1, n_mp // 2):
+        for owner in range(2):
+            yield pl.multiple_of(owner * half + above(place, core, k, n_mp) * piece, piece)
+    for k in (0, n_mp // 2):
+        yield pl.multiple_of(core * half + above(place, core, k, n_mp) * piece, piece)
+
+
+def gen_kernel(place, normed, mine, other, *refs):
+    preact_ref, active_ref, own, across = refs[:4]
+    blocks, rows_of = refs[4:-1], refs[-1]
     piece = own.shape[0]
-    n_mp = rows // piece
-    core = place[0]
-    rows_of = normed[pl.ds(row_at(core, rows), rows), :]
+    n_mp = rows_of.shape[0] // piece
+    for i, at in enumerate(gen_rows(place, place[0], piece, n_mp)):
+        rows_of[i * piece : (i + 1) * piece, :] = normed[pl.ds(at, piece), :]
 
     def run(w_in, w_out):
-        preact, active, partial = forward_part(rows_of, w_in[...], w_out[...])
+        preact, active, partial = forward_part(rows_of[...], w_in[...], w_out[...])
         preact_ref[...] = preact
         active_ref[...] = active
-        whole[...] = partial
+        for k, block in enumerate(blocks):
+            block[...] = partial[2 * k * piece : 2 * (k + 1) * piece, :]
+        at = 2 * len(blocks) * piece
+        own[...] = partial[at : at + piece, :]
+        across[...] = partial[at + piece :, :]
 
     on_core(place, run, mine, other)
-    own[...] = whole[pl.ds(row_at(place[2], piece), piece), :]
-    across[...] = whole[pl.ds(row_at(above(place, core, n_mp // 2, n_mp), piece), piece), :]
-    for k in range(1, n_mp // 2):
-        to = slice((k - 1) * piece, k * piece)
-        kept[to, :] = whole[pl.ds(row_at(above(place, core, k, n_mp), piece), piece), :]
-        away[to, :] = whole[pl.ds(row_at(above(place, 1 - core, k, n_mp), piece), piece), :]
-
-
-def join_kernel(kept, came, *outs):
-    piece = outs[0].shape[0] // 2
-    for k, out in enumerate(outs):
-        out[:piece, :] = kept[k * piece : (k + 1) * piece, :]
-        out[piece:, :] = came[k * piece : (k + 1) * piece, :]
-
-
-def sums_kernel(own, across, *refs):
+
+
+def sums_kernel(place, own, across, *refs):
     blocks, out = refs[:-1], refs[-1]
     piece = own.shape[0]
-    near = own[...].astype(F32) + across[...].astype(F32)
-    far = 0.0
+    total = 0.0
     for block in blocks:
-        near = near + block[:piece, :].astype(F32)
-        far = far + block[piece:, :].astype(F32)
-    out[:piece, :] = near
-    out[piece:, :] = far
+        total = total + block[...].astype(F32)
+    out[...] = total
+    at = pl.ds(row_at(place[0], piece), piece)
+    out[at, :] = out[at, :] + (own[...].astype(F32) + across[...].astype(F32))
 
 
 def latent_kernel(place, scales, sums, came, stream, scaled, latents, noised, mine):
     piece = mine.shape[0]
-    totals = (sums[:piece, :] + came[piece:, :], came[:piece, :] + sums[piece:, :])
-
-    def run(ordered):
-        for core, total in enumerate(ordered):
-            at = slice(core * piece, (core + 1) * piece)
-            latents[at, :] = stream[at, :] + total
-            noised[at, :] = (scales[0] * latents[at, :] + scaled[at, :]).astype(BF16)
-
-    pl.when(place[0] == 0)(lambda: run(totals))
-    pl.when(place[0] != 0)(lambda: run(totals[::-1]))
+    latents[...] = stream[...] + (sums[...] + came[...])
+    noised[...] = (scales[0] * latents[...] + scaled[...]).astype(BF16)
     mine[...] = noised[pl.ds(row_at(place[0], piece), piece), :]
-
-
-def order_kernel(*refs):
-    blocks, out = refs[:-1], refs[-1]
-    at = 0
-    for block in blocks:
-        out[at : at + block.shape[0], :] = block[...]
-        at += block.shape[0]
 
 
 def rows_in_order(place, own, came, pair, store):
     piece = pair.shape[0] // 2
-    n_mp = (own.shape[0] // piece + 1) // 2 * 2
+    n_mp = 2 * len(own)
     half = n_mp * piece
 
     def at(core, z):
@@ -197,18 +181,18 @@
 
     for core in range(2):
         store(at(core, place[2]), pair[core * piece : (core + 1) * piece, :])
-    for source, sender in ((own, place[0]), (came, 1 - place[0])):
-        for k in range(1, n_mp // 2):
-            z = above(place, sender, -k, n_mp)
+    for blocks, sender in ((own, place[0]), (came, 1 - place[0])):
+        for k, block in enumerate(blocks[:-1]):
+            z = above(place, sender, -(k + 1), n_mp)
             for core in range(2):
-                to = ((k - 1) * 2 + core) * piece
-                store(at(core, z), source[to : to + piece, :])
-        to = (n_mp - 2) * piece
-        store(at(sender, above(place, sender, n_mp // 2, n_mp)), source[to : to + piece, :])
-
-
-def score_kernel(place, pair, own, came, embed, weights, out, both):
+                store(at(core, z), block[core * piece : (core + 1) * piece, :])
+        store(at(sender, above(place, sender, n_mp // 2, n_mp)), blocks[-1][...])
+
+
+def score_kernel(place, pair, *refs):
+    embed, weights, out, both = refs[-4:]
     n_mp, piece = out.shape[0], out.shape[1] // 2
+    own, came = refs[: n_mp // 2], refs[n_mp // 2 : n_mp]
     width = embed.shape[1]
     half = n_mp * piece
     rows = 2 * half
@@ -243,15 +227,30 @@
         finish(uncond + GUIDANCE * (cond - uncond))
 
 
-def refresh_kernel(place, pair, own, came, embed, weights, normed, preact, active):
+def refresh_kernel(place, pair, *refs):
+    embed, weights, normed_gen, active_own, active_came, preact_own, preact_came = refs[-10:-3]
+    normed, preact, active = refs[-3:]
+    piece = pair.shape[0] // 2
+    n_mp = normed.shape[0] // (2 * piece)
+    own, came = refs[: n_mp // 2], refs[n_mp // 2 : n_mp]
+    hidden = preact.shape[1]
+
     def store(at, value):
-        rows = value.shape[0]
-        normed[pl.ds(at, rows), :] = normalize(value.astype(F32) + embed[...])
-
-    rows_in_order(place, own, came, pair, store)
-    hidden = preact.shape[1]
-    preact[...] = jnp.dot(normed[...], weights[:, :hidden], preferred_element_type=F32)
-    active[...] = jax.nn.gelu(preact[...]).astype(BF16)
+        normed[pl.ds(at, piece), :] = normalize(value.astype(F32) + embed[...])
+
+    @pl.when(place[0] == 0)
+    def _():
+        rows_in_order(place, own, came, pair, store)
+        preact[...] = jnp.dot(normed[...], weights[:, :hidden], preferred_element_type=F32)
+        active[...] = jax.nn.gelu(preact[...]).astype(BF16)
+
+    @pl.when(place[0] != 0)
+    def _():
+        normed[...] = normed_gen[...]
+        for core, acts, pres in ((1, active_own, preact_own), (0, active_came, preact_came)):
+            for i, at in enumerate(gen_rows(place, core, piece, n_mp)):
+                active[pl.ds(at, piece), :] = acts[i * piece : (i + 1) * piece, :]
+                preact[pl.ds(at, piece), :] = pres[i * piece : (i + 1) * piece, :]
 
 
 def total_kernel(blocks, out):
@@ -404,9 +403,8 @@
 
     def outgoing(models):
         lanes = hidden * len(models)
-        return call(
-            lay_kernel, "lay", models, [], [shape((4 * n_dp, row_piece, lanes), BF16)]
-        )[0]
+        blocks = [shape((4 * n_dp, row_piece, lanes), BF16)]
+        return call(lay_kernel, "lay", models, [], blocks, room=60)[0]
 
     def gather(blocks):
         return lax.all_to_all(blocks, PLANE, 0, 0, tiled=True).reshape(width, -1)
@@ -442,42 +440,38 @@
     gen_other = core_swap(gen_mine)
 
     steps = n_mp // 2 - 1
-    some = shape((steps * piece, width), BF16)
     one = shape((piece, width), BF16)
     two = shape((2 * piece, width), BF16)
-    preact_gen, active_gen, kept, across, own, away = call(
+    preact_gen, active_gen, own, across, *sent = call(
         gen_kernel,
         "generate",
         [normed_gen, gen_mine, gen_other],
         [place],
-        [shape((rows, hidden), F32), shape((rows, hidden), BF16), some, one, one, some],
+        [shape((rows, hidden), F32), shape((rows, hidden), BF16), one, one] + [two] * steps,
         2 * work,
         [pltpu.VMEM((rows, width), BF16)],
         room=60,
     )
-    joined = call(join_kernel, "join", [kept, core_swap(away)], [], [two] * steps)
-    came = [paired(block, k + 1) for k, block in enumerate(joined)]
+    came = [paired(block, k + 1) for k, block in enumerate(sent)]
     across = paired(across, n_mp // 2)
     both_f32 = shape((2 * piece, width), F32)
-    (sums,) = call(sums_kernel, "sums", [own, across] + came, [], [both_f32])
+    (sums,) = call(sums_kernel, "sums", [own, across] + came, [place], [both_f32], room=60)
     latents, noised, noised_mine = call(
         latent_kernel,
         "latent",
         [sums, core_swap(sums), stream, scaled_noise],
         [place, scales],
         [both_f32, two, one],
-    )
-    blocks = [paired(noised, k + 1) for k in range(steps)]
-    blocks.append(paired(noised_mine, n_mp // 2))
-    (around,) = call(
-        order_kernel, "order", blocks, [], [shape(((2 * steps + 1) * piece, width), BF16)]
-    )
+        room=60,
+    )
+    around = [paired(noised, k + 1) for k in range(steps)]
+    around.append(paired(noised_mine, n_mp // 2))
+    around += [core_swap(block) for block in around]
     score_weights, around = lax.optimization_barrier((score_weights, around))
-    around_other = core_swap(around)
     (score_parts,) = call(
         score_kernel,
         "score",
-        [noised, around, around_other, embedding, score_weights],
+        [noised] + around + [embedding, score_weights],
         [place],
         [shape((n_mp, 2 * piece, width + LANES), F32)],
         8 * work,
@@ -496,13 +490,17 @@
         [total, core_swap(total), latents, noised],
         [place],
         [shape((2 * piece, width + LANES), F32)],
-    )
-
-    message, around, around_other = lax.optimization_barrier((message, around, around_other))
-    normed_cond, preact_fake, active_fake = call(
+        room=60,
+    )
+
+    message, around = lax.optimization_barrier((message, around))
+    normed, preact, active = call(
         refresh_kernel,
         "refresh",
-        [noised, around, around_other, embedding, score_weights],
+        [noised]
+        + around
+        + [embedding, score_weights, normed_gen]
+        + [active_gen, core_swap(active_gen), preact_gen, core_swap(preact_gen)],
         [place],
         [
             shape((positions, width), BF16),
@@ -511,13 +509,6 @@
         ],
         2 * work,
     )
-    first = core == 0
-
-    def chosen(fake_value, gen_value):
-        gen_all = jnp.concatenate([core_swap(gen_value), gen_value], axis=0)
-        return jnp.where(first, fake_value, gen_all)
-
-    preact = chosen(preact_fake, preact_gen)
     slope = jax.vjp(jax.nn.gelu, preact)[1](jnp.ones_like(preact))[0]
     size = row_piece * hidden // LANES
     (grads,) = call(
@@ -527,10 +518,10 @@
         "grads",
         [
             exchange(jnp.broadcast_to(message[None], (n_mp,) + message.shape)),
-            jnp.where(first, score_weights[:, hidden:], gen_mine),
+            jnp.where(core == 0, score_weights[:, hidden:], gen_mine),
             slope,
-            jnp.where(first, normed_cond, normed_gen),
-            chosen(active_fake, active_gen),
+            normed,
+            active,
         ],
         [place],
         [shape((len(WALK), 4 * size + 16, LANES), F32)],

time: 209 us -> 217 us (1.038)
  waiting for transfers between devices: 49.3 us -> 42.2 us
  Pallas kernels: 19.6 us -> 26.2 us
  local copies, waits for them, and re-layouts: 11.1 us -> 16.2 us
  starting transfers between devices: 43.1 us -> 47.4 us
    pallas_call x15 -> x13, Pallas kernels: 19.6 us -> 26.2 us  [call(): pl.pallas_call(body, name=name, out_shape=outs, in_specs=[SMEM] * len(sca...]
    unnamed x52 -> x94, local copies, waits for them, and re-layouts: 9.01 us -> 14.1 us
    ppermute x8 -> x10, starting transfers between devices: 5.85 us -> 10.1 us  [core_swap(): return lax.ppermute(block, 'group', [(0, 1), (1, 0), (2, 3), (3, 2)])]
    ppermute x8, waiting for transfers between devices: 10.5 us -> 6.29 us  [paired(): return lax.ppermute(block, ('group', 'mp'), pairs)]
    all_to_all x1, blocking collectives: 45.1 us -> 47.6 us  [local(): lax.all_to_all(grads.astype(jnp.float16), PLANE, 0, 0, axis_index_groups=...]
    all_to_all x1, blocking collectives: 27.7 us -> 25.4 us  [exchange(): lax.all_to_all(blocks.astype(jnp.float16), 'mp', 0, 0, tiled=True)]
    ppermute x8 -> x10, waiting for transfers between devices: 9.1 us -> 7.23 us  [core_swap(): return lax.ppermute(block, 'group', [(0, 1), (1, 0), (2, 3), (3, 2)])]
  transfers between devices with their start and end apart: 19 -> 21, of which waited for: 10 -> 9; matrix products, arithmetic and copies ran while one was open for 4% -> 3% of each run, Pallas kernels for 4% -> 6%
where the time goes in v4:
time: 217 us; the launch traced here: 216 us
  blocking collectives  73 us (34%)
  starting transfers between devices  47.4 us (22%)
  waiting for transfers between devices  42.2 us (19%)
  Pallas kernels  26.2 us (12%)
  local copies, waits for them, and re-layouts  16.2 us (7%)
  other arithmetic  7.5 us (3%)
  between operations  3.65 us (2%)
    all_to_all x1, blocking collectives, local(): lax.all_to_all(grads.astype(jnp.float16), PLANE, 0, 0, axis_index_groups=...  47.6 us
    pallas_call x13, Pallas kernels, call(): pl.pallas_call(body, name=name, out_shape=outs, in_specs=[SMEM] * len(sca...  26.2 us
    all_to_all x1, blocking collectives, exchange(): lax.all_to_all(blocks.astype(jnp.float16), 'mp', 0, 0, tiled=True)  25.4 us
    ppermute x8, starting transfers between devices, paired(): return lax.ppermute(block, ('group', 'mp'), pairs)  19.9 us
    all_to_all x1, waiting for transfers between devices, exchange(): lax.all_to_all(blocks.astype(jnp.float16), 'mp', 0, 0, tiled=True)  15.6 us
    unnamed x94, local copies, waits for them, and re-layouts  14.1 us
    all_to_all x2, starting transfers between devices, gather(): return lax.all_to_all(blocks, PLANE, 0, 0, tiled=True).reshape(width, -1)  13.2 us
    all_to_all x2, waiting for transfers between devices, gather(): return lax.all_to_all(blocks, PLANE, 0, 0, tiled=True).reshape(width, -1)  13.1 us
  transfers between devices with their start and end apart: 21, of which 9 were waited for; matrix products, arithmetic and copies ran while one was open for 3% of the time, Pallas kernels for 6%

profile of v4, /device:TPU:1, one launch (start us, length us, event | category | flops | bytes accessed | tf_op | source)
XLA Modules:
  0.0 216.2 jit_solution(12096146884416653721)
XLA Ops:
  0.6 2.4 %lay.2 = bf16[32,40,640]{2,1,0:T(8,128)(2,1)} custom-call(bf16[40,2,640]{2,1,0:T(2,128)(2,1)} %refs_0_.2), custom_call_target="tpu_custom_call" | custom-call | bytes 1740800 | tf_op jit(solution)/shard_map/lay/pallas_call | solution.py:35
  3.0 8.8 %all-to-all-start = ((bf16[32,40,640]{2,1,0:T(8,128)(2,1)}), bf16[32,40,640]{2,1,0:T(8,128)(2,1)}, u32[]{:S(2)}, u32[]{:S(2)}) async-start(bf16[32,40,640]{2,1,0:T(8,128)(2,1)} %lay.2), calls=%async_computation | async-start | bytes 3276800 | tf_op jit(solution)/shard_map/all_to_all | solution.py:410
  15.6 3.3 %lay.3 = bf16[32,40,1280]{2,1,0:T(8,128)(2,1)} custom-call(bf16[40,2,640]{2,1,0:T(2,128)(2,1)} %refs_0_.3, bf16[40,2,640]{2,1,0:T(2,128)(2,1)} %refs_1_.1), custom_call_target="tpu_custom_call" | custom-call | bytes 3481600 | tf_op jit(solution)/shard_map/lay/pallas_call | solution.py:35
  19.8 0.8 prepare.1
  20.6 0.9 copy-done.1
  22.8 13.1 %all-to-all-done = bf16[32,40,640]{2,1,0:T(8,128)(2,1)} async-done(((bf16[32,40,640]{2,1,0:T(8,128)(2,1)}), bf16[32,40,640]{2,1,0:T(8,128)(2,1)}, u32[]{:S(2)}, u32[]{:S(2)}) %all-to-all-start) | async-done | bytes 1638432 | tf_op jit(solution)/shard_map/all_to_all | solution.py:410
  35.9 4.4 %all-to-all-start.1 = ((bf16[32,40,1280]{2,1,0:T(8,128)(2,1)}), bf16[32,40,1280]{2,1,0:T(8,128)(2,1)S(1)}, u32[]{:S(2)}, u32[]{:S(2)}) async-start(bf16[32,40,1280]{2,1,0:T(8,128)(2,1)} %lay.3), calls=%async_computation.1 | async-start | bytes 6553600 | tf_op jit(solution)/shard_map/all_to_all | solution.py:410
  40.7 3.6 %collective-permute-done.other = bf16[1280,640]{1,0:T(8,128)(2,1)} collective-permute-done((bf16[1280,640]{1,0:T(8,128)(2,1)}, bf16[1280,640]{1,0:T(8,128)(2,1)}, u32[]{:S(2)}, u32[]{:S(2)}) %collective-permute-start) | collective-permute-done | bytes 1638432 | tf_op jit(solution)/shard_map/ppermute | solution.py:67
  44.3 4.0 %generate.1 = (f32[128,640]{1,0:T(8,128)}, bf16[128,640]{1,0:T(8,128)(2,1)}, bf16[16,1280]{1,0:T(8,128)(2,1)}, bf16[16,1280]{1,0:T(8,128)(2,1)}, bf16[32,1280]{1...) custom-call(s32[3]{0:T(128)} %copy-done.29, bf16[256,1280]{1,0:T(8,128)(2,1)} %copy-done.1, ...), custom_call_target="tpu_custom_call" | custom-call | flops 419430400 | bytes 4751360 | tf_op jit(solution)/shard_map/generate/pallas_call | solution.py:35
  48.3 5.6 %collective-permute-start.2 = (bf16[32,1280]{1,0:T(8,128)(2,1)}, bf16[32,1280]{1,0:T(8,128)(2,1)S(1)}, u32[]{:S(2)}, u32[]{:S(2)}) collective-permute-start(bf16[32,1280]{1,0:T(8,128)(2,1)} %get-tuple-element.55), channel_id=1, source_target_pairs={{0,1},{1,2},{2,3},{3,4},{4,5},{5,6},{6,7},{7,0},{64,71},{65,64},{6... | collective-permute-start | bytes 245768 | tf_op jit(solution)/shard_map/ppermute | solution.py:77
  53.8 1.2 collective-permute-start.3
  55.5 4.5 %collective-permute-start.1 = (bf16[16,1280]{1,0:T(8,128)(2,1)}, bf16[16,1280]{1,0:T(8,128)(2,1)S(1)}, u32[]{:S(2)}, u32[]{:S(2)}) collective-permute-start(bf16[16,1280]{1,0:T(8,128)(2,1)} %get-tuple-element.54), channel_id=1, source_target_pairs={{0,4},{1,5},{2,6},{3,7},{4,0},{5,1},{6,2},{7,3},{64,68},{65,69},{6... | collective-permute-start | bytes 122888 | tf_op jit(solution)/shard_map/ppermute | solution.py:77
  59.9 4.3 %collective-permute-done.1.across = bf16[16,1280]{1,0:T(8,128)(2,1)S(1)} collective-permute-done((bf16[16,1280]{1,0:T(8,128)(2,1)}, bf16[16,1280]{1,0:T(8,128)(2,1)S(1)}, u32[]{:S(2)}, u32[]{:S(2)}) %collective-permute-start.1) | collective-permute-done | bytes 40992 | tf_op jit(solution)/shard_map/ppermute | solution.py:77
  64.9 1.7 sums.1
  66.7 1.7 collective-permute-start.5
  68.3 1.2 collective-permute-done.5.came
  70.2 1.9 latent.1
  72.2 2.0 collective-permute-start.8
  74.2 1.2 collective-permute-start.7
  75.4 2.4 %collective-permute-start.6 = (bf16[32,1280]{1,0:T(8,128)(2,1)}, bf16[32,1280]{1,0:T(8,128)(2,1)S(1)}, u32[]{:S(2)}, u32[]{:S(2)}) collective-permute-start(bf16[32,1280]{1,0:T(8,128)(2,1)} %get-tuple-element.60.pair.refs_4_), channel_id=1, source_target_pairs={{0,1},{1,2},{2,3},{3,4},{4,5},{5,6},{6,7},{7,0},{64,71},{65,64},{6... | collective-permute-start | bytes 245768 | tf_op jit(solution)/shard_map/ppermute | solution.py:77
  77.8 2.5 %collective-permute-start.9 = (bf16[16,1280]{1,0:T(8,128)(2,1)}, bf16[16,1280]{1,0:T(8,128)(2,1)S(1)}, u32[]{:S(2)}, u32[]{:S(2)}) collective-permute-start(bf16[16,1280]{1,0:T(8,128)(2,1)} %get-tuple-element.62), channel_id=1, source_target_pairs={{0,4},{1,5},{2,6},{3,7},{4,0},{5,1},{6,2},{7,3},{64,68},{65,69},{6... | collective-permute-start | bytes 122888 | tf_op jit(solution)/shard_map/ppermute | solution.py:77
  80.4 1.0 collective-permute-start.12
  81.4 2.8 %collective-permute-start.11 = (bf16[32,1280]{1,0:T(8,128)(2,1)S(1)}, bf16[32,1280]{1,0:T(8,128)(2,1)S(1)}, u32[]{:S(2)}, u32[]{:S(2)}) collective-permute-start(bf16[32,1280]{1,0:T(8,128)(2,1)S(1)} %collective-permute-done.7.refs_1_), channel_id=1, source_target_pairs={{0,64},{64,0},{128,192},{192,128},{1,65},{65,1},{129,193},{193,129... | collective-permute-start | bytes 245768 | tf_op jit(solution)/shard_map/ppermute | solution.py:67
  84.2 0.8 collective-permute-start.10
  85.0 2.0 collective-permute-done.9.refs_3_
  91.1 0.9 copy-done.11
  92.0 0.9 copy-done.21
  92.8 0.9 copy-done.24
  93.7 0.9 copy-done.27
  94.6 0.8 copy-done.33
  95.4 0.8 copy-done.36
  96.2 3.6 %score.1 = f32[8,32,1408]{2,1,0:T(8,128)S(1)} custom-call(s32[3]{0:T(128)S(1)} %copy-done.30, bf16[32,1280]{1,0:T(8,128)(2,1)S(1)} %copy-done.11, bf16[32,1280]{1,0:T(8,128)(2,1)S(1)} %collective-permute-done.6.refs_0_, bf16[32,1280]{1,0:T(8,128)(2,1)S(1)} %collective-permute-done.7.refs_1_, bf16[32,1280]{1,0:T(8,128)(2,1)S(1)} %collective-permute-done.8.refs_2_, ...), custom_call_target="tpu_custom_call" | custom-call | flops 1677721600 | bytes 5379072 | tf_op jit(solution)/shard_map/score/pallas_call | solution.py:35
  99.9 25.4 %all_to_all.25 = f16[8,32,1408]{2,1,0:T(8,128)(2,1)S(1)} all-to-all(f16[8,32,1408]{2,1,0:T(8,128)(2,1)S(1)} %convert_element_type.28), channel_id=1, replica_groups=mesh['group'=4,'dp'=8,'mp'=8] {'mp'}, dimensions={0} | all-to-all | bytes 1441792 | tf_op jit(solution)/shard_map/all_to_all | solution.py:482
  126.1 1.0 collective-permute-done.14.refs_2_
  127.7 2.0 pack.1
  129.8 0.9 convert_element_type.30
  130.7 0.9 broadcast_in_dim.2
  131.6 4.2 %all-to-all-start.3 = ((f16[8,32,1408]{2,1,0:T(8,128)(2,1)}), f16[8,32,1408]{2,1,0:T(8,128)(2,1)}, u32[]{:S(2)}, u32[]{:S(2)}) async-start(f16[8,32,1408]{2,1,0:T(8,128)(2,1)} %broadcast_in_dim.2), calls=%async_computation.3 | async-start | bytes 1441792 | tf_op jit(solution)/shard_map/all_to_all | solution.py:482
  136.6 3.0 %slice_select_fusion.refs_2_ = bf16[1280,640]{1,0:T(8,128)(2,1)} fusion(bf16[1280,640]{1,0:T(8,128)(2,1)} %bitcast.3.mine, bf16[1280,1280]{1,0:T(8,128)(2,1)S(1)} %bitcast.7, pred[]{:T(512)S(6)} %eq.5), kind=kLoop, calls=%fused_computation | loop fusion | flops 819200 | bytes 4915201 | tf_op jit(solution)/shard_map/jit(_where)/select_n | solution.py:521
  140.4 0.8 copy-done.5
  142.4 15.6 %all-to-all-done.3 = f16[8,32,1408]{2,1,0:T(8,128)(2,1)} async-done(((f16[8,32,1408]{2,1,0:T(8,128)(2,1)}), f16[8,32,1408]{2,1,0:T(8,128)(2,1)}, u32[]{:S(2)}, u32[]{:S(2)}) %all-to-all-start.3) | async-done | bytes 720928 | tf_op jit(solution)/shard_map/all_to_all | solution.py:482
  158.0 1.2 convert_element_type.31.refs_1_
  159.3 2.9 %grads.1 = f32[16,816,128]{2,1,0:T(8,128)S(1)} custom-call(s32[3]{0:T(128)S(1)} %copy-done.31, f32[8,32,1408]{2,1,0:T(8,128)S(1)} %convert_element_type.31.refs_1_, bf16[1280,640]{1,0:T(8,128)(2,1)S(1)} %copy-done, f32[256,640]{1,0:T(8,128)S(1)} %fusion.5.refs_3_, bf16[256,1280]{1,0:T(8,128)(2,1)S(1)} %copy-done.6, bf16[256,640]{1,0:T(8,128)(2,1)S(1)} %copy-done.10), custom_call_target="tpu_custom_call" | custom-call | flops 1258291200 | bytes 11403264 | tf_op jit(solution)/shard_map/grads/pallas_call | solution.py:35
  162.7 47.6 %all_to_all.26 = f16[16,816,128]{2,1,0:T(8,128)(2,1)S(1)} all-to-all(f16[16,816,128]{2,1,0:T(8,128)(2,1)S(1)} %convert_element_type.32), channel_id=1, replica_groups={{0,16,32,48,176,160,144,24,40,56,184,168,152,136,8,128},{64,80,96,112,2..., dimensions={0} | all-to-all | bytes 6684672 | tf_op jit(solution)/shard_map/all_to_all | solution.py:531
  210.8 1.2 collect.1
  211.9 1.6 collective-permute-start.17
  213.6 1.1 collective-permute-done.17.came
  214.6 1.5 place.1
  (117 shorter events, 14.5 us)
Async XLA Ops:
  3.0 8.8 %copy-start.45 = (s32[2]{0:T(128)S(1)}, s32[2]{0:T(128)}, u32[]{:S(2)}) copy-start(s32[2]{0:T(128)} %param.10) | copy-start | bytes 28
  3.0 10.2 %copy-start.46 = (s32[2]{0:T(128)S(1)}, s32[2]{0:T(128)}, u32[]{:S(2)}) copy-start(s32[2]{0:T(128)} %param.11) | copy-start | bytes 28
  3.0 32.9 %all-to-all-start = ((bf16[32,40,640]{2,1,0:T(8,128)(2,1)}), bf16[32,40,640]{2,1,0:T(8,128)(2,1)}, u32[]{:S(2)}, u32[]{:S(2)}) async-start(bf16[32,40,640]{2,1,0:T(8,128)(2,1)} %lay.2), calls=%async_computation | async-start | bytes 3276800 | tf_op jit(solution)/shard_map/all_to_all | solution.py:410
  15.6 4.2 %copy-start.3 = (bf16[2,256,1280]{2,1,0:T(8,128)(2,1)S(1)}, bf16[2,256,1280]{2,1,0:T(8,128)(2,1)}, u32[]{:S(2)}) copy-start(bf16[2,256,1280]{2,1,0:T(8,128)(2,1)} %refs_2_.1) | copy-start | bytes 3932164
  15.6 4.2 %copy-start.4 = (bf16[2,256,1280]{2,1,0:T(8,128)(2,1)S(1)}, bf16[2,256,1280]{2,1,0:T(8,128)(2,1)}, u32[]{:S(2)}) copy-start(bf16[2,256,1280]{2,1,0:T(8,128)(2,1)} %refs_3_.1) | copy-start | bytes 3932164
  18.9 17.0 %copy-start.38 = (f32[2]{0:T(128)}, f32[2]{0:T(128)S(1)}, u32[]{:S(2)}) copy-start(f32[2]{0:T(128)S(1)} %pad_maximum_fusion.refs_1_.scales) | copy-start | bytes 28
  19.0 16.9 %copy-start.29 = (s32[3]{0:T(128)}, s32[3]{0:T(128)S(1)}, u32[]{:S(2)}) copy-start(s32[3]{0:T(128)S(1)} %pad_add_fusion.refs_0_.place) | copy-start | bytes 40
  35.9 55.1 %all-to-all-start.1 = ((bf16[32,40,1280]{2,1,0:T(8,128)(2,1)}), bf16[32,40,1280]{2,1,0:T(8,128)(2,1)S(1)}, u32[]{:S(2)}, u32[]{:S(2)}) async-start(bf16[32,40,1280]{2,1,0:T(8,128)(2,1)} %lay.3), calls=%async_computation.1 | async-start | bytes 6553600 | tf_op jit(solution)/shard_map/all_to_all | solution.py:410
  40.3 50.7 %copy-start.30 = (s32[3]{0:T(128)S(1)}, s32[3]{0:T(128)}, u32[]{:S(2)}) copy-start(s32[3]{0:T(128)} %copy-done.29) | copy-start | bytes 40
  40.3 3.9 %collective-permute-start = (bf16[1280,640]{1,0:T(8,128)(2,1)}, bf16[1280,640]{1,0:T(8,128)(2,1)}, u32[]{:S(2)}, u32[]{:S(2)}) collective-permute-start(bf16[1280,640]{1,0:T(8,128)(2,1)} %bitcast.3.mine), channel_id=1, source_target_pairs={{0,64},{64,0},{128,192},{192,128},{1,65},{65,1},{129,193},{193,129... | collective-permute-start | bytes 4915208 | tf_op jit(solution)/shard_map/ppermute | solution.py:67
  48.3 15.9 %collective-permute-start.2 = (bf16[32,1280]{1,0:T(8,128)(2,1)}, bf16[32,1280]{1,0:T(8,128)(2,1)S(1)}, u32[]{:S(2)}, u32[]{:S(2)}) collective-permute-start(bf16[32,1280]{1,0:T(8,128)(2,1)} %get-tuple-element.55), channel_id=1, source_target_pairs={{0,1},{1,2},{2,3},{3,4},{4,5},{5,6},{6,7},{7,0},{64,71},{65,64},{6... | collective-permute-start | bytes 245768 | tf_op jit(solution)/shard_map/ppermute | solution.py:77
  53.8 10.4 %collective-permute-start.3 = (bf16[32,1280]{1,0:T(8,128)(2,1)}, bf16[32,1280]{1,0:T(8,128)(2,1)S(1)}, u32[]{:S(2)}, u32[]{:S(2)}) collective-permute-start(bf16[32,1280]{1,0:T(8,128)(2,1)} %get-tuple-element.56), channel_id=1, source_target_pairs={{0,2},{1,3},{2,4},{3,5},{4,6},{5,7},{6,0},{7,1},{64,70},{65,71},{6... | collective-permute-start | bytes 245768 | tf_op jit(solution)/shard_map/ppermute | solution.py:77
  55.0 9.2 %collective-permute-start.4 = (bf16[32,1280]{1,0:T(8,128)(2,1)}, bf16[32,1280]{1,0:T(8,128)(2,1)S(1)}, u32[]{:S(2)}, u32[]{:S(2)}) collective-permute-start(bf16[32,1280]{1,0:T(8,128)(2,1)} %get-tuple-element.57), channel_id=1, source_target_pairs={{0,3},{1,4},{2,5},{3,6},{4,7},{5,0},{6,1},{7,2},{64,69},{65,70},{6... | collective-permute-start | bytes 245768 | tf_op jit(solution)/shard_map/ppermute | solution.py:77
  55.5 8.7 %collective-permute-start.1 = (bf16[16,1280]{1,0:T(8,128)(2,1)}, bf16[16,1280]{1,0:T(8,128)(2,1)S(1)}, u32[]{:S(2)}, u32[]{:S(2)}) collective-permute-start(bf16[16,1280]{1,0:T(8,128)(2,1)} %get-tuple-element.54), channel_id=1, source_target_pairs={{0,4},{1,5},{2,6},{3,7},{4,0},{5,1},{6,2},{7,3},{64,68},{65,69},{6... | collective-permute-start | bytes 122888 | tf_op jit(solution)/shard_map/ppermute | solution.py:77
  66.7 2.9 %collective-permute-start.5 = (f32[32,1280]{1,0:T(8,128)}, f32[32,1280]{1,0:T(8,128)S(1)}, u32[]{:S(2)}, u32[]{:S(2)}) collective-permute-start(f32[32,1280]{1,0:T(8,128)} %sums.1), channel_id=1, source_target_pairs={{0,64},{64,0},{128,192},{192,128},{1,65},{65,1},{129,193},{193,129... | collective-permute-start | bytes 491528 | tf_op jit(solution)/shard_map/ppermute | solution.py:67
  72.2 8.2 %collective-permute-start.8 = (bf16[32,1280]{1,0:T(8,128)(2,1)}, bf16[32,1280]{1,0:T(8,128)(2,1)S(1)}, u32[]{:S(2)}, u32[]{:S(2)}) collective-permute-start(bf16[32,1280]{1,0:T(8,128)(2,1)} %get-tuple-element.60.pair.refs_4_), channel_id=1, source_target_pairs={{0,3},{1,4},{2,5},{3,6},{4,7},{5,0},{6,1},{7,2},{64,69},{65,70},{6... | collective-permute-start | bytes 245768 | tf_op jit(solution)/shard_map/ppermute | solution.py:77
  74.2 7.2 %collective-permute-start.7 = (bf16[32,1280]{1,0:T(8,128)(2,1)}, bf16[32,1280]{1,0:T(8,128)(2,1)S(1)}, u32[]{:S(2)}, u32[]{:S(2)}) collective-permute-start(bf16[32,1280]{1,0:T(8,128)(2,1)} %get-tuple-element.60.pair.refs_4_), channel_id=1, source_target_pairs={{0,2},{1,3},{2,4},{3,5},{4,6},{5,7},{6,0},{7,1},{64,70},{65,71},{6... | collective-permute-start | bytes 245768 | tf_op jit(solution)/shard_map/ppermute | solution.py:77
  75.4 8.8 %collective-permute-start.6 = (bf16[32,1280]{1,0:T(8,128)(2,1)}, bf16[32,1280]{1,0:T(8,128)(2,1)S(1)}, u32[]{:S(2)}, u32[]{:S(2)}) collective-permute-start(bf16[32,1280]{1,0:T(8,128)(2,1)} %get-tuple-element.60.pair.refs_4_), channel_id=1, source_target_pairs={{0,1},{1,2},{2,3},{3,4},{4,5},{5,6},{6,7},{7,0},{64,71},{65,64},{6... | collective-permute-start | bytes 245768 | tf_op jit(solution)/shard_map/ppermute | solution.py:77
  77.8 9.2 %collective-permute-start.9 = (bf16[16,1280]{1,0:T(8,128)(2,1)}, bf16[16,1280]{1,0:T(8,128)(2,1)S(1)}, u32[]{:S(2)}, u32[]{:S(2)}) collective-permute-start(bf16[16,1280]{1,0:T(8,128)(2,1)} %get-tuple-element.62), channel_id=1, source_target_pairs={{0,4},{1,5},{2,6},{3,7},{4,0},{5,1},{6,2},{7,3},{64,68},{65,69},{6... | collective-permute-start | bytes 122888 | tf_op jit(solution)/shard_map/ppermute | solution.py:77
  80.4 8.8 %collective-permute-start.12 = (bf16[32,1280]{1,0:T(8,128)(2,1)S(1)}, bf16[32,1280]{1,0:T(8,128)(2,1)S(1)}, u32[]{:S(2)}, u32[]{:S(2)}) collective-permute-start(bf16[32,1280]{1,0:T(8,128)(2,1)S(1)} %collective-permute-done.8.refs_2_), channel_id=1, source_target_pairs={{0,64},{64,0},{128,192},{192,128},{1,65},{65,1},{129,193},{193,129... | collective-permute-start | bytes 245768 | tf_op jit(solution)/shard_map/ppermute | solution.py:67
  81.4 18.3 %copy-start.16 = (bf16[32,1280]{1,0:T(8,128)(2,1)}, bf16[32,1280]{1,0:T(8,128)(2,1)S(1)}, u32[]{:S(2)}) copy-start(bf16[32,1280]{1,0:T(8,128)(2,1)S(1)} %collective-permute-done.7.refs_1_) | copy-start | bytes 245764
  81.4 8.4 %collective-permute-start.11 = (bf16[32,1280]{1,0:T(8,128)(2,1)S(1)}, bf16[32,1280]{1,0:T(8,128)(2,1)S(1)}, u32[]{:S(2)}, u32[]{:S(2)}) collective-permute-start(bf16[32,1280]{1,0:T(8,128)(2,1)S(1)} %collective-permute-done.7.refs_1_), channel_id=1, source_target_pairs={{0,64},{64,0},{128,192},{192,128},{1,65},{65,1},{129,193},{193,129... | collective-permute-start | bytes 245768 | tf_op jit(solution)/shard_map/ppermute | solution.py:67
  84.2 15.6 %copy-start.18 = (bf16[32,1280]{1,0:T(8,128)(2,1)}, bf16[32,1280]{1,0:T(8,128)(2,1)S(1)}, u32[]{:S(2)}) copy-start(bf16[32,1280]{1,0:T(8,128)(2,1)S(1)} %collective-permute-done.6.refs_0_) | copy-start | bytes 245764
  84.2 6.2 %collective-permute-start.10 = (bf16[32,1280]{1,0:T(8,128)(2,1)S(1)}, bf16[32,1280]{1,0:T(8,128)(2,1)S(1)}, u32[]{:S(2)}, u32[]{:S(2)}) collective-permute-start(bf16[32,1280]{1,0:T(8,128)(2,1)S(1)} %collective-permute-done.6.refs_0_), channel_id=1, source_target_pairs={{0,64},{64,0},{128,192},{192,128},{1,65},{65,1},{129,193},{193,129... | collective-permute-start | bytes 245768 | tf_op jit(solution)/shard_map/ppermute | solution.py:67
  87.0 1.5 collective-permute-start.13
  91.1 0.9 copy-start.11
  91.9 0.9 copy-start.21
  125.6 1.5 copy-start.7
  125.6 1.5 collective-permute-start.14
  127.7 8.1 %copy-start.13 = (bf16[128,640]{1,0:T(8,128)(2,1)S(1)}, bf16[128,640]{1,0:T(8,128)(2,1)}, u32[]{:S(2)}) copy-start(bf16[128,640]{1,0:T(8,128)(2,1)} %get-tuple-element.83.refs_11_) | copy-start | bytes 491524
  131.6 26.4 %all-to-all-start.3 = ((f16[8,32,1408]{2,1,0:T(8,128)(2,1)}), f16[8,32,1408]{2,1,0:T(8,128)(2,1)}, u32[]{:S(2)}, u32[]{:S(2)}) async-start(f16[8,32,1408]{2,1,0:T(8,128)(2,1)} %broadcast_in_dim.2), calls=%async_computation.3 | async-start | bytes 1441792 | tf_op jit(solution)/shard_map/all_to_all | solution.py:482
  135.9 3.8 %collective-permute-start.15 = (bf16[128,640]{1,0:T(8,128)(2,1)S(1)}, bf16[128,640]{1,0:T(8,128)(2,1)S(1)}, u32[]{:S(2)}, u32[]{:S(2)}) collective-permute-start(bf16[128,640]{1,0:T(8,128)(2,1)S(1)} %copy-done.13), channel_id=1, source_target_pairs={{0,64},{64,0},{128,192},{192,128},{1,65},{65,1},{129,193},{193,129... | collective-permute-start | bytes 491528 | tf_op jit(solution)/shard_map/ppermute | solution.py:67
  136.3 3.4 %copy-start.2 = (bf16[256,1280]{1,0:T(8,128)(2,1)S(1)}, bf16[256,1280]{1,0:T(8,128)(2,1)}, u32[]{:S(2)}) copy-start(bf16[256,1280]{1,0:T(8,128)(2,1)} %copy-done.1) | copy-start | bytes 1966084
  136.3 3.4 %copy-start.8 = (f32[128,640]{1,0:T(8,128)S(1)}, f32[128,640]{1,0:T(8,128)}, u32[]{:S(2)}) copy-start(f32[128,640]{1,0:T(8,128)} %get-tuple-element.84.refs_13_) | copy-start | bytes 983044
  136.3 3.4 %copy-start.12 = (bf16[32,1280]{1,0:T(8,128)(2,1)S(1)}, bf16[32,1280]{1,0:T(8,128)(2,1)}, u32[]{:S(2)}) copy-start(bf16[32,1280]{1,0:T(8,128)(2,1)} %get-tuple-element.60.pair.refs_4_) | copy-start | bytes 245764
  136.3 3.4 %copy-start.17 = (bf16[32,1280]{1,0:T(8,128)(2,1)S(1)}, bf16[32,1280]{1,0:T(8,128)(2,1)}, u32[]{:S(2)}) copy-start(bf16[32,1280]{1,0:T(8,128)(2,1)} %copy-done.16) | copy-start | bytes 245764
  136.3 3.4 %copy-start.19 = (bf16[32,1280]{1,0:T(8,128)(2,1)S(1)}, bf16[32,1280]{1,0:T(8,128)(2,1)}, u32[]{:S(2)}) copy-start(bf16[32,1280]{1,0:T(8,128)(2,1)} %copy-done.18) | copy-start | bytes 245764
  136.3 3.4 %copy-start.22 = (bf16[32,1280]{1,0:T(8,128)(2,1)S(1)}, bf16[32,1280]{1,0:T(8,128)(2,1)}, u32[]{:S(2)}) copy-start(bf16[32,1280]{1,0:T(8,128)(2,1)} %copy-done.20) | copy-start | bytes 245764
  136.3 3.4 %copy-start.25 = (bf16[32,1280]{1,0:T(8,128)(2,1)S(1)}, bf16[32,1280]{1,0:T(8,128)(2,1)}, u32[]{:S(2)}) copy-start(bf16[32,1280]{1,0:T(8,128)(2,1)} %copy-done.23) | copy-start | bytes 245764
  136.3 3.4 %copy-start.28 = (bf16[32,1280]{1,0:T(8,128)(2,1)S(1)}, bf16[32,1280]{1,0:T(8,128)(2,1)}, u32[]{:S(2)}) copy-start(bf16[32,1280]{1,0:T(8,128)(2,1)} %copy-done.26) | copy-start | bytes 245764
  136.3 3.4 %copy-start.31 = (s32[3]{0:T(128)S(1)}, s32[3]{0:T(128)}, u32[]{:S(2)}) copy-start(s32[3]{0:T(128)} %copy-done.29) | copy-start | bytes 40
  136.4 3.4 %copy-start.34 = (bf16[16,1280]{1,0:T(8,128)(2,1)S(1)}, bf16[16,1280]{1,0:T(8,128)(2,1)}, u32[]{:S(2)}) copy-start(bf16[16,1280]{1,0:T(8,128)(2,1)} %copy-done.32) | copy-start | bytes 122884
  136.4 3.4 %copy-start.37 = (bf16[16,1280]{1,0:T(8,128)(2,1)S(1)}, bf16[16,1280]{1,0:T(8,128)(2,1)}, u32[]{:S(2)}) copy-start(bf16[16,1280]{1,0:T(8,128)(2,1)} %copy-done.35) | copy-start | bytes 122884
  136.4 3.3 %collective-permute-start.16 = (f32[128,640]{1,0:T(8,128)}, f32[128,640]{1,0:T(8,128)S(1)}, u32[]{:S(2)}, u32[]{:S(2)}) collective-permute-start(f32[128,640]{1,0:T(8,128)} %get-tuple-element.84.refs_13_), channel_id=1, source_target_pairs={{0,64},{64,0},{128,192},{192,128},{1,65},{65,1},{129,193},{193,129... | collective-permute-start | bytes 983048 | tf_op jit(solution)/shard_map/ppermute | solution.py:67
  142.0 17.2 %copy-start = (bf16[1280,640]{1,0:T(8,128)(2,1)S(1)}, bf16[1280,640]{1,0:T(8,128)(2,1)}, u32[]{:S(2)}) copy-start(bf16[1280,640]{1,0:T(8,128)(2,1)} %slice_select_fusion.refs_2_) | copy-start | bytes 4915204
  142.0 17.2 %copy-start.6 = (bf16[256,1280]{1,0:T(8,128)(2,1)S(1)}, bf16[256,1280]{1,0:T(8,128)(2,1)}, u32[]{:S(2)}) copy-start(bf16[256,1280]{1,0:T(8,128)(2,1)} %copy-done.5) | copy-start | bytes 1966084
  142.0 17.2 %copy-start.10 = (bf16[256,640]{1,0:T(8,128)(2,1)S(1)}, bf16[256,640]{1,0:T(8,128)(2,1)}, u32[]{:S(2)}) copy-start(bf16[256,640]{1,0:T(8,128)(2,1)} %copy-done.9) | copy-start | bytes 983044
  211.9 2.7 %collective-permute-start.17 = (f32[400,128]{1,0:T(8,128)S(1)}, f32[400,128]{1,0:T(8,128)S(1)}, u32[]{:S(2)}, u32[]{:S(2)}) collective-permute-start(f32[400,128]{1,0:T(8,128)S(1)} %get-tuple-element.89), channel_id=1, source_target_pairs={{0,64},{64,0},{128,192},{192,128},{1,65},{65,1},{129,193},{193,129... | collective-permute-start | bytes 614408 | tf_op jit(solution)/shard_map/ppermute | solution.py:67
  (20 other events, 14.2 us)

commit v5 on v4

--- a/solution.py
+++ b/solution.py
@@ -171,9 +171,17 @@
     mine[...] = noised[pl.ds(row_at(place[0], piece), piece), :]
 
 
+def order_kernel(*refs):
+    blocks, out = refs[:-1], refs[-1]
+    at = 0
+    for block in blocks:
+        out[at : at + block.shape[0], :] = block[...]
+        at += block.shape[0]
+
+
 def rows_in_order(place, own, came, pair, store):
     piece = pair.shape[0] // 2
-    n_mp = 2 * len(own)
+    n_mp = (own.shape[0] // piece + 1) // 2 * 2
     half = n_mp * piece
 
     def at(core, z):
@@ -181,18 +189,18 @@
 
     for core in range(2):
         store(at(core, place[2]), pair[core * piece : (core + 1) * piece, :])
-    for blocks, sender in ((own, place[0]), (came, 1 - place[0])):
-        for k, block in enumerate(blocks[:-1]):
-            z = above(place, sender, -(k + 1), n_mp)
+    for source, sender in ((own, place[0]), (came, 1 - place[0])):
+        for k in range(1, n_mp // 2):
+            z = above(place, sender, -k, n_mp)
             for core in range(2):
-                store(at(core, z), block[core * piece : (core + 1) * piece, :])
-        store(at(sender, above(place, sender, n_mp // 2, n_mp)), blocks[-1][...])
-
-
-def score_kernel(place, pair, *refs):
-    embed, weights, out, both = refs[-4:]
+                to = ((k - 1) * 2 + core) * piece
+                store(at(core, z), source[to : to + piece, :])
+        to = (n_mp - 2) * piece
+        store(at(sender, above(place, sender, n_mp // 2, n_mp)), source[to : to + piece, :])
+
+
+def score_kernel(place, pair, own, came, embed, weights, out, both):
     n_mp, piece = out.shape[0], out.shape[1] // 2
-    own, came = refs[: n_mp // 2], refs[n_mp // 2 : n_mp]
     width = embed.shape[1]
     half = n_mp * piece
     rows = 2 * half
@@ -227,12 +235,11 @@
         finish(uncond + GUIDANCE * (cond - uncond))
 
 
-def refresh_kernel(place, pair, *refs):
+def refresh_kernel(place, pair, own, came, *refs):
     embed, weights, normed_gen, active_own, active_came, preact_own, preact_came = refs[-10:-3]
     normed, preact, active = refs[-3:]
     piece = pair.shape[0] // 2
     n_mp = normed.shape[0] // (2 * piece)
-    own, came = refs[: n_mp // 2], refs[n_mp // 2 : n_mp]
     hidden = preact.shape[1]
 
     def store(at, value):
@@ -404,7 +411,7 @@
     def outgoing(models):
         lanes = hidden * len(models)
         blocks = [shape((4 * n_dp, row_piece, lanes), BF16)]
-        return call(lay_kernel, "lay", models, [], blocks, room=60)[0]
+        return call(lay_kernel, "lay", models, [], blocks)[0]
 
     def gather(blocks):
         return lax.all_to_all(blocks, PLANE, 0, 0, tiled=True).reshape(width, -1)
@@ -455,23 +462,25 @@
     came = [paired(block, k + 1) for k, block in enumerate(sent)]
     across = paired(across, n_mp // 2)
     both_f32 = shape((2 * piece, width), F32)
-    (sums,) = call(sums_kernel, "sums", [own, across] + came, [place], [both_f32], room=60)
+    (sums,) = call(sums_kernel, "sums", [own, across] + came, [place], [both_f32])
     latents, noised, noised_mine = call(
         latent_kernel,
         "latent",
         [sums, core_swap(sums), stream, scaled_noise],
         [place, scales],
         [both_f32, two, one],
-        room=60,
     )
     around = [paired(noised, k + 1) for k in range(steps)]
     around.append(paired(noised_mine, n_mp // 2))
-    around += [core_swap(block) for block in around]
+    (around,) = call(
+        order_kernel, "order", around, [], [shape(((2 * steps + 1) * piece, width), BF16)]
+    )
     score_weights, around = lax.optimization_barrier((score_weights, around))
+    around_other = core_swap(around)
     (score_parts,) = call(
         score_kernel,
         "score",
-        [noised] + around + [embedding, score_weights],
+        [noised, around, around_other, embedding, score_weights],
         [place],
         [shape((n_mp, 2 * piece, width + LANES), F32)],
         8 * work,
@@ -490,16 +499,13 @@
         [total, core_swap(total), latents, noised],
         [place],
         [shape((2 * piece, width + LANES), F32)],
-        room=60,
-    )
-
-    message, around = lax.optimization_barrier((message, around))
+    )
+
+    message, around, around_other = lax.optimization_barrier((message, around, around_other))
     normed, preact, active = call(
         refresh_kernel,
         "refresh",
-        [noised]
-        + around
-        + [embedding, score_weights, normed_gen]
+        [noised, around, around_other, embedding, score_weights, normed_gen]
         + [active_gen, core_swap(active_gen), preact_gen, core_swap(preact_gen)],
         [place],
         [

time: 217 us -> 206 us (0.949)
  Pallas kernels: 26.2 us -> 19.1 us
  waiting for transfers between devices: 42.2 us -> 49.2 us
  local copies, waits for them, and re-layouts: 16.2 us -> 10.9 us
  starting transfers between devices: 47.4 us -> 42.7 us
    pallas_call x13 -> x14, Pallas kernels: 26.2 us -> 19.1 us  [call(): pl.pallas_call(body, name=name, out_shape=outs, in_specs=[SMEM] * len(sca...]
    unnamed x94 -> x58, local copies, waits for them, and re-layouts: 14.1 us -> 8.75 us
    ppermute x10 -> x7, starting transfers between devices: 10.1 us -> 5.42 us  [core_swap(): return lax.ppermute(block, 'group', [(0, 1), (1, 0), (2, 3), (3, 2)])]
    ppermute x8, waiting for transfers between devices: 6.29 us -> 10.7 us  [paired(): return lax.ppermute(block, ('group', 'mp'), pairs)]
    all_to_all x1, blocking collectives: 25.4 us -> 29.5 us  [exchange(): lax.all_to_all(blocks.astype(jnp.float16), 'mp', 0, 0, tiled=True)]
    all_to_all x1, blocking collectives: 47.6 us -> 43.7 us  [local(): lax.all_to_all(grads.astype(jnp.float16), PLANE, 0, 0, axis_index_groups=...]
    ppermute x10 -> x7, waiting for transfers between devices: 7.23 us -> 8.16 us  [core_swap(): return lax.ppermute(block, 'group', [(0, 1), (1, 0), (2, 3), (3, 2)])]
  transfers between devices with their start and end apart: 21 -> 18, of which waited for: 9 -> 9; matrix products, arithmetic and copies ran while one was open for 3% -> 3% of each run, Pallas kernels for 6% -> 4%
where the time goes in v5:
time: 206 us
  blocking collectives  73.3 us (36%)
  waiting for transfers between devices  49.2 us (24%)
  starting transfers between devices  42.7 us (21%)
  Pallas kernels  19.1 us (9%)
  local copies, waits for them, and re-layouts  10.9 us (5%)
  other arithmetic  6.61 us (3%)
  between operations  3.91 us (2%)
    all_to_all x1, blocking collectives, local(): lax.all_to_all(grads.astype(jnp.float16), PLANE, 0, 0, axis_index_groups=...  43.7 us
    all_to_all x1, blocking collectives, exchange(): lax.all_to_all(blocks.astype(jnp.float16), 'mp', 0, 0, tiled=True)  29.5 us
    ppermute x8, starting transfers between devices, paired(): return lax.ppermute(block, ('group', 'mp'), pairs)  19.9 us
    pallas_call x14, Pallas kernels, call(): pl.pallas_call(body, name=name, out_shape=outs, in_specs=[SMEM] * len(sca...  19.1 us
    all_to_all x1, waiting for transfers between devices, exchange(): lax.all_to_all(blocks.astype(jnp.float16), 'mp', 0, 0, tiled=True)  15.7 us
    all_to_all x2, waiting for transfers between devices, gather(): return lax.all_to_all(blocks, PLANE, 0, 0, tiled=True).reshape(width, -1)  14.5 us
    all_to_all x2, starting transfers between devices, gather(): return lax.all_to_all(blocks, PLANE, 0, 0, tiled=True).reshape(width, -1)  13.2 us
    ppermute x8, waiting for transfers between devices, paired(): return lax.ppermute(block, ('group', 'mp'), pairs)  10.7 us
  transfers between devices with their start and end apart: 18, of which 9 were waited for; matrix products, arithmetic and copies ran while one was open for 3% of the time, Pallas kernels for 4%

profile of v5, /device:TPU:1, one launch (start us, length us, event | category | flops | bytes accessed | tf_op | source)
XLA Modules:
  0.0 205.7 jit_solution(289594481107178474)
XLA Ops:
  0.6 0.9 copy-done.21
  1.5 1.5 lay.2
  3.0 8.8 %all-to-all-start = ((bf16[32,40,640]{2,1,0:T(8,128)(2,1)}), bf16[32,40,640]{2,1,0:T(8,128)(2,1)}, u32[]{:S(2)}, u32[]{:S(2)}) async-start(bf16[32,40,640]{2,1,0:T(8,128)(2,1)} %lay.2), calls=%async_computation | async-start | bytes 3276800 | tf_op jit(solution)/shard_map/all_to_all | solution.py:417
  13.3 0.7 dynamic_slice.12
  16.5 1.6 copy-done
  18.3 0.7 dynamic-slice_convert_fusion.refs_4_.embed.refs_0_
  19.1 0.8 prepare.1
  19.9 0.8 copy-done.2
  20.7 0.7 copy-done.17
  21.4 14.5 %all-to-all-done = bf16[32,40,640]{2,1,0:T(8,128)(2,1)} async-done(((bf16[32,40,640]{2,1,0:T(8,128)(2,1)}), bf16[32,40,640]{2,1,0:T(8,128)(2,1)}, u32[]{:S(2)}, u32[]{:S(2)}) %all-to-all-start) | async-done | bytes 1638432 | tf_op jit(solution)/shard_map/all_to_all | solution.py:417
  35.9 4.4 %all-to-all-start.1 = ((bf16[32,40,1280]{2,1,0:T(8,128)(2,1)}), bf16[32,40,1280]{2,1,0:T(8,128)(2,1)S(1)}, u32[]{:S(2)}, u32[]{:S(2)}) async-start(bf16[32,40,1280]{2,1,0:T(8,128)(2,1)} %copy-done), calls=%async_computation.1 | async-start | bytes 6553600 | tf_op jit(solution)/shard_map/all_to_all | solution.py:417
  40.7 3.6 %collective-permute-done.other = bf16[1280,640]{1,0:T(8,128)(2,1)} collective-permute-done((bf16[1280,640]{1,0:T(8,128)(2,1)}, bf16[1280,640]{1,0:T(8,128)(2,1)}, u32[]{:S(2)}, u32[]{:S(2)}) %collective-permute-start) | collective-permute-done | bytes 1638432 | tf_op jit(solution)/shard_map/ppermute | solution.py:67
  44.3 4.0 %generate.1 = (f32[128,640]{1,0:T(8,128)}, bf16[128,640]{1,0:T(8,128)(2,1)}, bf16[16,1280]{1,0:T(8,128)(2,1)}, bf16[16,1280]{1,0:T(8,128)(2,1)}, bf16[32,1280]{1...) custom-call(s32[3]{0:T(128)} %copy-done.24, bf16[256,1280]{1,0:T(8,128)(2,1)} %copy-done.2, ...), custom_call_target="tpu_custom_call" | custom-call | flops 419430400 | bytes 4751360 | tf_op jit(solution)/shard_map/generate/pallas_call | solution.py:35
  48.3 5.6 %collective-permute-start.2 = (bf16[32,1280]{1,0:T(8,128)(2,1)}, bf16[32,1280]{1,0:T(8,128)(2,1)S(1)}, u32[]{:S(2)}, u32[]{:S(2)}) collective-permute-start(bf16[32,1280]{1,0:T(8,128)(2,1)} %get-tuple-element.42), channel_id=1, source_target_pairs={{0,1},{1,2},{2,3},{3,4},{4,5},{5,6},{6,7},{7,0},{64,71},{65,64},{6... | collective-permute-start | bytes 245768 | tf_op jit(solution)/shard_map/ppermute | solution.py:77
  53.9 1.2 collective-permute-start.3
  55.5 4.5 %collective-permute-start.1 = (bf16[16,1280]{1,0:T(8,128)(2,1)}, bf16[16,1280]{1,0:T(8,128)(2,1)S(1)}, u32[]{:S(2)}, u32[]{:S(2)}) collective-permute-start(bf16[16,1280]{1,0:T(8,128)(2,1)} %get-tuple-element.41), channel_id=1, source_target_pairs={{0,4},{1,5},{2,6},{3,7},{4,0},{5,1},{6,2},{7,3},{64,68},{65,69},{6... | collective-permute-start | bytes 122888 | tf_op jit(solution)/shard_map/ppermute | solution.py:77
  60.0 4.3 %collective-permute-done.1.across = bf16[16,1280]{1,0:T(8,128)(2,1)S(1)} collective-permute-done((bf16[16,1280]{1,0:T(8,128)(2,1)}, bf16[16,1280]{1,0:T(8,128)(2,1)S(1)}, u32[]{:S(2)}, u32[]{:S(2)}) %collective-permute-start.1) | collective-permute-done | bytes 40992 | tf_op jit(solution)/shard_map/ppermute | solution.py:77
  64.3 0.8 copy-done.26
  65.7 1.8 collective-permute-start.5
  67.5 1.0 collective-permute-done.5.came
  69.1 0.7 copy-done.19
  69.8 2.1 %collective-permute-start.8 = (bf16[32,1280]{1,0:T(8,128)(2,1)S(1)}, bf16[32,1280]{1,0:T(8,128)(2,1)S(1)}, u32[]{:S(2)}, u32[]{:S(2)}) collective-permute-start(bf16[32,1280]{1,0:T(8,128)(2,1)S(1)} %get-tuple-element.47.pair.refs_4_), channel_id=1, source_target_pairs={{0,3},{1,4},{2,5},{3,6},{4,7},{5,0},{6,1},{7,2},{64,69},{65,70},{6... | collective-permute-start | bytes 245768 | tf_op jit(solution)/shard_map/ppermute | solution.py:77
  71.8 1.2 collective-permute-start.7
  73.0 2.4 %collective-permute-start.6 = (bf16[32,1280]{1,0:T(8,128)(2,1)S(1)}, bf16[32,1280]{1,0:T(8,128)(2,1)S(1)}, u32[]{:S(2)}, u32[]{:S(2)}) collective-permute-start(bf16[32,1280]{1,0:T(8,128)(2,1)S(1)} %get-tuple-element.47.pair.refs_4_), channel_id=1, source_target_pairs={{0,1},{1,2},{2,3},{3,4},{4,5},{5,6},{6,7},{7,0},{64,71},{65,64},{6... | collective-permute-start | bytes 245768 | tf_op jit(solution)/shard_map/ppermute | solution.py:77
  75.5 2.5 %collective-permute-start.9 = (bf16[16,1280]{1,0:T(8,128)(2,1)S(1)}, bf16[16,1280]{1,0:T(8,128)(2,1)S(1)}, u32[]{:S(2)}, u32[]{:S(2)}) collective-permute-start(bf16[16,1280]{1,0:T(8,128)(2,1)S(1)} %get-tuple-element.49), channel_id=1, source_target_pairs={{0,4},{1,5},{2,6},{3,7},{4,0},{5,1},{6,2},{7,3},{64,68},{65,69},{6... | collective-permute-start | bytes 122888 | tf_op jit(solution)/shard_map/ppermute | solution.py:77
  77.9 6.5 %collective-permute-done.9.refs_3_ = bf16[16,1280]{1,0:T(8,128)(2,1)S(1)} collective-permute-done((bf16[16,1280]{1,0:T(8,128)(2,1)S(1)}, bf16[16,1280]{1,0:T(8,128)(2,1)S(1)}, u32[]{:S(2)}, u32[]{:S(2)}) %collective-permute-start.9) | collective-permute-done | bytes 40992 | tf_op jit(solution)/shard_map/ppermute | solution.py:77
  84.5 0.7 copy-done.6
  85.2 0.6 collective-permute-start.10
  85.8 1.4 collective-permute-done.10.came
  87.2 1.0 copy-done.7
  88.2 3.7 %score.1 = f32[8,32,1408]{2,1,0:T(8,128)S(1)} custom-call(s32[3]{0:T(128)S(1)} %copy-done.25, bf16[32,1280]{1,0:T(8,128)(2,1)S(1)} %get-tuple-element.47.pair.refs_4_, bf16[112,1280]{1,0:T(8,128)(2,1)S(1)} %copy-done.7, bf16[112,1280]{1,0:T(8,128)(2,1)S(1)} %collective-permute-done.10.came, f32[1,1280]{1,0:T(1,128)S(1)} %dynamic-slice_convert_fusion.refs_4_.embed.refs_0_, ...), custom_call_target="tpu_custom_call" | custom-call | flops 1677721600 | bytes 5379072 | tf_op jit(solution)/shard_map/score/pallas_call | solution.py:35
  92.0 29.5 %all_to_all.25 = f16[8,32,1408]{2,1,0:T(8,128)(2,1)S(1)} all-to-all(f16[8,32,1408]{2,1,0:T(8,128)(2,1)S(1)} %convert_element_type.28), channel_id=1, replica_groups=mesh['group'=4,'dp'=8,'mp'=8] {'mp'}, dimensions={0} | all-to-all | bytes 1441792 | tf_op jit(solution)/shard_map/all_to_all | solution.py:491
  122.4 1.0 collective-permute-done.11.refs_2_
  123.4 0.7 pack.1
  124.2 0.9 broadcast_in_dim.2
  125.1 4.2 %all-to-all-start.3 = ((f16[8,32,1408]{2,1,0:T(8,128)(2,1)}), f16[8,32,1408]{2,1,0:T(8,128)(2,1)}, u32[]{:S(2)}, u32[]{:S(2)}) async-start(f16[8,32,1408]{2,1,0:T(8,128)(2,1)} %broadcast_in_dim.2), calls=%async_computation.3 | async-start | bytes 1441792 | tf_op jit(solution)/shard_map/all_to_all | solution.py:491
  130.0 3.0 %slice_select_fusion.refs_2_ = bf16[1280,640]{1,0:T(8,128)(2,1)} fusion(bf16[1280,640]{1,0:T(8,128)(2,1)} %bitcast.3.mine, bf16[1280,1280]{1,0:T(8,128)(2,1)S(1)} %bitcast.7, pred[]{:T(512)S(6)} %eq.5), kind=kLoop, calls=%fused_computation | loop fusion | flops 819200 | bytes 4915201 | tf_op jit(solution)/shard_map/jit(_where)/select_n | solution.py:527
  133.1 0.7 refresh.1
  133.8 0.8 copy-done.9
  134.6 0.7 copy-done.12
  135.7 15.7 %all-to-all-done.3 = f16[8,32,1408]{2,1,0:T(8,128)(2,1)} async-done(((f16[8,32,1408]{2,1,0:T(8,128)(2,1)}), f16[8,32,1408]{2,1,0:T(8,128)(2,1)}, u32[]{:S(2)}, u32[]{:S(2)}) %all-to-all-start.3) | async-done | bytes 720928 | tf_op jit(solution)/shard_map/all_to_all | solution.py:491
  151.5 1.2 convert_element_type.31.refs_1_
  152.7 3.0 %grads.1 = f32[16,816,128]{2,1,0:T(8,128)S(1)} custom-call(s32[3]{0:T(128)S(1)} %copy-done.25, f32[8,32,1408]{2,1,0:T(8,128)S(1)} %convert_element_type.31.refs_1_, bf16[1280,640]{1,0:T(8,128)(2,1)S(1)} %copy-done.1, f32[256,640]{1,0:T(8,128)S(1)} %fusion.5.refs_3_, bf16[256,1280]{1,0:T(8,128)(2,1)S(1)} %copy-done.10, bf16[256,640]{1,0:T(8,128)(2,1)S(1)} %copy-done.13), custom_call_target="tpu_custom_call" | custom-call | flops 1258291200 | bytes 11403264 | tf_op jit(solution)/shard_map/grads/pallas_call | solution.py:35
  156.2 43.7 %all_to_all.26 = f16[16,816,128]{2,1,0:T(8,128)(2,1)S(1)} all-to-all(f16[16,816,128]{2,1,0:T(8,128)(2,1)S(1)} %convert_element_type.32), channel_id=1, replica_groups={{0,16,32,48,176,160,144,24,40,56,184,168,152,136,8,128},{64,80,96,112,2..., dimensions={0} | all-to-all | bytes 6684672 | tf_op jit(solution)/shard_map/all_to_all | solution.py:537
  200.3 1.2 collect.1
  201.5 1.5 collective-permute-start.14
  203.0 1.1 collective-permute-done.14.came
  204.1 1.5 place.1
  (76 shorter events, 6.1 us)
Async XLA Ops:
  0.6 0.9 copy-start.21
  3.0 8.8 %copy-start.27 = (s32[2]{0:T(128)S(1)}, s32[2]{0:T(128)}, u32[]{:S(2)}) copy-start(s32[2]{0:T(128)} %param.10) | copy-start | bytes 28
  3.0 10.2 %copy-start.28 = (s32[2]{0:T(128)S(1)}, s32[2]{0:T(128)}, u32[]{:S(2)}) copy-start(s32[2]{0:T(128)} %param.11) | copy-start | bytes 28
  3.0 13.0 %copy-start.22 = (bf16[40,2,640]{2,1,0:T(2,128)(2,1)S(1)}, bf16[40,2,640]{2,1,0:T(2,128)(2,1)}, u32[]{:S(2)}) copy-start(bf16[40,2,640]{2,1,0:T(2,128)(2,1)} %refs_0_.3) | copy-start | bytes 307204
  3.0 13.0 %copy-start.23 = (bf16[40,2,640]{2,1,0:T(2,128)(2,1)S(1)}, bf16[40,2,640]{2,1,0:T(2,128)(2,1)}, u32[]{:S(2)}) copy-start(bf16[40,2,640]{2,1,0:T(2,128)(2,1)} %refs_1_.1) | copy-start | bytes 307204
  3.0 32.9 %all-to-all-start = ((bf16[32,40,640]{2,1,0:T(8,128)(2,1)}), bf16[32,40,640]{2,1,0:T(8,128)(2,1)}, u32[]{:S(2)}, u32[]{:S(2)}) async-start(bf16[32,40,640]{2,1,0:T(8,128)(2,1)} %lay.2), calls=%async_computation | async-start | bytes 3276800 | tf_op jit(solution)/shard_map/all_to_all | solution.py:417
  16.0 3.1 %copy-start.4 = (bf16[2,256,1280]{2,1,0:T(8,128)(2,1)S(1)}, bf16[2,256,1280]{2,1,0:T(8,128)(2,1)}, u32[]{:S(2)}) copy-start(bf16[2,256,1280]{2,1,0:T(8,128)(2,1)} %refs_2_.1) | copy-start | bytes 3932164
  16.0 3.1 %copy-start.5 = (bf16[2,256,1280]{2,1,0:T(8,128)(2,1)S(1)}, bf16[2,256,1280]{2,1,0:T(8,128)(2,1)}, u32[]{:S(2)}) copy-start(bf16[2,256,1280]{2,1,0:T(8,128)(2,1)} %refs_3_.1) | copy-start | bytes 3932164
  16.5 1.7 copy-start
  18.3 17.6 %copy-start.24 = (s32[3]{0:T(128)}, s32[3]{0:T(128)S(1)}, u32[]{:S(2)}) copy-start(s32[3]{0:T(128)S(1)} %pad_add_fusion.refs_0_.place) | copy-start | bytes 40
  19.9 0.8 copy-start.2
  20.7 0.7 copy-start.17
  35.9 49.2 %all-to-all-start.1 = ((bf16[32,40,1280]{2,1,0:T(8,128)(2,1)}), bf16[32,40,1280]{2,1,0:T(8,128)(2,1)S(1)}, u32[]{:S(2)}, u32[]{:S(2)}) async-start(bf16[32,40,1280]{2,1,0:T(8,128)(2,1)} %copy-done), calls=%async_computation.1 | async-start | bytes 6553600 | tf_op jit(solution)/shard_map/all_to_all | solution.py:417
  40.4 23.9 %copy-start.25 = (s32[3]{0:T(128)S(1)}, s32[3]{0:T(128)}, u32[]{:S(2)}) copy-start(s32[3]{0:T(128)} %copy-done.24) | copy-start | bytes 40
  40.4 28.1 %copy-start.18 = (f32[32,1280]{1,0:T(8,128)S(1)}, f32[32,1280]{1,0:T(8,128)}, u32[]{:S(2)}) copy-start(f32[32,1280]{1,0:T(8,128)} %copy-done.17) | copy-start | bytes 491524
  40.4 3.9 %collective-permute-start = (bf16[1280,640]{1,0:T(8,128)(2,1)}, bf16[1280,640]{1,0:T(8,128)(2,1)}, u32[]{:S(2)}, u32[]{:S(2)}) collective-permute-start(bf16[1280,640]{1,0:T(8,128)(2,1)} %bitcast.3.mine), channel_id=1, source_target_pairs={{0,64},{64,0},{128,192},{192,128},{1,65},{65,1},{129,193},{193,129... | collective-permute-start | bytes 4915208 | tf_op jit(solution)/shard_map/ppermute | solution.py:67
  48.3 15.9 %collective-permute-start.2 = (bf16[32,1280]{1,0:T(8,128)(2,1)}, bf16[32,1280]{1,0:T(8,128)(2,1)S(1)}, u32[]{:S(2)}, u32[]{:S(2)}) collective-permute-start(bf16[32,1280]{1,0:T(8,128)(2,1)} %get-tuple-element.42), channel_id=1, source_target_pairs={{0,1},{1,2},{2,3},{3,4},{4,5},{5,6},{6,7},{7,0},{64,71},{65,64},{6... | collective-permute-start | bytes 245768 | tf_op jit(solution)/shard_map/ppermute | solution.py:77
  53.9 10.4 %collective-permute-start.3 = (bf16[32,1280]{1,0:T(8,128)(2,1)}, bf16[32,1280]{1,0:T(8,128)(2,1)S(1)}, u32[]{:S(2)}, u32[]{:S(2)}) collective-permute-start(bf16[32,1280]{1,0:T(8,128)(2,1)} %get-tuple-element.43), channel_id=1, source_target_pairs={{0,2},{1,3},{2,4},{3,5},{4,6},{5,7},{6,0},{7,1},{64,70},{65,71},{6... | collective-permute-start | bytes 245768 | tf_op jit(solution)/shard_map/ppermute | solution.py:77
  55.1 9.2 %collective-permute-start.4 = (bf16[32,1280]{1,0:T(8,128)(2,1)}, bf16[32,1280]{1,0:T(8,128)(2,1)S(1)}, u32[]{:S(2)}, u32[]{:S(2)}) collective-permute-start(bf16[32,1280]{1,0:T(8,128)(2,1)} %get-tuple-element.44), channel_id=1, source_target_pairs={{0,3},{1,4},{2,5},{3,6},{4,7},{5,0},{6,1},{7,2},{64,69},{65,70},{6... | collective-permute-start | bytes 245768 | tf_op jit(solution)/shard_map/ppermute | solution.py:77
  55.5 8.7 %collective-permute-start.1 = (bf16[16,1280]{1,0:T(8,128)(2,1)}, bf16[16,1280]{1,0:T(8,128)(2,1)S(1)}, u32[]{:S(2)}, u32[]{:S(2)}) collective-permute-start(bf16[16,1280]{1,0:T(8,128)(2,1)} %get-tuple-element.41), channel_id=1, source_target_pairs={{0,4},{1,5},{2,6},{3,7},{4,0},{5,1},{6,2},{7,3},{64,68},{65,69},{6... | collective-permute-start | bytes 122888 | tf_op jit(solution)/shard_map/ppermute | solution.py:77
  64.3 0.8 copy-start.26
  65.7 2.8 %collective-permute-start.5 = (f32[32,1280]{1,0:T(8,128)S(1)}, f32[32,1280]{1,0:T(8,128)S(1)}, u32[]{:S(2)}, u32[]{:S(2)}) collective-permute-start(f32[32,1280]{1,0:T(8,128)S(1)} %sums.1), channel_id=1, source_target_pairs={{0,64},{64,0},{128,192},{192,128},{1,65},{65,1},{129,193},{193,129... | collective-permute-start | bytes 491528 | tf_op jit(solution)/shard_map/ppermute | solution.py:67
  69.1 0.7 copy-start.19
  69.8 14.7 %collective-permute-start.8 = (bf16[32,1280]{1,0:T(8,128)(2,1)S(1)}, bf16[32,1280]{1,0:T(8,128)(2,1)S(1)}, u32[]{:S(2)}, u32[]{:S(2)}) collective-permute-start(bf16[32,1280]{1,0:T(8,128)(2,1)S(1)} %get-tuple-element.47.pair.refs_4_), channel_id=1, source_target_pairs={{0,3},{1,4},{2,5},{3,6},{4,7},{5,0},{6,1},{7,2},{64,69},{65,70},{6... | collective-permute-start | bytes 245768 | tf_op jit(solution)/shard_map/ppermute | solution.py:77
  71.8 12.6 %collective-permute-start.7 = (bf16[32,1280]{1,0:T(8,128)(2,1)S(1)}, bf16[32,1280]{1,0:T(8,128)(2,1)S(1)}, u32[]{:S(2)}, u32[]{:S(2)}) collective-permute-start(bf16[32,1280]{1,0:T(8,128)(2,1)S(1)} %get-tuple-element.47.pair.refs_4_), channel_id=1, source_target_pairs={{0,2},{1,3},{2,4},{3,5},{4,6},{5,7},{6,0},{7,1},{64,70},{65,71},{6... | collective-permute-start | bytes 245768 | tf_op jit(solution)/shard_map/ppermute | solution.py:77
  73.0 11.4 %collective-permute-start.6 = (bf16[32,1280]{1,0:T(8,128)(2,1)S(1)}, bf16[32,1280]{1,0:T(8,128)(2,1)S(1)}, u32[]{:S(2)}, u32[]{:S(2)}) collective-permute-start(bf16[32,1280]{1,0:T(8,128)(2,1)S(1)} %get-tuple-element.47.pair.refs_4_), channel_id=1, source_target_pairs={{0,1},{1,2},{2,3},{3,4},{4,5},{5,6},{6,7},{7,0},{64,71},{65,64},{6... | collective-permute-start | bytes 245768 | tf_op jit(solution)/shard_map/ppermute | solution.py:77
  75.5 9.0 %collective-permute-start.9 = (bf16[16,1280]{1,0:T(8,128)(2,1)S(1)}, bf16[16,1280]{1,0:T(8,128)(2,1)S(1)}, u32[]{:S(2)}, u32[]{:S(2)}) collective-permute-start(bf16[16,1280]{1,0:T(8,128)(2,1)S(1)} %get-tuple-element.49), channel_id=1, source_target_pairs={{0,4},{1,5},{2,6},{3,7},{4,0},{5,1},{6,2},{7,3},{64,68},{65,69},{6... | collective-permute-start | bytes 122888 | tf_op jit(solution)/shard_map/ppermute | solution.py:77
  84.5 0.7 copy-start.6
  85.2 2.0 collective-permute-start.10
  87.2 1.0 copy-start.7
  88.2 3.7 %copy-start.14 = (bf16[112,1280]{1,0:T(8,128)(2,1)}, bf16[112,1280]{1,0:T(8,128)(2,1)S(1)}, u32[]{:S(2)}) copy-start(bf16[112,1280]{1,0:T(8,128)(2,1)S(1)} %collective-permute-done.10.came) | copy-start | bytes 860164
  121.5 1.8 copy-start.20
  121.9 1.5 collective-permute-start.11
  123.4 5.9 %copy-start.16 = (bf16[128,640]{1,0:T(8,128)(2,1)S(1)}, bf16[128,640]{1,0:T(8,128)(2,1)}, u32[]{:S(2)}) copy-start(bf16[128,640]{1,0:T(8,128)(2,1)} %get-tuple-element.57.refs_3_) | copy-start | bytes 491524
  125.1 26.4 %all-to-all-start.3 = ((f16[8,32,1408]{2,1,0:T(8,128)(2,1)}), f16[8,32,1408]{2,1,0:T(8,128)(2,1)}, u32[]{:S(2)}, u32[]{:S(2)}) async-start(f16[8,32,1408]{2,1,0:T(8,128)(2,1)} %broadcast_in_dim.2), calls=%async_computation.3 | async-start | bytes 1441792 | tf_op jit(solution)/shard_map/all_to_all | solution.py:491
  129.3 3.7 %collective-permute-start.12 = (bf16[128,640]{1,0:T(8,128)(2,1)S(1)}, bf16[128,640]{1,0:T(8,128)(2,1)S(1)}, u32[]{:S(2)}, u32[]{:S(2)}) collective-permute-start(bf16[128,640]{1,0:T(8,128)(2,1)S(1)} %copy-done.16), channel_id=1, source_target_pairs={{0,64},{64,0},{128,192},{192,128},{1,65},{65,1},{129,193},{193,129... | collective-permute-start | bytes 491528 | tf_op jit(solution)/shard_map/ppermute | solution.py:67
  129.7 3.3 %copy-start.3 = (bf16[256,1280]{1,0:T(8,128)(2,1)S(1)}, bf16[256,1280]{1,0:T(8,128)(2,1)}, u32[]{:S(2)}) copy-start(bf16[256,1280]{1,0:T(8,128)(2,1)} %copy-done.2) | copy-start | bytes 1966084
  129.8 3.3 %copy-start.8 = (bf16[112,1280]{1,0:T(8,128)(2,1)S(1)}, bf16[112,1280]{1,0:T(8,128)(2,1)}, u32[]{:S(2)}) copy-start(bf16[112,1280]{1,0:T(8,128)(2,1)} %copy-done.6) | copy-start | bytes 860164
  129.8 3.3 %copy-start.11 = (f32[128,640]{1,0:T(8,128)S(1)}, f32[128,640]{1,0:T(8,128)}, u32[]{:S(2)}) copy-start(f32[128,640]{1,0:T(8,128)} %get-tuple-element.58.refs_5_) | copy-start | bytes 983044
  129.8 3.3 %copy-start.15 = (bf16[112,1280]{1,0:T(8,128)(2,1)S(1)}, bf16[112,1280]{1,0:T(8,128)(2,1)}, u32[]{:S(2)}) copy-start(bf16[112,1280]{1,0:T(8,128)(2,1)} %copy-done.14) | copy-start | bytes 860164
  129.8 3.3 %collective-permute-start.13 = (f32[128,640]{1,0:T(8,128)}, f32[128,640]{1,0:T(8,128)S(1)}, u32[]{:S(2)}, u32[]{:S(2)}) collective-permute-start(f32[128,640]{1,0:T(8,128)} %get-tuple-element.58.refs_5_), channel_id=1, source_target_pairs={{0,64},{64,0},{128,192},{192,128},{1,65},{65,1},{129,193},{193,129... | collective-permute-start | bytes 983048 | tf_op jit(solution)/shard_map/ppermute | solution.py:67
  133.8 0.8 copy-start.9
  134.6 0.7 copy-start.12
  135.3 17.4 %copy-start.1 = (bf16[1280,640]{1,0:T(8,128)(2,1)S(1)}, bf16[1280,640]{1,0:T(8,128)(2,1)}, u32[]{:S(2)}) copy-start(bf16[1280,640]{1,0:T(8,128)(2,1)} %slice_select_fusion.refs_2_) | copy-start | bytes 4915204
  135.3 17.4 %copy-start.10 = (bf16[256,1280]{1,0:T(8,128)(2,1)S(1)}, bf16[256,1280]{1,0:T(8,128)(2,1)}, u32[]{:S(2)}) copy-start(bf16[256,1280]{1,0:T(8,128)(2,1)} %copy-done.9) | copy-start | bytes 1966084
  135.3 17.4 %copy-start.13 = (bf16[256,640]{1,0:T(8,128)(2,1)S(1)}, bf16[256,640]{1,0:T(8,128)(2,1)}, u32[]{:S(2)}) copy-start(bf16[256,640]{1,0:T(8,128)(2,1)} %copy-done.12) | copy-start | bytes 983044
  201.5 2.6 %collective-permute-start.14 = (f32[400,128]{1,0:T(8,128)S(1)}, f32[400,128]{1,0:T(8,128)S(1)}, u32[]{:S(2)}, u32[]{:S(2)}) collective-permute-start(f32[400,128]{1,0:T(8,128)S(1)} %get-tuple-element.63), channel_id=1, source_target_pairs={{0,64},{64,0},{128,192},{192,128},{1,65},{65,1},{129,193},{193,129... | collective-permute-start | bytes 614408 | tf_op jit(solution)/shard_map/ppermute | solution.py:67

commit v6 on v5

--- a/solution.py
+++ b/solution.py
@@ -475,8 +475,8 @@
     (around,) = call(
         order_kernel, "order", around, [], [shape(((2 * steps + 1) * piece, width), BF16)]
     )
-    score_weights, around = lax.optimization_barrier((score_weights, around))
     around_other = core_swap(around)
+    score_weights, around_other = lax.optimization_barrier((score_weights, around_other))
     (score_parts,) = call(
         score_kernel,
         "score",

time: 206 us -> 207 us (level)
    unnamed x58 -> x60, local copies, waits for them, and re-layouts: 8.75 us -> 9.78 us
where the time goes in v6:
time: 207 us; the launch traced here: 206 us
  blocking collectives  73 us (35%)
  waiting for transfers between devices  48.7 us (24%)
  starting transfers between devices  43 us (21%)
  Pallas kernels  19.1 us (9%)
  local copies, waits for them, and re-layouts  11.9 us (6%)
  other arithmetic  6.63 us (3%)
  between operations  3.53 us (2%)
    all_to_all x1, blocking collectives, local(): lax.all_to_all(grads.astype(jnp.float16), PLANE, 0, 0, axis_index_groups=...  44.9 us
    all_to_all x1, blocking collectives, exchange(): lax.all_to_all(blocks.astype(jnp.float16), 'mp', 0, 0, tiled=True)  28.1 us
    ppermute x8, starting transfers between devices, paired(): return lax.ppermute(block, ('group', 'mp'), pairs)  19.9 us
    pallas_call x14, Pallas kernels, call(): pl.pallas_call(body, name=name, out_shape=outs, in_specs=[SMEM] * len(sca...  19.1 us
    all_to_all x1, waiting for transfers between devices, exchange(): lax.all_to_all(blocks.astype(jnp.float16), 'mp', 0, 0, tiled=True)  15.7 us
    all_to_all x2, waiting for transfers between devices, gather(): return lax.all_to_all(blocks, PLANE, 0, 0, tiled=True).reshape(width, -1)  15 us
    all_to_all x2, starting transfers between devices, gather(): return lax.all_to_all(blocks, PLANE, 0, 0, tiled=True).reshape(width, -1)  13.2 us
    ppermute x8, waiting for transfers between devices, paired(): return lax.ppermute(block, ('group', 'mp'), pairs)  10.7 us
  transfers between devices with their start and end apart: 18, of which 9 were waited for; matrix products, arithmetic and copies ran while one was open for 3% of the time, Pallas kernels for 4%

profile of v6, /device:TPU:1, one launch (start us, length us, event | category | flops | bytes accessed | tf_op | source)
XLA Modules:
  0.0 205.8 jit_solution(7633748184452093929)
XLA Ops:
  0.6 0.9 copy-done.22
  1.5 1.5 lay.2
  3.0 8.8 %all-to-all-start = ((bf16[32,40,640]{2,1,0:T(8,128)(2,1)}), bf16[32,40,640]{2,1,0:T(8,128)(2,1)}, u32[]{:S(2)}, u32[]{:S(2)}) async-start(bf16[32,40,640]{2,1,0:T(8,128)(2,1)} %lay.2), calls=%async_computation | async-start | bytes 3276800 | tf_op jit(solution)/shard_map/all_to_all | solution.py:417
  16.1 1.7 copy-done
  17.9 0.7 dynamic-slice_convert_fusion.refs_4_.embed.refs_0_
  18.7 0.8 prepare.1
  19.5 0.8 copy-done.2
  20.3 0.7 copy-done.18
  21.0 15.0 %all-to-all-done = bf16[32,40,640]{2,1,0:T(8,128)(2,1)} async-done(((bf16[32,40,640]{2,1,0:T(8,128)(2,1)}), bf16[32,40,640]{2,1,0:T(8,128)(2,1)}, u32[]{:S(2)}, u32[]{:S(2)}) %all-to-all-start) | async-done | bytes 1638432 | tf_op jit(solution)/shard_map/all_to_all | solution.py:417
  35.9 4.4 %all-to-all-start.1 = ((bf16[32,40,1280]{2,1,0:T(8,128)(2,1)}), bf16[32,40,1280]{2,1,0:T(8,128)(2,1)S(1)}, u32[]{:S(2)}, u32[]{:S(2)}) async-start(bf16[32,40,1280]{2,1,0:T(8,128)(2,1)} %copy-done), calls=%async_computation.1 | async-start | bytes 6553600 | tf_op jit(solution)/shard_map/all_to_all | solution.py:417
  40.7 3.6 %collective-permute-done.other = bf16[1280,640]{1,0:T(8,128)(2,1)} collective-permute-done((bf16[1280,640]{1,0:T(8,128)(2,1)}, bf16[1280,640]{1,0:T(8,128)(2,1)}, u32[]{:S(2)}, u32[]{:S(2)}) %collective-permute-start) | collective-permute-done | bytes 1638432 | tf_op jit(solution)/shard_map/ppermute | solution.py:67
  44.3 4.0 %generate.1 = (f32[128,640]{1,0:T(8,128)}, bf16[128,640]{1,0:T(8,128)(2,1)}, bf16[16,1280]{1,0:T(8,128)(2,1)}, bf16[16,1280]{1,0:T(8,128)(2,1)}, bf16[32,1280]{1...) custom-call(s32[3]{0:T(128)} %copy-done.25, bf16[256,1280]{1,0:T(8,128)(2,1)} %copy-done.2, ...), custom_call_target="tpu_custom_call" | custom-call | flops 419430400 | bytes 4751360 | tf_op jit(solution)/shard_map/generate/pallas_call | solution.py:35
  48.3 5.6 %collective-permute-start.2 = (bf16[32,1280]{1,0:T(8,128)(2,1)}, bf16[32,1280]{1,0:T(8,128)(2,1)S(1)}, u32[]{:S(2)}, u32[]{:S(2)}) collective-permute-start(bf16[32,1280]{1,0:T(8,128)(2,1)} %get-tuple-element.42), channel_id=1, source_target_pairs={{0,1},{1,2},{2,3},{3,4},{4,5},{5,6},{6,7},{7,0},{64,71},{65,64},{6... | collective-permute-start | bytes 245768 | tf_op jit(solution)/shard_map/ppermute | solution.py:77
  53.9 1.2 collective-permute-start.3
  55.5 4.5 %collective-permute-start.1 = (bf16[16,1280]{1,0:T(8,128)(2,1)}, bf16[16,1280]{1,0:T(8,128)(2,1)S(1)}, u32[]{:S(2)}, u32[]{:S(2)}) collective-permute-start(bf16[16,1280]{1,0:T(8,128)(2,1)} %get-tuple-element.41), channel_id=1, source_target_pairs={{0,4},{1,5},{2,6},{3,7},{4,0},{5,1},{6,2},{7,3},{64,68},{65,69},{6... | collective-permute-start | bytes 122888 | tf_op jit(solution)/shard_map/ppermute | solution.py:77
  60.0 4.3 %collective-permute-done.1.across = bf16[16,1280]{1,0:T(8,128)(2,1)S(1)} collective-permute-done((bf16[16,1280]{1,0:T(8,128)(2,1)}, bf16[16,1280]{1,0:T(8,128)(2,1)S(1)}, u32[]{:S(2)}, u32[]{:S(2)}) %collective-permute-start.1) | collective-permute-done | bytes 40992 | tf_op jit(solution)/shard_map/ppermute | solution.py:77
  64.3 0.8 copy-done.27
  65.7 1.8 collective-permute-start.5
  67.5 1.0 collective-permute-done.5.came
  68.5 0.6 latent.1
  69.1 2.2 %collective-permute-start.8 = (bf16[32,1280]{1,0:T(8,128)(2,1)S(1)}, bf16[32,1280]{1,0:T(8,128)(2,1)S(1)}, u32[]{:S(2)}, u32[]{:S(2)}) collective-permute-start(bf16[32,1280]{1,0:T(8,128)(2,1)S(1)} %get-tuple-element.47.pair.refs_4_), channel_id=1, source_target_pairs={{0,3},{1,4},{2,5},{3,6},{4,7},{5,0},{6,1},{7,2},{64,69},{65,70},{6... | collective-permute-start | bytes 245768 | tf_op jit(solution)/shard_map/ppermute | solution.py:77
  71.3 1.2 collective-permute-start.7
  72.4 2.4 %collective-permute-start.6 = (bf16[32,1280]{1,0:T(8,128)(2,1)S(1)}, bf16[32,1280]{1,0:T(8,128)(2,1)S(1)}, u32[]{:S(2)}, u32[]{:S(2)}) collective-permute-start(bf16[32,1280]{1,0:T(8,128)(2,1)S(1)} %get-tuple-element.47.pair.refs_4_), channel_id=1, source_target_pairs={{0,1},{1,2},{2,3},{3,4},{4,5},{5,6},{6,7},{7,0},{64,71},{65,64},{6... | collective-permute-start | bytes 245768 | tf_op jit(solution)/shard_map/ppermute | solution.py:77
  74.9 2.5 %collective-permute-start.9 = (bf16[16,1280]{1,0:T(8,128)(2,1)S(1)}, bf16[16,1280]{1,0:T(8,128)(2,1)S(1)}, u32[]{:S(2)}, u32[]{:S(2)}) collective-permute-start(bf16[16,1280]{1,0:T(8,128)(2,1)S(1)} %get-tuple-element.48), channel_id=1, source_target_pairs={{0,4},{1,5},{2,6},{3,7},{4,0},{5,1},{6,2},{7,3},{64,68},{65,69},{6... | collective-permute-start | bytes 122888 | tf_op jit(solution)/shard_map/ppermute | solution.py:77
  77.4 6.5 %collective-permute-done.9.refs_3_ = bf16[16,1280]{1,0:T(8,128)(2,1)S(1)} collective-permute-done((bf16[16,1280]{1,0:T(8,128)(2,1)S(1)}, bf16[16,1280]{1,0:T(8,128)(2,1)S(1)}, u32[]{:S(2)}, u32[]{:S(2)}) %collective-permute-start.9) | collective-permute-done | bytes 40992 | tf_op jit(solution)/shard_map/ppermute | solution.py:77
  83.9 0.7 collective-permute-start.10
  84.6 0.7 copy-done.6
  85.8 0.7 copy-done.14
  86.5 1.0 copy-done.7
  87.5 1.0 copy-done.15
  88.4 3.7 %score.1 = f32[8,32,1408]{2,1,0:T(8,128)S(1)} custom-call(s32[3]{0:T(128)S(1)} %copy-done.26, bf16[32,1280]{1,0:T(8,128)(2,1)S(1)} %get-tuple-element.47.pair.refs_4_, bf16[112,1280]{1,0:T(8,128)(2,1)S(1)} %copy-done.7, bf16[112,1280]{1,0:T(8,128)(2,1)S(1)} %copy-done.15, f32[1,1280]{1,0:T(1,128)S(1)} %dynamic-slice_convert_fusion.refs_4_.embed.refs_0_, ...), custom_call_target="tpu_custom_call" | custom-call | flops 1677721600 | bytes 5379072 | tf_op jit(solution)/shard_map/score/pallas_call | solution.py:35
  92.3 28.1 %all_to_all.25 = f16[8,32,1408]{2,1,0:T(8,128)(2,1)S(1)} all-to-all(f16[8,32,1408]{2,1,0:T(8,128)(2,1)S(1)} %convert_element_type.28), channel_id=1, replica_groups=mesh['group'=4,'dp'=8,'mp'=8] {'mp'}, dimensions={0} | all-to-all | bytes 1441792 | tf_op jit(solution)/shard_map/all_to_all | solution.py:491
  121.2 1.0 collective-permute-done.11.refs_2_
  122.3 0.7 pack.1
  123.0 0.9 broadcast_in_dim.2
  123.9 4.2 %all-to-all-start.3 = ((f16[8,32,1408]{2,1,0:T(8,128)(2,1)}), f16[8,32,1408]{2,1,0:T(8,128)(2,1)}, u32[]{:S(2)}, u32[]{:S(2)}) async-start(f16[8,32,1408]{2,1,0:T(8,128)(2,1)} %broadcast_in_dim.2), calls=%async_computation.3 | async-start | bytes 1441792 | tf_op jit(solution)/shard_map/all_to_all | solution.py:491
  128.9 3.1 %slice_select_fusion.refs_2_ = bf16[1280,640]{1,0:T(8,128)(2,1)} fusion(bf16[1280,640]{1,0:T(8,128)(2,1)} %bitcast.3.mine, bf16[1280,1280]{1,0:T(8,128)(2,1)S(1)} %bitcast.7, pred[]{:T(512)S(6)} %eq.5), kind=kLoop, calls=%fused_computation | loop fusion | flops 819200 | bytes 4915201 | tf_op jit(solution)/shard_map/jit(_where)/select_n | solution.py:527
  132.0 0.7 refresh.1
  132.7 0.8 copy-done.9
  133.5 0.7 copy-done.12
  134.6 15.7 %all-to-all-done.3 = f16[8,32,1408]{2,1,0:T(8,128)(2,1)} async-done(((f16[8,32,1408]{2,1,0:T(8,128)(2,1)}), f16[8,32,1408]{2,1,0:T(8,128)(2,1)}, u32[]{:S(2)}, u32[]{:S(2)}) %all-to-all-start.3) | async-done | bytes 720928 | tf_op jit(solution)/shard_map/all_to_all | solution.py:491
  150.3 1.2 convert_element_type.31.refs_1_
  151.6 3.0 %grads.1 = f32[16,816,128]{2,1,0:T(8,128)S(1)} custom-call(s32[3]{0:T(128)S(1)} %copy-done.26, f32[8,32,1408]{2,1,0:T(8,128)S(1)} %convert_element_type.31.refs_1_, bf16[1280,640]{1,0:T(8,128)(2,1)S(1)} %copy-done.1, f32[256,640]{1,0:T(8,128)S(1)} %fusion.5.refs_3_, bf16[256,1280]{1,0:T(8,128)(2,1)S(1)} %copy-done.10, bf16[256,640]{1,0:T(8,128)(2,1)S(1)} %copy-done.13), custom_call_target="tpu_custom_call" | custom-call | flops 1258291200 | bytes 11403264 | tf_op jit(solution)/shard_map/grads/pallas_call | solution.py:35
  155.0 44.9 %all_to_all.26 = f16[16,816,128]{2,1,0:T(8,128)(2,1)S(1)} all-to-all(f16[16,816,128]{2,1,0:T(8,128)(2,1)S(1)} %convert_element_type.32), channel_id=1, replica_groups={{0,16,32,48,176,160,144,24,40,56,184,168,152,136,8,128},{64,80,96,112,2..., dimensions={0} | all-to-all | bytes 6684672 | tf_op jit(solution)/shard_map/all_to_all | solution.py:537
  200.3 1.2 collect.1
  201.5 1.7 collective-permute-start.14
  203.2 1.1 collective-permute-done.14.came
  204.3 1.5 place.1
  (78 shorter events, 6.6 us)
Async XLA Ops:
  0.6 0.9 copy-start.22
  3.0 8.8 %copy-start.28 = (s32[2]{0:T(128)S(1)}, s32[2]{0:T(128)}, u32[]{:S(2)}) copy-start(s32[2]{0:T(128)} %param.10) | copy-start | bytes 28
  3.0 10.2 %copy-start.29 = (s32[2]{0:T(128)S(1)}, s32[2]{0:T(128)}, u32[]{:S(2)}) copy-start(s32[2]{0:T(128)} %param.11) | copy-start | bytes 28
  3.0 12.5 %copy-start.23 = (bf16[40,2,640]{2,1,0:T(2,128)(2,1)S(1)}, bf16[40,2,640]{2,1,0:T(2,128)(2,1)}, u32[]{:S(2)}) copy-start(bf16[40,2,640]{2,1,0:T(2,128)(2,1)} %refs_0_.3) | copy-start | bytes 307204
  3.0 12.5 %copy-start.24 = (bf16[40,2,640]{2,1,0:T(2,128)(2,1)S(1)}, bf16[40,2,640]{2,1,0:T(2,128)(2,1)}, u32[]{:S(2)}) copy-start(bf16[40,2,640]{2,1,0:T(2,128)(2,1)} %refs_1_.1) | copy-start | bytes 307204
  3.0 32.9 %all-to-all-start = ((bf16[32,40,640]{2,1,0:T(8,128)(2,1)}), bf16[32,40,640]{2,1,0:T(8,128)(2,1)}, u32[]{:S(2)}, u32[]{:S(2)}) async-start(bf16[32,40,640]{2,1,0:T(8,128)(2,1)} %lay.2), calls=%async_computation | async-start | bytes 3276800 | tf_op jit(solution)/shard_map/all_to_all | solution.py:417
  15.6 3.1 %copy-start.4 = (bf16[2,256,1280]{2,1,0:T(8,128)(2,1)S(1)}, bf16[2,256,1280]{2,1,0:T(8,128)(2,1)}, u32[]{:S(2)}) copy-start(bf16[2,256,1280]{2,1,0:T(8,128)(2,1)} %refs_2_.1) | copy-start | bytes 3932164
  15.6 3.1 %copy-start.5 = (bf16[2,256,1280]{2,1,0:T(8,128)(2,1)S(1)}, bf16[2,256,1280]{2,1,0:T(8,128)(2,1)}, u32[]{:S(2)}) copy-start(bf16[2,256,1280]{2,1,0:T(8,128)(2,1)} %refs_3_.1) | copy-start | bytes 3932164
  16.1 1.7 copy-start
  17.9 18.1 %copy-start.25 = (s32[3]{0:T(128)}, s32[3]{0:T(128)S(1)}, u32[]{:S(2)}) copy-start(s32[3]{0:T(128)S(1)} %pad_add_fusion.refs_0_.place) | copy-start | bytes 40
  19.5 0.8 copy-start.2
  20.3 0.7 copy-start.18
  35.9 50.6 %all-to-all-start.1 = ((bf16[32,40,1280]{2,1,0:T(8,128)(2,1)}), bf16[32,40,1280]{2,1,0:T(8,128)(2,1)S(1)}, u32[]{:S(2)}, u32[]{:S(2)}) async-start(bf16[32,40,1280]{2,1,0:T(8,128)(2,1)} %copy-done), calls=%async_computation.1 | async-start | bytes 6553600 | tf_op jit(solution)/shard_map/all_to_all | solution.py:417
  40.4 23.9 %copy-start.26 = (s32[3]{0:T(128)S(1)}, s32[3]{0:T(128)}, u32[]{:S(2)}) copy-start(s32[3]{0:T(128)} %copy-done.25) | copy-start | bytes 40
  40.4 28.1 %copy-start.19 = (f32[32,1280]{1,0:T(8,128)S(1)}, f32[32,1280]{1,0:T(8,128)}, u32[]{:S(2)}) copy-start(f32[32,1280]{1,0:T(8,128)} %copy-done.18) | copy-start | bytes 491524
  40.4 3.9 %collective-permute-start = (bf16[1280,640]{1,0:T(8,128)(2,1)}, bf16[1280,640]{1,0:T(8,128)(2,1)}, u32[]{:S(2)}, u32[]{:S(2)}) collective-permute-start(bf16[1280,640]{1,0:T(8,128)(2,1)} %bitcast.3.mine), channel_id=1, source_target_pairs={{0,64},{64,0},{128,192},{192,128},{1,65},{65,1},{129,193},{193,129... | collective-permute-start | bytes 4915208 | tf_op jit(solution)/shard_map/ppermute | solution.py:67
  48.3 15.9 %collective-permute-start.2 = (bf16[32,1280]{1,0:T(8,128)(2,1)}, bf16[32,1280]{1,0:T(8,128)(2,1)S(1)}, u32[]{:S(2)}, u32[]{:S(2)}) collective-permute-start(bf16[32,1280]{1,0:T(8,128)(2,1)} %get-tuple-element.42), channel_id=1, source_target_pairs={{0,1},{1,2},{2,3},{3,4},{4,5},{5,6},{6,7},{7,0},{64,71},{65,64},{6... | collective-permute-start | bytes 245768 | tf_op jit(solution)/shard_map/ppermute | solution.py:77
  53.9 10.4 %collective-permute-start.3 = (bf16[32,1280]{1,0:T(8,128)(2,1)}, bf16[32,1280]{1,0:T(8,128)(2,1)S(1)}, u32[]{:S(2)}, u32[]{:S(2)}) collective-permute-start(bf16[32,1280]{1,0:T(8,128)(2,1)} %get-tuple-element.43), channel_id=1, source_target_pairs={{0,2},{1,3},{2,4},{3,5},{4,6},{5,7},{6,0},{7,1},{64,70},{65,71},{6... | collective-permute-start | bytes 245768 | tf_op jit(solution)/shard_map/ppermute | solution.py:77
  55.1 9.2 %collective-permute-start.4 = (bf16[32,1280]{1,0:T(8,128)(2,1)}, bf16[32,1280]{1,0:T(8,128)(2,1)S(1)}, u32[]{:S(2)}, u32[]{:S(2)}) collective-permute-start(bf16[32,1280]{1,0:T(8,128)(2,1)} %get-tuple-element.44), channel_id=1, source_target_pairs={{0,3},{1,4},{2,5},{3,6},{4,7},{5,0},{6,1},{7,2},{64,69},{65,70},{6... | collective-permute-start | bytes 245768 | tf_op jit(solution)/shard_map/ppermute | solution.py:77
  55.5 8.8 %collective-permute-start.1 = (bf16[16,1280]{1,0:T(8,128)(2,1)}, bf16[16,1280]{1,0:T(8,128)(2,1)S(1)}, u32[]{:S(2)}, u32[]{:S(2)}) collective-permute-start(bf16[16,1280]{1,0:T(8,128)(2,1)} %get-tuple-element.41), channel_id=1, source_target_pairs={{0,4},{1,5},{2,6},{3,7},{4,0},{5,1},{6,2},{7,3},{64,68},{65,69},{6... | collective-permute-start | bytes 122888 | tf_op jit(solution)/shard_map/ppermute | solution.py:77
  64.3 0.8 copy-start.27
  65.7 2.8 %collective-permute-start.5 = (f32[32,1280]{1,0:T(8,128)S(1)}, f32[32,1280]{1,0:T(8,128)S(1)}, u32[]{:S(2)}, u32[]{:S(2)}) collective-permute-start(f32[32,1280]{1,0:T(8,128)S(1)} %sums.1), channel_id=1, source_target_pairs={{0,64},{64,0},{128,192},{192,128},{1,65},{65,1},{129,193},{193,129... | collective-permute-start | bytes 491528 | tf_op jit(solution)/shard_map/ppermute | solution.py:67
  69.1 15.5 %copy-start.20 = (f32[32,1280]{1,0:T(8,128)}, f32[32,1280]{1,0:T(8,128)S(1)}, u32[]{:S(2)}) copy-start(f32[32,1280]{1,0:T(8,128)S(1)} %get-tuple-element.53.refs_3_) | copy-start | bytes 491524
  69.1 14.7 %collective-permute-start.8 = (bf16[32,1280]{1,0:T(8,128)(2,1)S(1)}, bf16[32,1280]{1,0:T(8,128)(2,1)S(1)}, u32[]{:S(2)}, u32[]{:S(2)}) collective-permute-start(bf16[32,1280]{1,0:T(8,128)(2,1)S(1)} %get-tuple-element.47.pair.refs_4_), channel_id=1, source_target_pairs={{0,3},{1,4},{2,5},{3,6},{4,7},{5,0},{6,1},{7,2},{64,69},{65,70},{6... | collective-permute-start | bytes 245768 | tf_op jit(solution)/shard_map/ppermute | solution.py:77
  71.3 12.6 %collective-permute-start.7 = (bf16[32,1280]{1,0:T(8,128)(2,1)S(1)}, bf16[32,1280]{1,0:T(8,128)(2,1)S(1)}, u32[]{:S(2)}, u32[]{:S(2)}) collective-permute-start(bf16[32,1280]{1,0:T(8,128)(2,1)S(1)} %get-tuple-element.47.pair.refs_4_), channel_id=1, source_target_pairs={{0,2},{1,3},{2,4},{3,5},{4,6},{5,7},{6,0},{7,1},{64,70},{65,71},{6... | collective-permute-start | bytes 245768 | tf_op jit(solution)/shard_map/ppermute | solution.py:77
  72.4 11.4 %collective-permute-start.6 = (bf16[32,1280]{1,0:T(8,128)(2,1)S(1)}, bf16[32,1280]{1,0:T(8,128)(2,1)S(1)}, u32[]{:S(2)}, u32[]{:S(2)}) collective-permute-start(bf16[32,1280]{1,0:T(8,128)(2,1)S(1)} %get-tuple-element.47.pair.refs_4_), channel_id=1, source_target_pairs={{0,1},{1,2},{2,3},{3,4},{4,5},{5,6},{6,7},{7,0},{64,71},{65,64},{6... | collective-permute-start | bytes 245768 | tf_op jit(solution)/shard_map/ppermute | solution.py:77
  74.9 8.9 %collective-permute-start.9 = (bf16[16,1280]{1,0:T(8,128)(2,1)S(1)}, bf16[16,1280]{1,0:T(8,128)(2,1)S(1)}, u32[]{:S(2)}, u32[]{:S(2)}) collective-permute-start(bf16[16,1280]{1,0:T(8,128)(2,1)S(1)} %get-tuple-element.48), channel_id=1, source_target_pairs={{0,4},{1,5},{2,6},{3,7},{4,0},{5,1},{6,2},{7,3},{64,68},{65,69},{6... | collective-permute-start | bytes 122888 | tf_op jit(solution)/shard_map/ppermute | solution.py:77
  83.9 1.9 collective-permute-start.10
  84.6 0.7 copy-start.6
  85.8 0.7 copy-start.14
  86.5 1.0 copy-start.7
  87.5 1.0 copy-start.15
  120.4 1.8 copy-start.21
  120.7 1.5 collective-permute-start.11
  122.3 5.9 %copy-start.17 = (bf16[128,640]{1,0:T(8,128)(2,1)S(1)}, bf16[128,640]{1,0:T(8,128)(2,1)}, u32[]{:S(2)}) copy-start(bf16[128,640]{1,0:T(8,128)(2,1)} %get-tuple-element.57.refs_3_) | copy-start | bytes 491524
  123.9 26.4 %all-to-all-start.3 = ((f16[8,32,1408]{2,1,0:T(8,128)(2,1)}), f16[8,32,1408]{2,1,0:T(8,128)(2,1)}, u32[]{:S(2)}, u32[]{:S(2)}) async-start(f16[8,32,1408]{2,1,0:T(8,128)(2,1)} %broadcast_in_dim.2), calls=%async_computation.3 | async-start | bytes 1441792 | tf_op jit(solution)/shard_map/all_to_all | solution.py:491
  128.2 3.8 %collective-permute-start.12 = (bf16[128,640]{1,0:T(8,128)(2,1)S(1)}, bf16[128,640]{1,0:T(8,128)(2,1)S(1)}, u32[]{:S(2)}, u32[]{:S(2)}) collective-permute-start(bf16[128,640]{1,0:T(8,128)(2,1)S(1)} %copy-done.17), channel_id=1, source_target_pairs={{0,64},{64,0},{128,192},{192,128},{1,65},{65,1},{129,193},{193,129... | collective-permute-start | bytes 491528 | tf_op jit(solution)/shard_map/ppermute | solution.py:67
  128.6 3.3 %copy-start.3 = (bf16[256,1280]{1,0:T(8,128)(2,1)S(1)}, bf16[256,1280]{1,0:T(8,128)(2,1)}, u32[]{:S(2)}) copy-start(bf16[256,1280]{1,0:T(8,128)(2,1)} %copy-done.2) | copy-start | bytes 1966084
  128.6 3.3 %copy-start.8 = (bf16[112,1280]{1,0:T(8,128)(2,1)S(1)}, bf16[112,1280]{1,0:T(8,128)(2,1)}, u32[]{:S(2)}) copy-start(bf16[112,1280]{1,0:T(8,128)(2,1)} %copy-done.6) | copy-start | bytes 860164
  128.6 3.3 %copy-start.11 = (f32[128,640]{1,0:T(8,128)S(1)}, f32[128,640]{1,0:T(8,128)}, u32[]{:S(2)}) copy-start(f32[128,640]{1,0:T(8,128)} %get-tuple-element.58.refs_5_) | copy-start | bytes 983044
  128.6 3.3 %copy-start.16 = (bf16[112,1280]{1,0:T(8,128)(2,1)S(1)}, bf16[112,1280]{1,0:T(8,128)(2,1)}, u32[]{:S(2)}) copy-start(bf16[112,1280]{1,0:T(8,128)(2,1)} %copy-done.14) | copy-start | bytes 860164
  128.6 3.3 %collective-permute-start.13 = (f32[128,640]{1,0:T(8,128)}, f32[128,640]{1,0:T(8,128)S(1)}, u32[]{:S(2)}, u32[]{:S(2)}) collective-permute-start(f32[128,640]{1,0:T(8,128)} %get-tuple-element.58.refs_5_), channel_id=1, source_target_pairs={{0,64},{64,0},{128,192},{192,128},{1,65},{65,1},{129,193},{193,129... | collective-permute-start | bytes 983048 | tf_op jit(solution)/shard_map/ppermute | solution.py:67
  132.6 0.8 copy-start.9
  133.5 0.7 copy-start.12
  134.2 17.4 %copy-start.1 = (bf16[1280,640]{1,0:T(8,128)(2,1)S(1)}, bf16[1280,640]{1,0:T(8,128)(2,1)}, u32[]{:S(2)}) copy-start(bf16[1280,640]{1,0:T(8,128)(2,1)} %slice_select_fusion.refs_2_) | copy-start | bytes 4915204
  134.2 17.4 %copy-start.10 = (bf16[256,1280]{1,0:T(8,128)(2,1)S(1)}, bf16[256,1280]{1,0:T(8,128)(2,1)}, u32[]{:S(2)}) copy-start(bf16[256,1280]{1,0:T(8,128)(2,1)} %copy-done.9) | copy-start | bytes 1966084
  134.2 17.4 %copy-start.13 = (bf16[256,640]{1,0:T(8,128)(2,1)S(1)}, bf16[256,640]{1,0:T(8,128)(2,1)}, u32[]{:S(2)}) copy-start(bf16[256,640]{1,0:T(8,128)(2,1)} %copy-done.12) | copy-start | bytes 983044
  201.5 2.7 %collective-permute-start.14 = (f32[400,128]{1,0:T(8,128)S(1)}, f32[400,128]{1,0:T(8,128)S(1)}, u32[]{:S(2)}, u32[]{:S(2)}) collective-permute-start(f32[400,128]{1,0:T(8,128)S(1)} %get-tuple-element.63), channel_id=1, source_target_pairs={{0,64},{64,0},{128,192},{192,128},{1,65},{65,1},{129,193},{193,129... | collective-permute-start | bytes 614408 | tf_op jit(solution)/shard_map/ppermute | solution.py:67

commit v7 on v6

--- a/solution.py
+++ b/solution.py
@@ -26,22 +26,24 @@
 PEERS = [[((y % 2) * 2 + core) * 8 + x * 2 + y // 2 for x, y in WALK] for core in range(2)]
 SMEM = pl.BlockSpec(memory_space=pltpu.SMEM)
 VMEM = pl.BlockSpec(memory_space=pltpu.VMEM)
+HBM = pl.BlockSpec(memory_space=pltpu.HBM)
 F32 = jnp.float32
 BF16 = jnp.bfloat16
 
 
-def call(body, name, inputs, scalars, outs, flops=0, scratch=(), room=40):
-    moved = sum(math.prod(a.shape) * a.dtype.itemsize for a in list(inputs) + list(outs))
+def call(body, name, inputs, scalars, outs, flops=0, scratch=(), room=40, far=()):
+    arrays = list(inputs) + list(far)
+    moved = sum(math.prod(a.shape) * a.dtype.itemsize for a in arrays + list(outs))
     return pl.pallas_call(
         body,
         name=name,
         out_shape=outs,
-        in_specs=[SMEM] * len(scalars) + [VMEM] * len(inputs),
+        in_specs=[SMEM] * len(scalars) + [VMEM] * len(inputs) + [HBM] * len(far),
         out_specs=[VMEM] * len(outs),
         scratch_shapes=list(scratch),
         compiler_params=pltpu.CompilerParams(vmem_limit_bytes=room * 2**20),
         cost_estimate=pl.CostEstimate(flops=flops, bytes_accessed=moved, transcendentals=0),
-    )(*scalars, *inputs)
+    )(*scalars, *arrays)
 
 
 def shape(dims, dtype):
@@ -199,12 +201,18 @@
         store(at(sender, above(place, sender, n_mp // 2, n_mp)), source[to : to + piece, :])
 
 
-def score_kernel(place, pair, own, came, embed, weights, out, both):
+def score_kernel(place, pair, own, came, embed, weights, out, both, w_in, w_out, sems):
     n_mp, piece = out.shape[0], out.shape[1] // 2
     width = embed.shape[1]
     half = n_mp * piece
     rows = 2 * half
-    hidden = weights.shape[1] // 2
+    hidden = w_in.shape[1]
+    copies = [
+        pltpu.make_async_copy(weights.at[:, pl.ds(i * hidden, hidden)], target, sems.at[i])
+        for i, target in enumerate((w_in, w_out))
+    ]
+    for copy in copies:
+        copy.start()
 
     def store(at, value):
         summed = value.astype(F32)
@@ -212,6 +220,8 @@
         both[pl.ds(pl.multiple_of(rows + at, piece), piece), :] = normalize(summed)
 
     rows_in_order(place, own, came, pair, store)
+    for copy in copies:
+        copy.wait()
 
     def finish(value):
         power = power_of(top_of(value))
@@ -225,12 +235,12 @@
 
     @pl.when(place[0] == 0)
     def _():
-        fake = forward_part(both[:rows, :], weights[:, :hidden], weights[:, hidden:])[2]
+        fake = forward_part(both[:rows, :], w_in[...], w_out[...])[2]
         finish(fake.astype(F32))
 
     @pl.when(place[0] != 0)
     def _():
-        real = forward_part(both[...], weights[:, :hidden], weights[:, hidden:])[2]
+        real = forward_part(both[...], w_in[...], w_out[...])[2]
         uncond, cond = real[rows:].astype(F32), real[:rows].astype(F32)
         finish(uncond + GUIDANCE * (cond - uncond))
 
@@ -480,11 +490,15 @@
     (score_parts,) = call(
         score_kernel,
         "score",
-        [noised, around, around_other, embedding, score_weights],
+        [noised, around, around_other, embedding],
         [place],
         [shape((n_mp, 2 * piece, width + LANES), F32)],
         8 * work,
-        [pltpu.VMEM((2 * positions, width), BF16)],
+        [pltpu.VMEM((2 * positions, width), BF16)]
+        + [pltpu.VMEM((width, hidden), BF16)] * 2
+        + [pltpu.SemaphoreType.DMA((2,))],
+        room=60,
+        far=[score_weights],
     )
 
     def exchange(blocks):

time: 207 us -> 210 us (1.014)
  Pallas kernels: 19.1 us -> 22.8 us
    pallas_call x14, Pallas kernels: 19.1 us -> 22.8 us  [call(): pl.pallas_call(body, name=name, out_shape=outs, in_specs=[SMEM] * len(sca...]
    unnamed x60 -> x66, local copies, waits for them, and re-layouts: 9.78 us -> 8.16 us
where the time goes in v7:
time: 210 us
  blocking collectives  73 us (35%)
  waiting for transfers between devices  49.2 us (23%)
  starting transfers between devices  43 us (20%)
  Pallas kernels  22.8 us (11%)
  local copies, waits for them, and re-layouts  10.2 us (5%)
  other arithmetic  7.94 us (4%)
  between operations  3.52 us (2%)
    all_to_all x1, blocking collectives, local(): lax.all_to_all(grads.astype(jnp.float16), PLANE, 0, 0, axis_index_groups=...  44.3 us
    all_to_all x1, blocking collectives, exchange(): lax.all_to_all(blocks.astype(jnp.float16), 'mp', 0, 0, tiled=True)  28.7 us
    pallas_call x14, Pallas kernels, call(): pl.pallas_call(body, name=name, out_shape=outs, in_specs=[SMEM] * len(sca...  22.8 us
    ppermute x8, starting transfers between devices, paired(): return lax.ppermute(block, ('group', 'mp'), pairs)  20 us
    all_to_all x1, waiting for transfers between devices, exchange(): lax.all_to_all(blocks.astype(jnp.float16), 'mp', 0, 0, tiled=True)  15.3 us
    all_to_all x2, waiting for transfers between devices, gather(): return lax.all_to_all(blocks, PLANE, 0, 0, tiled=True).reshape(width, -1)  15 us
    all_to_all x2, starting transfers between devices, gather(): return lax.all_to_all(blocks, PLANE, 0, 0, tiled=True).reshape(width, -1)  13.2 us
    ppermute x8, waiting for transfers between devices, paired(): return lax.ppermute(block, ('group', 'mp'), pairs)  10.7 us
  transfers between devices with their start and end apart: 18, of which 9 were waited for; matrix products, arithmetic and copies ran while one was open for 3% of the time, Pallas kernels for 4%

profile of v7, /device:TPU:1, one launch (start us, length us, event | category | flops | bytes accessed | tf_op | source)
XLA Modules:
  0.0 209.7 jit_solution(17606768047090061176)
XLA Ops:
  0.6 0.9 copy-done.22
  1.5 1.5 lay.2
  3.0 8.8 %all-to-all-start = ((bf16[32,40,640]{2,1,0:T(8,128)(2,1)}), bf16[32,40,640]{2,1,0:T(8,128)(2,1)}, u32[]{:S(2)}, u32[]{:S(2)}) async-start(bf16[32,40,640]{2,1,0:T(8,128)(2,1)} %lay.2), calls=%async_computation | async-start | bytes 3276800 | tf_op jit(solution)/shard_map/all_to_all | solution.py:427
  16.0 1.7 copy-done.2
  17.8 0.7 dynamic-slice_convert_fusion.refs_4_.embed.refs_0_
  18.6 0.8 prepare.1
  19.4 0.8 copy-done.4
  20.3 0.7 copy-done.18
  20.9 15.0 %all-to-all-done = bf16[32,40,640]{2,1,0:T(8,128)(2,1)} async-done(((bf16[32,40,640]{2,1,0:T(8,128)(2,1)}), bf16[32,40,640]{2,1,0:T(8,128)(2,1)}, u32[]{:S(2)}, u32[]{:S(2)}) %all-to-all-start) | async-done | bytes 1638432 | tf_op jit(solution)/shard_map/all_to_all | solution.py:427
  35.9 4.4 %all-to-all-start.1 = ((bf16[32,40,1280]{2,1,0:T(8,128)(2,1)}), bf16[32,40,1280]{2,1,0:T(8,128)(2,1)S(1)}, u32[]{:S(2)}, u32[]{:S(2)}) async-start(bf16[32,40,1280]{2,1,0:T(8,128)(2,1)} %copy-done.2), calls=%async_computation.1 | async-start | bytes 6553600 | tf_op jit(solution)/shard_map/all_to_all | solution.py:427
  40.7 3.6 %collective-permute-done.other = bf16[1280,640]{1,0:T(8,128)(2,1)} collective-permute-done((bf16[1280,640]{1,0:T(8,128)(2,1)}, bf16[1280,640]{1,0:T(8,128)(2,1)}, u32[]{:S(2)}, u32[]{:S(2)}) %collective-permute-start) | collective-permute-done | bytes 1638432 | tf_op jit(solution)/shard_map/ppermute | solution.py:69
  44.3 4.0 %generate.1 = (f32[128,640]{1,0:T(8,128)}, bf16[128,640]{1,0:T(8,128)(2,1)}, bf16[16,1280]{1,0:T(8,128)(2,1)}, bf16[16,1280]{1,0:T(8,128)(2,1)}, bf16[32,1280]{1...) custom-call(s32[3]{0:T(128)} %copy-done.25, bf16[256,1280]{1,0:T(8,128)(2,1)} %copy-done.4, ...), custom_call_target="tpu_custom_call" | custom-call | flops 419430400 | bytes 4751360 | tf_op jit(solution)/shard_map/generate/pallas_call | solution.py:37
  48.3 5.6 %collective-permute-start.2 = (bf16[32,1280]{1,0:T(8,128)(2,1)}, bf16[32,1280]{1,0:T(8,128)(2,1)S(1)}, u32[]{:S(2)}, u32[]{:S(2)}) collective-permute-start(bf16[32,1280]{1,0:T(8,128)(2,1)} %get-tuple-element.42), channel_id=1, source_target_pairs={{0,1},{1,2},{2,3},{3,4},{4,5},{5,6},{6,7},{7,0},{64,71},{65,64},{6... | collective-permute-start | bytes 245768 | tf_op jit(solution)/shard_map/ppermute | solution.py:79
  53.9 1.2 collective-permute-start.3
  55.5 4.5 %collective-permute-start.1 = (bf16[16,1280]{1,0:T(8,128)(2,1)}, bf16[16,1280]{1,0:T(8,128)(2,1)S(1)}, u32[]{:S(2)}, u32[]{:S(2)}) collective-permute-start(bf16[16,1280]{1,0:T(8,128)(2,1)} %get-tuple-element.41), channel_id=1, source_target_pairs={{0,4},{1,5},{2,6},{3,7},{4,0},{5,1},{6,2},{7,3},{64,68},{65,69},{6... | collective-permute-start | bytes 122888 | tf_op jit(solution)/shard_map/ppermute | solution.py:79
  60.0 4.3 %collective-permute-done.1.across = bf16[16,1280]{1,0:T(8,128)(2,1)S(1)} collective-permute-done((bf16[16,1280]{1,0:T(8,128)(2,1)}, bf16[16,1280]{1,0:T(8,128)(2,1)S(1)}, u32[]{:S(2)}, u32[]{:S(2)}) %collective-permute-start.1) | collective-permute-done | bytes 40992 | tf_op jit(solution)/shard_map/ppermute | solution.py:79
  64.3 0.8 copy-done.30
  65.1 0.6 sums.1
  65.6 1.8 collective-permute-start.5
  67.4 1.0 collective-permute-done.5.came
  68.5 0.6 latent.1
  69.1 2.2 %collective-permute-start.8 = (bf16[32,1280]{1,0:T(8,128)(2,1)S(1)}, bf16[32,1280]{1,0:T(8,128)(2,1)S(1)}, u32[]{:S(2)}, u32[]{:S(2)}) collective-permute-start(bf16[32,1280]{1,0:T(8,128)(2,1)S(1)} %get-tuple-element.47.pair.refs_4_), channel_id=1, source_target_pairs={{0,3},{1,4},{2,5},{3,6},{4,7},{5,0},{6,1},{7,2},{64,69},{65,70},{6... | collective-permute-start | bytes 245768 | tf_op jit(solution)/shard_map/ppermute | solution.py:79
  71.3 1.2 collective-permute-start.7
  72.4 2.4 %collective-permute-start.6 = (bf16[32,1280]{1,0:T(8,128)(2,1)S(1)}, bf16[32,1280]{1,0:T(8,128)(2,1)S(1)}, u32[]{:S(2)}, u32[]{:S(2)}) collective-permute-start(bf16[32,1280]{1,0:T(8,128)(2,1)S(1)} %get-tuple-element.47.pair.refs_4_), channel_id=1, source_target_pairs={{0,1},{1,2},{2,3},{3,4},{4,5},{5,6},{6,7},{7,0},{64,71},{65,64},{6... | collective-permute-start | bytes 245768 | tf_op jit(solution)/shard_map/ppermute | solution.py:79
  74.9 2.5 %collective-permute-start.9 = (bf16[16,1280]{1,0:T(8,128)(2,1)S(1)}, bf16[16,1280]{1,0:T(8,128)(2,1)S(1)}, u32[]{:S(2)}, u32[]{:S(2)}) collective-permute-start(bf16[16,1280]{1,0:T(8,128)(2,1)S(1)} %get-tuple-element.48), channel_id=1, source_target_pairs={{0,4},{1,5},{2,6},{3,7},{4,0},{5,1},{6,2},{7,3},{64,68},{65,69},{6... | collective-permute-start | bytes 122888 | tf_op jit(solution)/shard_map/ppermute | solution.py:79
  77.4 6.5 %collective-permute-done.9.refs_3_ = bf16[16,1280]{1,0:T(8,128)(2,1)S(1)} collective-permute-done((bf16[16,1280]{1,0:T(8,128)(2,1)S(1)}, bf16[16,1280]{1,0:T(8,128)(2,1)S(1)}, u32[]{:S(2)}, u32[]{:S(2)}) %collective-permute-start.9) | collective-permute-done | bytes 40992 | tf_op jit(solution)/shard_map/ppermute | solution.py:79
  83.9 0.7 collective-permute-start.10
  84.6 1.3 collective-permute-done.10.came
  85.9 1.7 copy-done
  87.6 7.1 %score.1 = f32[8,32,1408]{2,1,0:T(8,128)} custom-call(s32[3]{0:T(128)} %copy-done.25, bf16[32,1280]{1,0:T(8,128)(2,1)} %copy-done.15, bf16[112,1280]{1,0:T(8,128)(2,1)} %copy-done.8, bf16[112,1280]{1,0:T(8,128)(2,1)} %collective-permute-done.10.came, f32[1,1280]{1,0:T(1,128)} %copy-done.28, bf16[1280,1280]{1,0:T(8,128)(2,1)} %bitcast.6), custom_call_target="tpu_custom_call" | custom-call | flops 1677721600 | bytes 5379072 | tf_op jit(solution)/shard_map/score/pallas_call | solution.py:37
  94.7 1.4 convert_element_type.28
  96.1 28.7 %all_to_all.25 = f16[8,32,1408]{2,1,0:T(8,128)(2,1)S(1)} all-to-all(f16[8,32,1408]{2,1,0:T(8,128)(2,1)S(1)} %convert_element_type.28), channel_id=1, replica_groups=mesh['group'=4,'dp'=8,'mp'=8] {'mp'}, dimensions={0} | all-to-all | bytes 1441792 | tf_op jit(solution)/shard_map/all_to_all | solution.py:505
  125.7 1.0 collective-permute-done.11.refs_2_
  126.7 0.7 pack.1
  127.5 0.9 broadcast_in_dim.2
  128.5 4.2 %all-to-all-start.3 = ((f16[8,32,1408]{2,1,0:T(8,128)(2,1)}), f16[8,32,1408]{2,1,0:T(8,128)(2,1)}, u32[]{:S(2)}, u32[]{:S(2)}) async-start(f16[8,32,1408]{2,1,0:T(8,128)(2,1)} %broadcast_in_dim.2), calls=%async_computation.3 | async-start | bytes 1441792 | tf_op jit(solution)/shard_map/all_to_all | solution.py:505
  133.4 3.0 %slice_select_fusion.refs_2_ = bf16[1280,640]{1,0:T(8,128)(2,1)} fusion(bf16[1280,640]{1,0:T(8,128)(2,1)} %bitcast.3.mine, bf16[1280,1280]{1,0:T(8,128)(2,1)S(1)} %bitcast.7, pred[]{:T(512)S(6)} %eq.5), kind=kLoop, calls=%fused_computation | loop fusion | flops 819200 | bytes 4915201 | tf_op jit(solution)/shard_map/jit(_where)/select_n | solution.py:541
  136.4 1.1 refresh.1
  137.6 0.8 copy-done.10
  138.4 0.7 copy-done.13
  139.5 15.3 %all-to-all-done.3 = f16[8,32,1408]{2,1,0:T(8,128)(2,1)} async-done(((f16[8,32,1408]{2,1,0:T(8,128)(2,1)}), f16[8,32,1408]{2,1,0:T(8,128)(2,1)}, u32[]{:S(2)}, u32[]{:S(2)}) %all-to-all-start.3) | async-done | bytes 720928 | tf_op jit(solution)/shard_map/all_to_all | solution.py:505
  154.9 1.2 convert_element_type.31.refs_1_
  156.1 3.0 %grads.1 = f32[16,816,128]{2,1,0:T(8,128)S(1)} custom-call(s32[3]{0:T(128)S(1)} %copy-done.27, f32[8,32,1408]{2,1,0:T(8,128)S(1)} %convert_element_type.31.refs_1_, bf16[1280,640]{1,0:T(8,128)(2,1)S(1)} %copy-done.3, f32[256,640]{1,0:T(8,128)S(1)} %fusion.5.refs_3_, bf16[256,1280]{1,0:T(8,128)(2,1)S(1)} %copy-done.11, bf16[256,640]{1,0:T(8,128)(2,1)S(1)} %copy-done.14), custom_call_target="tpu_custom_call" | custom-call | flops 1258291200 | bytes 11403264 | tf_op jit(solution)/shard_map/grads/pallas_call | solution.py:37
  159.6 44.3 %all_to_all.26 = f16[16,816,128]{2,1,0:T(8,128)(2,1)S(1)} all-to-all(f16[16,816,128]{2,1,0:T(8,128)(2,1)S(1)} %convert_element_type.32), channel_id=1, replica_groups={{0,16,32,48,176,160,144,24,40,56,184,168,152,136,8,128},{64,80,96,112,2..., dimensions={0} | all-to-all | bytes 6684672 | tf_op jit(solution)/shard_map/all_to_all | solution.py:551
  204.3 1.2 collect.1
  205.5 1.6 collective-permute-start.14
  207.1 1.1 collective-permute-done.14.came
  208.2 1.5 place.1
  (84 shorter events, 5.5 us)
Async XLA Ops:
  0.6 0.9 copy-start.22
  3.0 8.8 %copy-start.31 = (s32[2]{0:T(128)S(1)}, s32[2]{0:T(128)}, u32[]{:S(2)}) copy-start(s32[2]{0:T(128)} %param.10) | copy-start | bytes 28
  3.0 10.2 %copy-start.32 = (s32[2]{0:T(128)S(1)}, s32[2]{0:T(128)}, u32[]{:S(2)}) copy-start(s32[2]{0:T(128)} %param.11) | copy-start | bytes 28
  3.0 12.4 %copy-start.23 = (bf16[40,2,640]{2,1,0:T(2,128)(2,1)S(1)}, bf16[40,2,640]{2,1,0:T(2,128)(2,1)}, u32[]{:S(2)}) copy-start(bf16[40,2,640]{2,1,0:T(2,128)(2,1)} %refs_0_.3) | copy-start | bytes 307204
  3.0 12.5 %copy-start.24 = (bf16[40,2,640]{2,1,0:T(2,128)(2,1)S(1)}, bf16[40,2,640]{2,1,0:T(2,128)(2,1)}, u32[]{:S(2)}) copy-start(bf16[40,2,640]{2,1,0:T(2,128)(2,1)} %refs_1_.1) | copy-start | bytes 307204
  3.0 32.9 %all-to-all-start = ((bf16[32,40,640]{2,1,0:T(8,128)(2,1)}), bf16[32,40,640]{2,1,0:T(8,128)(2,1)}, u32[]{:S(2)}, u32[]{:S(2)}) async-start(bf16[32,40,640]{2,1,0:T(8,128)(2,1)} %lay.2), calls=%async_computation | async-start | bytes 3276800 | tf_op jit(solution)/shard_map/all_to_all | solution.py:427
  15.5 3.1 %copy-start.6 = (bf16[2,256,1280]{2,1,0:T(8,128)(2,1)S(1)}, bf16[2,256,1280]{2,1,0:T(8,128)(2,1)}, u32[]{:S(2)}) copy-start(bf16[2,256,1280]{2,1,0:T(8,128)(2,1)} %refs_2_.1) | copy-start | bytes 3932164
  15.5 3.1 %copy-start.7 = (bf16[2,256,1280]{2,1,0:T(8,128)(2,1)S(1)}, bf16[2,256,1280]{2,1,0:T(8,128)(2,1)}, u32[]{:S(2)}) copy-start(bf16[2,256,1280]{2,1,0:T(8,128)(2,1)} %refs_3_.1) | copy-start | bytes 3932164
  16.0 1.7 copy-start.2
  17.8 18.1 %copy-start.25 = (s32[3]{0:T(128)}, s32[3]{0:T(128)S(1)}, u32[]{:S(2)}) copy-start(s32[3]{0:T(128)S(1)} %pad_add_fusion.refs_0_.place) | copy-start | bytes 40
  18.6 17.4 %copy-start.28 = (f32[1,1280]{1,0:T(1,128)}, f32[1,1280]{1,0:T(1,128)S(1)}, u32[]{:S(2)}) copy-start(f32[1,1280]{1,0:T(1,128)S(1)} %dynamic-slice_convert_fusion.refs_4_.embed.refs_0_) | copy-start | bytes 15364
  19.4 0.8 copy-start.4
  35.9 50.0 %all-to-all-start.1 = ((bf16[32,40,1280]{2,1,0:T(8,128)(2,1)}), bf16[32,40,1280]{2,1,0:T(8,128)(2,1)S(1)}, u32[]{:S(2)}, u32[]{:S(2)}) async-start(bf16[32,40,1280]{2,1,0:T(8,128)(2,1)} %copy-done.2), calls=%async_computation.1 | async-start | bytes 6553600 | tf_op jit(solution)/shard_map/all_to_all | solution.py:427
  40.3 23.9 %copy-start.26 = (s32[3]{0:T(128)S(1)}, s32[3]{0:T(128)}, u32[]{:S(2)}) copy-start(s32[3]{0:T(128)} %copy-done.25) | copy-start | bytes 40
  40.4 28.1 %copy-start.19 = (f32[32,1280]{1,0:T(8,128)S(1)}, f32[32,1280]{1,0:T(8,128)}, u32[]{:S(2)}) copy-start(f32[32,1280]{1,0:T(8,128)} %copy-done.18) | copy-start | bytes 491524
  40.4 3.9 %collective-permute-start = (bf16[1280,640]{1,0:T(8,128)(2,1)}, bf16[1280,640]{1,0:T(8,128)(2,1)}, u32[]{:S(2)}, u32[]{:S(2)}) collective-permute-start(bf16[1280,640]{1,0:T(8,128)(2,1)} %bitcast.3.mine), channel_id=1, source_target_pairs={{0,64},{64,0},{128,192},{192,128},{1,65},{65,1},{129,193},{193,129... | collective-permute-start | bytes 4915208 | tf_op jit(solution)/shard_map/ppermute | solution.py:69
  48.3 15.9 %collective-permute-start.2 = (bf16[32,1280]{1,0:T(8,128)(2,1)}, bf16[32,1280]{1,0:T(8,128)(2,1)S(1)}, u32[]{:S(2)}, u32[]{:S(2)}) collective-permute-start(bf16[32,1280]{1,0:T(8,128)(2,1)} %get-tuple-element.42), channel_id=1, source_target_pairs={{0,1},{1,2},{2,3},{3,4},{4,5},{5,6},{6,7},{7,0},{64,71},{65,64},{6... | collective-permute-start | bytes 245768 | tf_op jit(solution)/shard_map/ppermute | solution.py:79
  53.9 10.4 %collective-permute-start.3 = (bf16[32,1280]{1,0:T(8,128)(2,1)}, bf16[32,1280]{1,0:T(8,128)(2,1)S(1)}, u32[]{:S(2)}, u32[]{:S(2)}) collective-permute-start(bf16[32,1280]{1,0:T(8,128)(2,1)} %get-tuple-element.43), channel_id=1, source_target_pairs={{0,2},{1,3},{2,4},{3,5},{4,6},{5,7},{6,0},{7,1},{64,70},{65,71},{6... | collective-permute-start | bytes 245768 | tf_op jit(solution)/shard_map/ppermute | solution.py:79
  55.1 9.2 %collective-permute-start.4 = (bf16[32,1280]{1,0:T(8,128)(2,1)}, bf16[32,1280]{1,0:T(8,128)(2,1)S(1)}, u32[]{:S(2)}, u32[]{:S(2)}) collective-permute-start(bf16[32,1280]{1,0:T(8,128)(2,1)} %get-tuple-element.44), channel_id=1, source_target_pairs={{0,3},{1,4},{2,5},{3,6},{4,7},{5,0},{6,1},{7,2},{64,69},{65,70},{6... | collective-permute-start | bytes 245768 | tf_op jit(solution)/shard_map/ppermute | solution.py:79
  55.5 8.7 %collective-permute-start.1 = (bf16[16,1280]{1,0:T(8,128)(2,1)}, bf16[16,1280]{1,0:T(8,128)(2,1)S(1)}, u32[]{:S(2)}, u32[]{:S(2)}) collective-permute-start(bf16[16,1280]{1,0:T(8,128)(2,1)} %get-tuple-element.41), channel_id=1, source_target_pairs={{0,4},{1,5},{2,6},{3,7},{4,0},{5,1},{6,2},{7,3},{64,68},{65,69},{6... | collective-permute-start | bytes 122888 | tf_op jit(solution)/shard_map/ppermute | solution.py:79
  64.3 0.8 copy-start.30
  65.6 2.8 %collective-permute-start.5 = (f32[32,1280]{1,0:T(8,128)S(1)}, f32[32,1280]{1,0:T(8,128)S(1)}, u32[]{:S(2)}, u32[]{:S(2)}) collective-permute-start(f32[32,1280]{1,0:T(8,128)S(1)} %sums.1), channel_id=1, source_target_pairs={{0,64},{64,0},{128,192},{192,128},{1,65},{65,1},{129,193},{193,129... | collective-permute-start | bytes 491528 | tf_op jit(solution)/shard_map/ppermute | solution.py:69
  69.1 15.5 %copy-start.20 = (f32[32,1280]{1,0:T(8,128)}, f32[32,1280]{1,0:T(8,128)S(1)}, u32[]{:S(2)}) copy-start(f32[32,1280]{1,0:T(8,128)S(1)} %get-tuple-element.53.refs_3_) | copy-start | bytes 491524
  69.1 16.9 %copy-start.15 = (bf16[32,1280]{1,0:T(8,128)(2,1)}, bf16[32,1280]{1,0:T(8,128)(2,1)S(1)}, u32[]{:S(2)}) copy-start(bf16[32,1280]{1,0:T(8,128)(2,1)S(1)} %get-tuple-element.47.pair.refs_4_) | copy-start | bytes 245764
  69.1 14.7 %collective-permute-start.8 = (bf16[32,1280]{1,0:T(8,128)(2,1)S(1)}, bf16[32,1280]{1,0:T(8,128)(2,1)S(1)}, u32[]{:S(2)}, u32[]{:S(2)}) collective-permute-start(bf16[32,1280]{1,0:T(8,128)(2,1)S(1)} %get-tuple-element.47.pair.refs_4_), channel_id=1, source_target_pairs={{0,3},{1,4},{2,5},{3,6},{4,7},{5,0},{6,1},{7,2},{64,69},{65,70},{6... | collective-permute-start | bytes 245768 | tf_op jit(solution)/shard_map/ppermute | solution.py:79
  71.3 12.6 %collective-permute-start.7 = (bf16[32,1280]{1,0:T(8,128)(2,1)S(1)}, bf16[32,1280]{1,0:T(8,128)(2,1)S(1)}, u32[]{:S(2)}, u32[]{:S(2)}) collective-permute-start(bf16[32,1280]{1,0:T(8,128)(2,1)S(1)} %get-tuple-element.47.pair.refs_4_), channel_id=1, source_target_pairs={{0,2},{1,3},{2,4},{3,5},{4,6},{5,7},{6,0},{7,1},{64,70},{65,71},{6... | collective-permute-start | bytes 245768 | tf_op jit(solution)/shard_map/ppermute | solution.py:79
  72.4 11.4 %collective-permute-start.6 = (bf16[32,1280]{1,0:T(8,128)(2,1)S(1)}, bf16[32,1280]{1,0:T(8,128)(2,1)S(1)}, u32[]{:S(2)}, u32[]{:S(2)}) collective-permute-start(bf16[32,1280]{1,0:T(8,128)(2,1)S(1)} %get-tuple-element.47.pair.refs_4_), channel_id=1, source_target_pairs={{0,1},{1,2},{2,3},{3,4},{4,5},{5,6},{6,7},{7,0},{64,71},{65,64},{6... | collective-permute-start | bytes 245768 | tf_op jit(solution)/shard_map/ppermute | solution.py:79
  74.9 8.9 %collective-permute-start.9 = (bf16[16,1280]{1,0:T(8,128)(2,1)S(1)}, bf16[16,1280]{1,0:T(8,128)(2,1)S(1)}, u32[]{:S(2)}, u32[]{:S(2)}) collective-permute-start(bf16[16,1280]{1,0:T(8,128)(2,1)S(1)} %get-tuple-element.48), channel_id=1, source_target_pairs={{0,4},{1,5},{2,6},{3,7},{4,0},{5,1},{6,2},{7,3},{64,68},{65,69},{6... | collective-permute-start | bytes 122888 | tf_op jit(solution)/shard_map/ppermute | solution.py:79
  83.9 2.1 collective-permute-start.10
  85.9 1.7 copy-start
  124.9 1.9 copy-start.16
  124.9 1.9 copy-start.21
  124.9 1.9 copy-start.27
  125.0 7.7 %copy-start.17 = (bf16[128,640]{1,0:T(8,128)(2,1)S(1)}, bf16[128,640]{1,0:T(8,128)(2,1)}, u32[]{:S(2)}) copy-start(bf16[128,640]{1,0:T(8,128)(2,1)} %get-tuple-element.57.refs_3_) | copy-start | bytes 491524
  125.2 1.5 collective-permute-start.11
  126.7 6.6 %copy-start.1 = (bf16[32,40,1280]{2,1,0:T(8,128)(2,1)S(1)}, bf16[32,40,1280]{2,1,0:T(8,128)(2,1)}, u32[]{:S(2)}) copy-start(bf16[32,40,1280]{2,1,0:T(8,128)(2,1)} %copy-done) | copy-start | bytes 9830404
  128.5 26.4 %all-to-all-start.3 = ((f16[8,32,1408]{2,1,0:T(8,128)(2,1)}), f16[8,32,1408]{2,1,0:T(8,128)(2,1)}, u32[]{:S(2)}, u32[]{:S(2)}) async-start(f16[8,32,1408]{2,1,0:T(8,128)(2,1)} %broadcast_in_dim.2), calls=%async_computation.3 | async-start | bytes 1441792 | tf_op jit(solution)/shard_map/all_to_all | solution.py:505
  132.7 3.7 %collective-permute-start.12 = (bf16[128,640]{1,0:T(8,128)(2,1)S(1)}, bf16[128,640]{1,0:T(8,128)(2,1)S(1)}, u32[]{:S(2)}, u32[]{:S(2)}) collective-permute-start(bf16[128,640]{1,0:T(8,128)(2,1)S(1)} %copy-done.17), channel_id=1, source_target_pairs={{0,64},{64,0},{128,192},{192,128},{1,65},{65,1},{129,193},{193,129... | collective-permute-start | bytes 491528 | tf_op jit(solution)/shard_map/ppermute | solution.py:69
  133.1 3.3 %copy-start.5 = (bf16[256,1280]{1,0:T(8,128)(2,1)S(1)}, bf16[256,1280]{1,0:T(8,128)(2,1)}, u32[]{:S(2)}) copy-start(bf16[256,1280]{1,0:T(8,128)(2,1)} %copy-done.4) | copy-start | bytes 1966084
  133.1 3.3 %copy-start.9 = (bf16[112,1280]{1,0:T(8,128)(2,1)S(1)}, bf16[112,1280]{1,0:T(8,128)(2,1)}, u32[]{:S(2)}) copy-start(bf16[112,1280]{1,0:T(8,128)(2,1)} %copy-done.8) | copy-start | bytes 860164
  133.1 3.3 %copy-start.12 = (f32[128,640]{1,0:T(8,128)S(1)}, f32[128,640]{1,0:T(8,128)}, u32[]{:S(2)}) copy-start(f32[128,640]{1,0:T(8,128)} %get-tuple-element.58.refs_5_) | copy-start | bytes 983044
  133.2 3.3 %copy-start.29 = (f32[1,1280]{1,0:T(1,128)S(1)}, f32[1,1280]{1,0:T(1,128)}, u32[]{:S(2)}) copy-start(f32[1,1280]{1,0:T(1,128)} %copy-done.28) | copy-start | bytes 15364
  133.2 3.3 %collective-permute-start.13 = (f32[128,640]{1,0:T(8,128)}, f32[128,640]{1,0:T(8,128)S(1)}, u32[]{:S(2)}, u32[]{:S(2)}) collective-permute-start(f32[128,640]{1,0:T(8,128)} %get-tuple-element.58.refs_5_), channel_id=1, source_target_pairs={{0,64},{64,0},{128,192},{192,128},{1,65},{65,1},{129,193},{193,129... | collective-permute-start | bytes 983048 | tf_op jit(solution)/shard_map/ppermute | solution.py:69
  137.6 0.8 copy-start.10
  139.1 17.0 %copy-start.3 = (bf16[1280,640]{1,0:T(8,128)(2,1)S(1)}, bf16[1280,640]{1,0:T(8,128)(2,1)}, u32[]{:S(2)}) copy-start(bf16[1280,640]{1,0:T(8,128)(2,1)} %slice_select_fusion.refs_2_) | copy-start | bytes 4915204
  139.1 17.0 %copy-start.11 = (bf16[256,1280]{1,0:T(8,128)(2,1)S(1)}, bf16[256,1280]{1,0:T(8,128)(2,1)}, u32[]{:S(2)}) copy-start(bf16[256,1280]{1,0:T(8,128)(2,1)} %copy-done.10) | copy-start | bytes 1966084
  139.1 17.0 %copy-start.14 = (bf16[256,640]{1,0:T(8,128)(2,1)S(1)}, bf16[256,640]{1,0:T(8,128)(2,1)}, u32[]{:S(2)}) copy-start(bf16[256,640]{1,0:T(8,128)(2,1)} %copy-done.13) | copy-start | bytes 983044
  205.5 2.7 %collective-permute-start.14 = (f32[400,128]{1,0:T(8,128)S(1)}, f32[400,128]{1,0:T(8,128)S(1)}, u32[]{:S(2)}, u32[]{:S(2)}) collective-permute-start(f32[400,128]{1,0:T(8,128)S(1)} %get-tuple-element.63), channel_id=1, source_target_pairs={{0,64},{64,0},{128,192},{192,128},{1,65},{65,1},{129,193},{193,129... | collective-permute-start | bytes 614408 | tf_op jit(solution)/shard_map/ppermute | solution.py:69
  (3 other events, 2.1 us)

commit v8 on v6

--- a/solution.py
+++ b/solution.py
@@ -172,10 +172,11 @@
 
 
 def order_kernel(*refs):
-    blocks, out = refs[:-1], refs[-1]
+    blocks, outs = refs[:-2], refs[-2:]
     at = 0
     for block in blocks:
-        out[at : at + block.shape[0], :] = block[...]
+        for out in outs:
+            out[at : at + block.shape[0], :] = block[...]
         at += block.shape[0]
 
 
@@ -472,8 +473,8 @@
     )
     around = [paired(noised, k + 1) for k in range(steps)]
     around.append(paired(noised_mine, n_mp // 2))
-    (around,) = call(
-        order_kernel, "order", around, [], [shape(((2 * steps + 1) * piece, width), BF16)]
+    around, later = call(
+        order_kernel, "order", around, [], [shape(((2 * steps + 1) * piece, width), BF16)] * 2
     )
     around_other = core_swap(around)
     score_weights, around_other = lax.optimization_barrier((score_weights, around_other))
@@ -501,11 +502,11 @@
         [shape((2 * piece, width + LANES), F32)],
     )
 
-    message, around, around_other = lax.optimization_barrier((message, around, around_other))
+    message, later = lax.optimization_barrier((message, later))
     normed, preact, active = call(
         refresh_kernel,
         "refresh",
-        [noised, around, around_other, embedding, score_weights, normed_gen]
+        [noised, later, core_swap(later), embedding, score_weights, normed_gen]
         + [active_gen, core_swap(active_gen), preact_gen, core_swap(preact_gen)],
         [place],
         [

time: 207 us -> 208 us (level)
    ppermute x7 -> x8, starting transfers between devices: 5.67 us -> 5.81 us  [core_swap(): return lax.ppermute(block, 'group', [(0, 1), (1, 0), (2, 3), (3, 2)])]
    ppermute x7 -> x8, waiting for transfers between devices: 7.25 us -> 7.25 us  [core_swap(): return lax.ppermute(block, 'group', [(0, 1), (1, 0), (2, 3), (3, 2)])]
  transfers between devices with their start and end apart: 18 -> 19, of which waited for: 9 -> 9; matrix products, arithmetic and copies ran while one was open for 3% -> 3% of each run, Pallas kernels for 4% -> 3%
where the time goes in v8:
time: 208 us; the launch traced here: 207 us
  blocking collectives  73 us (35%)
  waiting for transfers between devices  48.3 us (23%)
  starting transfers between devices  43.1 us (21%)
  Pallas kernels  19.1 us (9%)
  local copies, waits for them, and re-layouts  13.3 us (6%)
  other arithmetic  6.51 us (3%)
  between operations  3.69 us (2%)
    all_to_all x1, blocking collectives, local(): lax.all_to_all(grads.astype(jnp.float16), PLANE, 0, 0, axis_index_groups=...  46.1 us
    all_to_all x1, blocking collectives, exchange(): lax.all_to_all(blocks.astype(jnp.float16), 'mp', 0, 0, tiled=True)  27 us
    ppermute x8, starting transfers between devices, paired(): return lax.ppermute(block, ('group', 'mp'), pairs)  19.9 us
    pallas_call x14, Pallas kernels, call(): pl.pallas_call(body, name=name, out_shape=outs, in_specs=[SMEM] * len(sca...  19.1 us
    all_to_all x1, waiting for transfers between devices, exchange(): lax.all_to_all(blocks.astype(jnp.float16), 'mp', 0, 0, tiled=True)  15.6 us
    all_to_all x2, waiting for transfers between devices, gather(): return lax.all_to_all(blocks, PLANE, 0, 0, tiled=True).reshape(width, -1)  14.8 us
    all_to_all x2, starting transfers between devices, gather(): return lax.all_to_all(blocks, PLANE, 0, 0, tiled=True).reshape(width, -1)  13.2 us
    unnamed x60, local copies, waits for them, and re-layouts  11.1 us
  transfers between devices with their start and end apart: 19, of which 9 were waited for; matrix products, arithmetic and copies ran while one was open for 3% of the time, Pallas kernels for 3%

profile of v8, /device:TPU:1, one launch (start us, length us, event | category | flops | bytes accessed | tf_op | source)
XLA Modules:
  0.0 207.0 jit_solution(5143863826417595410)
XLA Ops:
  0.6 0.9 copy-done.18
  1.5 1.5 lay.2
  3.0 8.8 %all-to-all-start = ((bf16[32,40,640]{2,1,0:T(8,128)(2,1)}), bf16[32,40,640]{2,1,0:T(8,128)(2,1)}, u32[]{:S(2)}, u32[]{:S(2)}) async-start(bf16[32,40,640]{2,1,0:T(8,128)(2,1)} %lay.2), calls=%async_computation | async-start | bytes 3276800 | tf_op jit(solution)/shard_map/all_to_all | solution.py:418
  16.3 1.6 copy-done
  18.1 0.7 dynamic-slice_convert_fusion.refs_4_.embed.refs_0_
  18.8 0.8 prepare.1
  19.7 0.8 copy-done.2
  20.5 0.7 copy-done.14
  21.2 14.8 %all-to-all-done = bf16[32,40,640]{2,1,0:T(8,128)(2,1)} async-done(((bf16[32,40,640]{2,1,0:T(8,128)(2,1)}), bf16[32,40,640]{2,1,0:T(8,128)(2,1)}, u32[]{:S(2)}, u32[]{:S(2)}) %all-to-all-start) | async-done | bytes 1638432 | tf_op jit(solution)/shard_map/all_to_all | solution.py:418
  35.9 4.4 %all-to-all-start.1 = ((bf16[32,40,1280]{2,1,0:T(8,128)(2,1)}), bf16[32,40,1280]{2,1,0:T(8,128)(2,1)S(1)}, u32[]{:S(2)}, u32[]{:S(2)}) async-start(bf16[32,40,1280]{2,1,0:T(8,128)(2,1)} %copy-done), calls=%async_computation.1 | async-start | bytes 6553600 | tf_op jit(solution)/shard_map/all_to_all | solution.py:418
  40.7 3.6 %collective-permute-done.other = bf16[1280,640]{1,0:T(8,128)(2,1)} collective-permute-done((bf16[1280,640]{1,0:T(8,128)(2,1)}, bf16[1280,640]{1,0:T(8,128)(2,1)}, u32[]{:S(2)}, u32[]{:S(2)}) %collective-permute-start) | collective-permute-done | bytes 1638432 | tf_op jit(solution)/shard_map/ppermute | solution.py:67
  44.3 4.0 %generate.1 = (f32[128,640]{1,0:T(8,128)}, bf16[128,640]{1,0:T(8,128)(2,1)}, bf16[16,1280]{1,0:T(8,128)(2,1)}, bf16[16,1280]{1,0:T(8,128)(2,1)}, bf16[32,1280]{1...) custom-call(s32[3]{0:T(128)} %copy-done.21, bf16[256,1280]{1,0:T(8,128)(2,1)} %copy-done.2, ...), custom_call_target="tpu_custom_call" | custom-call | flops 419430400 | bytes 4751360 | tf_op jit(solution)/shard_map/generate/pallas_call | solution.py:35
  48.3 5.6 %collective-permute-start.2 = (bf16[32,1280]{1,0:T(8,128)(2,1)}, bf16[32,1280]{1,0:T(8,128)(2,1)S(1)}, u32[]{:S(2)}, u32[]{:S(2)}) collective-permute-start(bf16[32,1280]{1,0:T(8,128)(2,1)} %get-tuple-element.43), channel_id=1, source_target_pairs={{0,1},{1,2},{2,3},{3,4},{4,5},{5,6},{6,7},{7,0},{64,71},{65,64},{6... | collective-permute-start | bytes 245768 | tf_op jit(solution)/shard_map/ppermute | solution.py:77
  53.9 1.2 collective-permute-start.3
  55.5 4.5 %collective-permute-start.1 = (bf16[16,1280]{1,0:T(8,128)(2,1)}, bf16[16,1280]{1,0:T(8,128)(2,1)S(1)}, u32[]{:S(2)}, u32[]{:S(2)}) collective-permute-start(bf16[16,1280]{1,0:T(8,128)(2,1)} %get-tuple-element.42), channel_id=1, source_target_pairs={{0,4},{1,5},{2,6},{3,7},{4,0},{5,1},{6,2},{7,3},{64,68},{65,69},{6... | collective-permute-start | bytes 122888 | tf_op jit(solution)/shard_map/ppermute | solution.py:77
  60.0 4.3 %collective-permute-done.1.across = bf16[16,1280]{1,0:T(8,128)(2,1)S(1)} collective-permute-done((bf16[16,1280]{1,0:T(8,128)(2,1)}, bf16[16,1280]{1,0:T(8,128)(2,1)S(1)}, u32[]{:S(2)}, u32[]{:S(2)}) %collective-permute-start.1) | collective-permute-done | bytes 40992 | tf_op jit(solution)/shard_map/ppermute | solution.py:77
  64.3 0.8 copy-done.23
  65.7 1.8 collective-permute-start.5
  67.5 1.0 collective-permute-done.5.came
  69.1 0.7 copy-done.16
  69.8 2.1 collective-permute-start.8
  71.8 1.2 collective-permute-start.7
  73.0 2.4 %collective-permute-start.6 = (bf16[32,1280]{1,0:T(8,128)(2,1)S(1)}, bf16[32,1280]{1,0:T(8,128)(2,1)S(1)}, u32[]{:S(2)}, u32[]{:S(2)}) collective-permute-start(bf16[32,1280]{1,0:T(8,128)(2,1)S(1)} %get-tuple-element.48.pair.refs_4_), channel_id=1, source_target_pairs={{0,1},{1,2},{2,3},{3,4},{4,5},{5,6},{6,7},{7,0},{64,71},{65,64},{6... | collective-permute-start | bytes 245768 | tf_op jit(solution)/shard_map/ppermute | solution.py:77
  75.4 2.5 %collective-permute-start.9 = (bf16[16,1280]{1,0:T(8,128)(2,1)S(1)}, bf16[16,1280]{1,0:T(8,128)(2,1)S(1)}, u32[]{:S(2)}, u32[]{:S(2)}) collective-permute-start(bf16[16,1280]{1,0:T(8,128)(2,1)S(1)} %get-tuple-element.49), channel_id=1, source_target_pairs={{0,4},{1,5},{2,6},{3,7},{4,0},{5,1},{6,2},{7,3},{64,68},{65,69},{6... | collective-permute-start | bytes 122888 | tf_op jit(solution)/shard_map/ppermute | solution.py:77
  77.9 6.5 %collective-permute-done.9.refs_3_ = bf16[16,1280]{1,0:T(8,128)(2,1)S(1)} collective-permute-done((bf16[16,1280]{1,0:T(8,128)(2,1)S(1)}, bf16[16,1280]{1,0:T(8,128)(2,1)S(1)}, u32[]{:S(2)}, u32[]{:S(2)}) %collective-permute-start.9) | collective-permute-done | bytes 40992 | tf_op jit(solution)/shard_map/ppermute | solution.py:77
  84.5 0.7 copy-done.11
  85.8 0.7 copy-done.24
  87.0 0.7 copy-done.26
  87.7 1.0 copy-done.25
  88.7 1.0 copy-done.27
  89.6 3.7 %score.1 = f32[8,32,1408]{2,1,0:T(8,128)S(1)} custom-call(s32[3]{0:T(128)S(1)} %copy-done.22, bf16[32,1280]{1,0:T(8,128)(2,1)S(1)} %get-tuple-element.48.pair.refs_4_, bf16[112,1280]{1,0:T(8,128)(2,1)S(1)} %copy-done.25, bf16[112,1280]{1,0:T(8,128)(2,1)S(1)} %copy-done.27, f32[1,1280]{1,0:T(1,128)S(1)} %dynamic-slice_convert_fusion.refs_4_.embed.refs_0_, ...), custom_call_target="tpu_custom_call" | custom-call | flops 1677721600 | bytes 5379072 | tf_op jit(solution)/shard_map/score/pallas_call | solution.py:35
  93.5 27.0 %all_to_all.25 = f16[8,32,1408]{2,1,0:T(8,128)(2,1)S(1)} all-to-all(f16[8,32,1408]{2,1,0:T(8,128)(2,1)S(1)} %convert_element_type.28), channel_id=1, replica_groups=mesh['group'=4,'dp'=8,'mp'=8] {'mp'}, dimensions={0} | all-to-all | bytes 1441792 | tf_op jit(solution)/shard_map/all_to_all | solution.py:492
  121.2 1.0 collective-permute-done.11.refs_2_
  122.3 0.7 pack.1
  123.0 0.9 broadcast_in_dim.2
  123.9 4.2 %all-to-all-start.3 = ((f16[8,32,1408]{2,1,0:T(8,128)(2,1)}), f16[8,32,1408]{2,1,0:T(8,128)(2,1)}, u32[]{:S(2)}, u32[]{:S(2)}) async-start(f16[8,32,1408]{2,1,0:T(8,128)(2,1)} %broadcast_in_dim.2), calls=%async_computation.3 | async-start | bytes 1441792 | tf_op jit(solution)/shard_map/all_to_all | solution.py:492
  129.1 2.9 %slice_select_fusion.refs_2_ = bf16[1280,640]{1,0:T(8,128)(2,1)} fusion(bf16[1280,640]{1,0:T(8,128)(2,1)} %bitcast.3.mine, bf16[1280,1280]{1,0:T(8,128)(2,1)S(1)} %bitcast.7, pred[]{:T(512)S(6)} %eq.5), kind=kLoop, calls=%fused_computation | loop fusion | flops 819200 | bytes 4915201 | tf_op jit(solution)/shard_map/jit(_where)/select_n | solution.py:528
  132.1 0.7 refresh.1
  132.8 0.8 copy-done.6
  133.6 0.7 copy-done.9
  134.8 15.6 %all-to-all-done.3 = f16[8,32,1408]{2,1,0:T(8,128)(2,1)} async-done(((f16[8,32,1408]{2,1,0:T(8,128)(2,1)}), f16[8,32,1408]{2,1,0:T(8,128)(2,1)}, u32[]{:S(2)}, u32[]{:S(2)}) %all-to-all-start.3) | async-done | bytes 720928 | tf_op jit(solution)/shard_map/all_to_all | solution.py:492
  150.3 1.2 convert_element_type.31.refs_1_
  151.6 3.0 %grads.1 = f32[16,816,128]{2,1,0:T(8,128)S(1)} custom-call(s32[3]{0:T(128)S(1)} %copy-done.22, f32[8,32,1408]{2,1,0:T(8,128)S(1)} %convert_element_type.31.refs_1_, bf16[1280,640]{1,0:T(8,128)(2,1)S(1)} %copy-done.1, f32[256,640]{1,0:T(8,128)S(1)} %fusion.5.refs_3_, bf16[256,1280]{1,0:T(8,128)(2,1)S(1)} %copy-done.7, bf16[256,640]{1,0:T(8,128)(2,1)S(1)} %copy-done.10), custom_call_target="tpu_custom_call" | custom-call | flops 1258291200 | bytes 11403264 | tf_op jit(solution)/shard_map/grads/pallas_call | solution.py:35
  155.0 46.1 %all_to_all.26 = f16[16,816,128]{2,1,0:T(8,128)(2,1)S(1)} all-to-all(f16[16,816,128]{2,1,0:T(8,128)(2,1)S(1)} %convert_element_type.32), channel_id=1, replica_groups={{0,16,32,48,176,160,144,24,40,56,184,168,152,136,8,128},{64,80,96,112,2..., dimensions={0} | all-to-all | bytes 6684672 | tf_op jit(solution)/shard_map/all_to_all | solution.py:538
  201.6 1.2 collect.1
  202.7 1.6 collective-permute-start.15
  204.4 1.1 collective-permute-done.15.came
  205.5 1.5 place.1
  (80 shorter events, 8.2 us)
Async XLA Ops:
  0.6 0.9 copy-start.18
  3.0 8.8 %copy-start.28 = (s32[2]{0:T(128)S(1)}, s32[2]{0:T(128)}, u32[]{:S(2)}) copy-start(s32[2]{0:T(128)} %param.10) | copy-start | bytes 28
  3.0 10.2 %copy-start.29 = (s32[2]{0:T(128)S(1)}, s32[2]{0:T(128)}, u32[]{:S(2)}) copy-start(s32[2]{0:T(128)} %param.11) | copy-start | bytes 28
  3.0 12.7 %copy-start.19 = (bf16[40,2,640]{2,1,0:T(2,128)(2,1)S(1)}, bf16[40,2,640]{2,1,0:T(2,128)(2,1)}, u32[]{:S(2)}) copy-start(bf16[40,2,640]{2,1,0:T(2,128)(2,1)} %refs_0_.3) | copy-start | bytes 307204
  3.0 12.7 %copy-start.20 = (bf16[40,2,640]{2,1,0:T(2,128)(2,1)S(1)}, bf16[40,2,640]{2,1,0:T(2,128)(2,1)}, u32[]{:S(2)}) copy-start(bf16[40,2,640]{2,1,0:T(2,128)(2,1)} %refs_1_.1) | copy-start | bytes 307204
  3.0 32.9 %all-to-all-start = ((bf16[32,40,640]{2,1,0:T(8,128)(2,1)}), bf16[32,40,640]{2,1,0:T(8,128)(2,1)}, u32[]{:S(2)}, u32[]{:S(2)}) async-start(bf16[32,40,640]{2,1,0:T(8,128)(2,1)} %lay.2), calls=%async_computation | async-start | bytes 3276800 | tf_op jit(solution)/shard_map/all_to_all | solution.py:418
  15.8 3.1 %copy-start.4 = (bf16[2,256,1280]{2,1,0:T(8,128)(2,1)S(1)}, bf16[2,256,1280]{2,1,0:T(8,128)(2,1)}, u32[]{:S(2)}) copy-start(bf16[2,256,1280]{2,1,0:T(8,128)(2,1)} %refs_2_.1) | copy-start | bytes 3932164
  15.8 3.1 %copy-start.5 = (bf16[2,256,1280]{2,1,0:T(8,128)(2,1)S(1)}, bf16[2,256,1280]{2,1,0:T(8,128)(2,1)}, u32[]{:S(2)}) copy-start(bf16[2,256,1280]{2,1,0:T(8,128)(2,1)} %refs_3_.1) | copy-start | bytes 3932164
  16.3 1.7 copy-start
  18.1 17.9 %copy-start.21 = (s32[3]{0:T(128)}, s32[3]{0:T(128)S(1)}, u32[]{:S(2)}) copy-start(s32[3]{0:T(128)S(1)} %pad_add_fusion.refs_0_.place) | copy-start | bytes 40
  19.7 0.8 copy-start.2
  35.9 51.8 %all-to-all-start.1 = ((bf16[32,40,1280]{2,1,0:T(8,128)(2,1)}), bf16[32,40,1280]{2,1,0:T(8,128)(2,1)S(1)}, u32[]{:S(2)}, u32[]{:S(2)}) async-start(bf16[32,40,1280]{2,1,0:T(8,128)(2,1)} %copy-done), calls=%async_computation.1 | async-start | bytes 6553600 | tf_op jit(solution)/shard_map/all_to_all | solution.py:418
  40.3 23.9 %copy-start.22 = (s32[3]{0:T(128)S(1)}, s32[3]{0:T(128)}, u32[]{:S(2)}) copy-start(s32[3]{0:T(128)} %copy-done.21) | copy-start | bytes 40
  40.4 28.1 %copy-start.15 = (f32[32,1280]{1,0:T(8,128)S(1)}, f32[32,1280]{1,0:T(8,128)}, u32[]{:S(2)}) copy-start(f32[32,1280]{1,0:T(8,128)} %copy-done.14) | copy-start | bytes 491524
  40.4 3.9 %collective-permute-start = (bf16[1280,640]{1,0:T(8,128)(2,1)}, bf16[1280,640]{1,0:T(8,128)(2,1)}, u32[]{:S(2)}, u32[]{:S(2)}) collective-permute-start(bf16[1280,640]{1,0:T(8,128)(2,1)} %bitcast.3.mine), channel_id=1, source_target_pairs={{0,64},{64,0},{128,192},{192,128},{1,65},{65,1},{129,193},{193,129... | collective-permute-start | bytes 4915208 | tf_op jit(solution)/shard_map/ppermute | solution.py:67
  48.3 16.0 %collective-permute-start.2 = (bf16[32,1280]{1,0:T(8,128)(2,1)}, bf16[32,1280]{1,0:T(8,128)(2,1)S(1)}, u32[]{:S(2)}, u32[]{:S(2)}) collective-permute-start(bf16[32,1280]{1,0:T(8,128)(2,1)} %get-tuple-element.43), channel_id=1, source_target_pairs={{0,1},{1,2},{2,3},{3,4},{4,5},{5,6},{6,7},{7,0},{64,71},{65,64},{6... | collective-permute-start | bytes 245768 | tf_op jit(solution)/shard_map/ppermute | solution.py:77
  53.9 10.4 %collective-permute-start.3 = (bf16[32,1280]{1,0:T(8,128)(2,1)}, bf16[32,1280]{1,0:T(8,128)(2,1)S(1)}, u32[]{:S(2)}, u32[]{:S(2)}) collective-permute-start(bf16[32,1280]{1,0:T(8,128)(2,1)} %get-tuple-element.44), channel_id=1, source_target_pairs={{0,2},{1,3},{2,4},{3,5},{4,6},{5,7},{6,0},{7,1},{64,70},{65,71},{6... | collective-permute-start | bytes 245768 | tf_op jit(solution)/shard_map/ppermute | solution.py:77
  55.1 9.2 %collective-permute-start.4 = (bf16[32,1280]{1,0:T(8,128)(2,1)}, bf16[32,1280]{1,0:T(8,128)(2,1)S(1)}, u32[]{:S(2)}, u32[]{:S(2)}) collective-permute-start(bf16[32,1280]{1,0:T(8,128)(2,1)} %get-tuple-element.45), channel_id=1, source_target_pairs={{0,3},{1,4},{2,5},{3,6},{4,7},{5,0},{6,1},{7,2},{64,69},{65,70},{6... | collective-permute-start | bytes 245768 | tf_op jit(solution)/shard_map/ppermute | solution.py:77
  55.5 8.8 %collective-permute-start.1 = (bf16[16,1280]{1,0:T(8,128)(2,1)}, bf16[16,1280]{1,0:T(8,128)(2,1)S(1)}, u32[]{:S(2)}, u32[]{:S(2)}) collective-permute-start(bf16[16,1280]{1,0:T(8,128)(2,1)} %get-tuple-element.42), channel_id=1, source_target_pairs={{0,4},{1,5},{2,6},{3,7},{4,0},{5,1},{6,2},{7,3},{64,68},{65,69},{6... | collective-permute-start | bytes 122888 | tf_op jit(solution)/shard_map/ppermute | solution.py:77
  64.3 0.8 copy-start.23
  65.7 2.8 %collective-permute-start.5 = (f32[32,1280]{1,0:T(8,128)S(1)}, f32[32,1280]{1,0:T(8,128)S(1)}, u32[]{:S(2)}, u32[]{:S(2)}) collective-permute-start(f32[32,1280]{1,0:T(8,128)S(1)} %sums.1), channel_id=1, source_target_pairs={{0,64},{64,0},{128,192},{192,128},{1,65},{65,1},{129,193},{193,129... | collective-permute-start | bytes 491528 | tf_op jit(solution)/shard_map/ppermute | solution.py:67
  69.1 0.7 copy-start.16
  69.8 14.7 %collective-permute-start.8 = (bf16[32,1280]{1,0:T(8,128)(2,1)S(1)}, bf16[32,1280]{1,0:T(8,128)(2,1)S(1)}, u32[]{:S(2)}, u32[]{:S(2)}) collective-permute-start(bf16[32,1280]{1,0:T(8,128)(2,1)S(1)} %get-tuple-element.48.pair.refs_4_), channel_id=1, source_target_pairs={{0,3},{1,4},{2,5},{3,6},{4,7},{5,0},{6,1},{7,2},{64,69},{65,70},{6... | collective-permute-start | bytes 245768 | tf_op jit(solution)/shard_map/ppermute | solution.py:77
  71.8 12.6 %collective-permute-start.7 = (bf16[32,1280]{1,0:T(8,128)(2,1)S(1)}, bf16[32,1280]{1,0:T(8,128)(2,1)S(1)}, u32[]{:S(2)}, u32[]{:S(2)}) collective-permute-start(bf16[32,1280]{1,0:T(8,128)(2,1)S(1)} %get-tuple-element.48.pair.refs_4_), channel_id=1, source_target_pairs={{0,2},{1,3},{2,4},{3,5},{4,6},{5,7},{6,0},{7,1},{64,70},{65,71},{6... | collective-permute-start | bytes 245768 | tf_op jit(solution)/shard_map/ppermute | solution.py:77
  73.0 11.4 %collective-permute-start.6 = (bf16[32,1280]{1,0:T(8,128)(2,1)S(1)}, bf16[32,1280]{1,0:T(8,128)(2,1)S(1)}, u32[]{:S(2)}, u32[]{:S(2)}) collective-permute-start(bf16[32,1280]{1,0:T(8,128)(2,1)S(1)} %get-tuple-element.48.pair.refs_4_), channel_id=1, source_target_pairs={{0,1},{1,2},{2,3},{3,4},{4,5},{5,6},{6,7},{7,0},{64,71},{65,64},{6... | collective-permute-start | bytes 245768 | tf_op jit(solution)/shard_map/ppermute | solution.py:77
  75.4 9.0 %collective-permute-start.9 = (bf16[16,1280]{1,0:T(8,128)(2,1)S(1)}, bf16[16,1280]{1,0:T(8,128)(2,1)S(1)}, u32[]{:S(2)}, u32[]{:S(2)}) collective-permute-start(bf16[16,1280]{1,0:T(8,128)(2,1)S(1)} %get-tuple-element.49), channel_id=1, source_target_pairs={{0,4},{1,5},{2,6},{3,7},{4,0},{5,1},{6,2},{7,3},{64,68},{65,69},{6... | collective-permute-start | bytes 122888 | tf_op jit(solution)/shard_map/ppermute | solution.py:77
  84.5 0.7 copy-start.11
  85.2 1.8 collective-permute-start.10
  85.8 0.7 copy-start.24
  87.0 0.7 copy-start.26
  87.7 1.0 copy-start.25
  88.7 1.0 copy-start.27
  120.4 1.8 copy-start.17
  120.7 1.5 collective-permute-start.11
  122.3 5.9 %copy-start.13 = (bf16[128,640]{1,0:T(8,128)(2,1)S(1)}, bf16[128,640]{1,0:T(8,128)(2,1)}, u32[]{:S(2)}) copy-start(bf16[128,640]{1,0:T(8,128)(2,1)} %get-tuple-element.59.refs_3_) | copy-start | bytes 491524
  123.9 26.4 %all-to-all-start.3 = ((f16[8,32,1408]{2,1,0:T(8,128)(2,1)}), f16[8,32,1408]{2,1,0:T(8,128)(2,1)}, u32[]{:S(2)}, u32[]{:S(2)}) async-start(f16[8,32,1408]{2,1,0:T(8,128)(2,1)} %broadcast_in_dim.2), calls=%async_computation.3 | async-start | bytes 1441792 | tf_op jit(solution)/shard_map/all_to_all | solution.py:492
  128.2 3.9 %collective-permute-start.13 = (bf16[128,640]{1,0:T(8,128)(2,1)S(1)}, bf16[128,640]{1,0:T(8,128)(2,1)S(1)}, u32[]{:S(2)}, u32[]{:S(2)}) collective-permute-start(bf16[128,640]{1,0:T(8,128)(2,1)S(1)} %copy-done.13), channel_id=1, source_target_pairs={{0,64},{64,0},{128,192},{192,128},{1,65},{65,1},{129,193},{193,129... | collective-permute-start | bytes 491528 | tf_op jit(solution)/shard_map/ppermute | solution.py:67
  128.6 3.5 %copy-start.3 = (bf16[256,1280]{1,0:T(8,128)(2,1)S(1)}, bf16[256,1280]{1,0:T(8,128)(2,1)}, u32[]{:S(2)}) copy-start(bf16[256,1280]{1,0:T(8,128)(2,1)} %copy-done.2) | copy-start | bytes 1966084
  128.6 3.5 %copy-start.8 = (f32[128,640]{1,0:T(8,128)S(1)}, f32[128,640]{1,0:T(8,128)}, u32[]{:S(2)}) copy-start(f32[128,640]{1,0:T(8,128)} %get-tuple-element.60.refs_5_) | copy-start | bytes 983044
  128.6 3.5 %copy-start.12 = (bf16[112,1280]{1,0:T(8,128)(2,1)S(1)}, bf16[112,1280]{1,0:T(8,128)(2,1)}, u32[]{:S(2)}) copy-start(bf16[112,1280]{1,0:T(8,128)(2,1)} %copy-done.11) | copy-start | bytes 860164
  128.6 3.5 %collective-permute-start.14 = (f32[128,640]{1,0:T(8,128)}, f32[128,640]{1,0:T(8,128)S(1)}, u32[]{:S(2)}, u32[]{:S(2)}) collective-permute-start(f32[128,640]{1,0:T(8,128)} %get-tuple-element.60.refs_5_), channel_id=1, source_target_pairs={{0,64},{64,0},{128,192},{192,128},{1,65},{65,1},{129,193},{193,129... | collective-permute-start | bytes 983048 | tf_op jit(solution)/shard_map/ppermute | solution.py:67
  128.8 3.3 %collective-permute-start.12 = (bf16[112,1280]{1,0:T(8,128)(2,1)}, bf16[112,1280]{1,0:T(8,128)(2,1)S(1)}, u32[]{:S(2)}, u32[]{:S(2)}) collective-permute-start(bf16[112,1280]{1,0:T(8,128)(2,1)} %copy-done.11), channel_id=1, source_target_pairs={{0,64},{64,0},{128,192},{192,128},{1,65},{65,1},{129,193},{193,129... | collective-permute-start | bytes 860168 | tf_op jit(solution)/shard_map/ppermute | solution.py:67
  132.8 0.8 copy-start.6
  133.6 0.7 copy-start.9
  134.4 17.2 %copy-start.1 = (bf16[1280,640]{1,0:T(8,128)(2,1)S(1)}, bf16[1280,640]{1,0:T(8,128)(2,1)}, u32[]{:S(2)}) copy-start(bf16[1280,640]{1,0:T(8,128)(2,1)} %slice_select_fusion.refs_2_) | copy-start | bytes 4915204
  134.4 17.2 %copy-start.7 = (bf16[256,1280]{1,0:T(8,128)(2,1)S(1)}, bf16[256,1280]{1,0:T(8,128)(2,1)}, u32[]{:S(2)}) copy-start(bf16[256,1280]{1,0:T(8,128)(2,1)} %copy-done.6) | copy-start | bytes 1966084
  134.4 17.2 %copy-start.10 = (bf16[256,640]{1,0:T(8,128)(2,1)S(1)}, bf16[256,640]{1,0:T(8,128)(2,1)}, u32[]{:S(2)}) copy-start(bf16[256,640]{1,0:T(8,128)(2,1)} %copy-done.9) | copy-start | bytes 983044
  202.7 2.7 %collective-permute-start.15 = (f32[400,128]{1,0:T(8,128)S(1)}, f32[400,128]{1,0:T(8,128)S(1)}, u32[]{:S(2)}, u32[]{:S(2)}) collective-permute-start(f32[400,128]{1,0:T(8,128)S(1)} %get-tuple-element.65), channel_id=1, source_target_pairs={{0,64},{64,0},{128,192},{192,128},{1,65},{65,1},{129,193},{193,129... | collective-permute-start | bytes 614408 | tf_op jit(solution)/shard_map/ppermute | solution.py:67
  (1 other events, 0.7 us)
